TPU v7x, 32 devices: a whole 2x2x4 slice. The times are simulated.
32 devices in a mesh: dp: 8 (over z, core), fsdp: 4 (over y, x).
Axes of the slice: x: 2, y: 2, z: 4, core: 2. Of those that a mesh axis runs over, the one named last changes fastest.
Arguments:
- tokens: bfloat16 [64, 384, 1024], P(('dp', 'fsdp')), may hold values from -6 to 6
- text_states: bfloat16 [64, 128, 1024], P(('dp', 'fsdp')), may hold values from -6 to 6
- caption_len: int32 [64], P(('dp', 'fsdp')), may hold values from 1 to 128, as said below
- out_grad: bfloat16 [64, 384, 1024], P(('dp', 'fsdp')), may hold values from -6 to 6
- norm1_gain: bfloat16 [1024], P(('dp', 'fsdp')), may hold values from 0.099609375 to 1.8984375
- norm1_bias: bfloat16 [1024], P(('dp', 'fsdp')), may hold values from -3 to 3
- qkv_weight: bfloat16 [1024, 3072], P(('dp', 'fsdp')), may hold values from -0.1875 to 0.1875
- self_out: bfloat16 [1024, 1024], P(('dp', 'fsdp')), may hold values from -0.75 to 0.75
- norm2_gain: bfloat16 [1024], P(('dp', 'fsdp')), may hold values from 0.099609375 to 1.8984375
- norm2_bias: bfloat16 [1024], P(('dp', 'fsdp')), may hold values from -3 to 3
- cross_query: bfloat16 [1024, 1024], P(('dp', 'fsdp')), may hold values from -0.1875 to 0.1875
- cross_kv: bfloat16 [1024, 2048], P(('dp', 'fsdp')), may hold values from -0.1875 to 0.1875
- cross_out: bfloat16 [1024, 1024], P(('dp', 'fsdp')), may hold values from -0.375 to 0.375
- norm3_gain: bfloat16 [1024], P(('dp', 'fsdp')), may hold values from 0.099609375 to 1.8984375
- norm3_bias: bfloat16 [1024], P(('dp', 'fsdp')), may hold values from -3 to 3
- ff_in: bfloat16 [1024, 4096], P(('dp', 'fsdp')), may hold values from -0.1875 to 0.1875
- ff_in_bias: bfloat16 [4096], P(('dp', 'fsdp')), may hold values from -3 to 3
- ff_out: bfloat16 [4096, 1024], P(('dp', 'fsdp')), may hold values from -0.09375 to 0.09375
- ff_out_bias: bfloat16 [1024], P(('dp', 'fsdp')), may hold values from -3 to 3
Outputs:
- result: bfloat16 [64, 384, 1024], P(('dp', 'fsdp'))
- tokens_grad: bfloat16 [64, 384, 1024], P(('dp', 'fsdp'))
- text_grad: bfloat16 [64, 128, 1024], P(('dp', 'fsdp'))
- norm1_gain_grad: float32 [1024], P(('dp', 'fsdp'))
- norm1_bias_grad: float32 [1024], P(('dp', 'fsdp'))
- qkv_weight_grad: float32 [1024, 3072], P(('dp', 'fsdp'))
- self_out_grad: float32 [1024, 1024], P(('dp', 'fsdp'))
- norm2_gain_grad: float32 [1024], P(('dp', 'fsdp'))
- norm2_bias_grad: float32 [1024], P(('dp', 'fsdp'))
- cross_query_grad: float32 [1024, 1024], P(('dp', 'fsdp'))
- cross_kv_grad: float32 [1024, 2048], P(('dp', 'fsdp'))
- cross_out_grad: float32 [1024, 1024], P(('dp', 'fsdp'))
- norm3_gain_grad: float32 [1024], P(('dp', 'fsdp'))
- norm3_bias_grad: float32 [1024], P(('dp', 'fsdp'))
- ff_in_grad: float32 [1024, 4096], P(('dp', 'fsdp'))
- ff_in_bias_grad: float32 [4096], P(('dp', 'fsdp'))
- ff_out_grad: float32 [4096, 1024], P(('dp', 'fsdp'))
- ff_out_bias_grad: float32 [1024], P(('dp', 'fsdp'))
Inputs may be any that keep to these rules, and one draw needn't show every extreme that they name: `caption_len`: each item's caption length; some item's is exactly 128.
All inputs are finite; a program needn't handle non-finite values.
Results may differ from a plain program's by a relative error of at most 0.017.
Values may be sent and summed in bfloat16 or wider, within the bound.
No kernel may reach another device: no remote copies, remote signals or barrier semaphores. Data moves between devices by JAX's collectives and lax.ppermute only.
A program may use at most 320 MiB of HBM per device.

v0:
```python
import functools

import jax
import jax.numpy as jnp
from jax import lax
from jax.experimental import pallas as pl
from jax.experimental.pallas import tpu as pltpu
from jax.sharding import PartitionSpec as P

HEADS = 16
EPSILON = 1e-05
NEGATIVE = -1e30
AXES = ("dp", "fsdp")
F32 = jnp.float32
BF16 = jnp.bfloat16
LANES = 128
HBM_BYTES = 6400000
VMEM_MIB = {
    "project_qkv": 14,
    "self_attention": 11,
    "self_out_norm": 10,
    "project_query": 11,
    "cross_out_norm": 11,
    "hidden_layer": 14,
    "last_layer": 20,
    "hidden_grad": 14,
    "norm3_grad": 25,
    "cross_attention_grads": 10,
    "norm2_grad": 17,
    "self_attention_grads": 22,
    "norm1_grad": 20,
    "qkv_grad_other": 11,
    "qkv_grad_own": 17,
    "self_out_grad_own": 10,
    "cross_kv_grad_own": 10,
    "cross_query_grad_own": 10,
    "cross_out_grad_own": 10,
    "ff_in_grad_other": 14,
    "ff_in_grad_own": 22,
    "ff_out_grad_other": 11,
    "ff_out_grad_own": 23,
}


def nt(first, second):
    return lax.dot_general(first, second, (((1,), (1,)), ((), ())), preferred_element_type=F32)


def tn(first, second):
    return lax.dot_general(first, second, (((0,), (0,)), ((), ())), preferred_element_type=F32)


def nn(first, second):
    return lax.dot_general(first, second, (((1,), (0,)), ((), ())), preferred_element_type=F32)


def call(place, body, grid, in_specs, out_specs, out_shape, args, scratch=(), name=None, aliases=None):
    spec = pltpu.PrefetchScalarGridSpec(
        num_scalar_prefetch=1, grid=grid, in_specs=in_specs, out_specs=out_specs,
        scratch_shapes=list(scratch),
    )
    out_shape = jax.tree.map(
        lambda o: pltpu.HBM(o.shape, o.dtype) if is_large(o) else o, out_shape
    )
    out = pl.pallas_call(
        body, grid_spec=spec, out_shape=out_shape, name=name, input_output_aliases=aliases or {},
        cost_estimate=pl.CostEstimate(flops=1, bytes_accessed=1, transcendentals=0),
        compiler_params=pltpu.CompilerParams(vmem_limit_bytes=(VMEM_MIB.get(name, 8) if place.relative else 48) * 2**20),
    )(place.scalars, *[in_hbm(arg) for arg in args])
    return place.wait(out)


def is_large(value):
    return isinstance(value, (jax.Array, jax.ShapeDtypeStruct)) and (
        value.size * value.dtype.itemsize >= HBM_BYTES
    )


def pinned(value):
    return pltpu.with_memory_space_constraint(value, pltpu.HBM)


def in_hbm(value):
    if not is_large(value):
        return value
    return pinned(value)


class Place:
    def __init__(self, lines, planes, rows, lengths):
        self.lines = lines
        self.planes = planes
        self.bits = [1 << k for k in range(planes.bit_length() - 1)]
        self.line_bits = [1 << k for k in range(lines.bit_length() - 1)]
        dp = lax.axis_index("dp")
        self.line = dp // 2
        self.core = dp % 2
        self.plane = lax.axis_index("fsdp")
        self.relative = planes * rows % LANES == 0
        self.flip = (self.core if self.relative else jnp.zeros_like(self.core)).astype(jnp.int32)
        self.blocks = 2 * lines if self.relative else 2
        stages = len(self.bits)
        self.masks = [[0], [0]]
        for core in range(2):
            for stage in range(stages):
                bit = self.stage_bit(stage, core)
                self.masks[core] = self.masks[core] + [m ^ bit for m in self.masks[core]]
        masks = jnp.where(self.core == 0, jnp.array(self.masks[0]), jnp.array(self.masks[1]))
        self.plane_slots = (masks ^ self.plane).astype(jnp.int32)
        self.line_slots = ((self.line - jnp.arange(lines)) % lines).astype(jnp.int32)
        self.core_slots = (jnp.arange(2) ^ self.core).astype(jnp.int32)
        parts = [
            self.flip[None], lengths, self.plane_slots, self.line_slots, self.core_slots,
            (self.line ^ jnp.array(self.reversed_lines())).astype(jnp.int32),
        ]
        starts = [0]
        for part in parts:
            starts.append(starts[-1] + part.shape[0])
        _, self.at_length, self.at_plane, self.at_line, self.at_core, self.at_lines, _ = starts
        self.scalars = jnp.concatenate(parts)

    def wait(self, values):
        values, self.scalars = lax.optimization_barrier((values, self.scalars))
        return values

    def reversed_lines(self):
        order = [0]
        for bit in reversed(self.line_bits):
            order = order + [mask ^ bit for mask in order]
        return order

    def stage_bit(self, stage, core):
        return self.bits[(stage + core) % len(self.bits)]

    def _permute(self, value, target):
        pairs = []
        for line in range(self.lines):
            for core in range(2):
                for plane in range(self.planes):
                    l, c, p = target(line, core, plane)
                    pairs.append(
                        ((line * 2 + core) * self.planes + plane, (l * 2 + c) * self.planes + p)
                    )
        return lax.ppermute(value, AXES, pairs)

    def shift_line(self, value, step):
        return self._permute(value, lambda l, c, p: ((l + step) % self.lines, c, p))

    def swap_plane(self, value, stage):
        return self._permute(value, lambda l, c, p: (l, c, p ^ self.stage_bit(stage, c)))

    def swap_line(self, value, bit):
        return self._permute(value, lambda l, c, p: (l ^ bit, c, p))

    def swap_core(self, value):
        return self._permute(value, lambda l, c, p: (l, 1 - c, p))


def interleave(place, pieces, first):
    count = len(pieces)
    outer, rows, width = pieces[0].shape
    tile = width

    def body(slots_ref, *refs):
        out_ref = refs[count]
        for k in range(count):
            out_ref[0, pl.ds(slots_ref[first + k], 1)] = refs[k][...]

    moved = 2 * count * pieces[0].size * pieces[0].dtype.itemsize
    return call(
        place, body,
        (outer, width // tile),
        [pl.BlockSpec((1, rows, tile), lambda a, n, s: (a, 0, n))] * count,
        pl.BlockSpec((1, count, rows, tile), lambda a, n, s: (a, 0, 0, n)),
        jax.ShapeDtypeStruct((outer, count, rows, width), pieces[0].dtype),
        pieces,
        name="interleave",
    )


class Gather:
    def __init__(self, place, shard):
        self.place = place
        self.rows, self.width = shard.shape
        shard = place.wait(shard)
        self.pieces = [shard] + [place.shift_line(shard, s) for s in range(1, place.lines)]
        self.stage = 0

    def wait(self):
        self.pieces = self.place.wait(self.pieces)

    def join_line(self):
        place = self.place
        self.wait()
        held = interleave(place, [piece[None] for piece in self.pieces], place.at_line)
        self.pieces = [held.reshape(place.lines, self.rows, self.width)]
        self.swap()

    def swap(self):
        if self.stage:
            self.wait()
        self.pieces = self.pieces + [
            self.place.swap_plane(piece, self.stage) for piece in self.pieces
        ]
        self.stage += 1

    def join_plane(self):
        place = self.place
        while self.stage < len(place.bits):
            self.swap()
        self.wait()
        half = interleave(place, self.pieces, place.at_plane)
        self.own = half.reshape(place.lines, place.planes * self.rows, self.width)
        self.other = place.swap_core(self.own)

    def weight(self):
        place = self.place
        self.other = place.wait(self.other)
        if place.relative:
            return Weight(place, self.own[:, None], self.other[:, None])
        both = interleave(place, [self.own, self.other], place.at_core)
        return Weight(place, both.reshape(-1, self.width))


class Weight:
    def __init__(self, place, *arrays):
        self.full = len(arrays) == 1
        self.width = arrays[0].shape[-1]
        if self.full:
            arrays = (arrays[0].reshape(place.blocks // 2, 2, -1, self.width),) * 2
        self.arrays = arrays
        self.lines, _, self.rows, _ = arrays[0].shape
        self.half = self.lines * self.rows

    def specs(self, lines, columns, index, **more):
        def make(part):
            def index_map(*args):
                line, column = index(*args[:-1])
                which = args[-1][0] ^ part if self.full else 0
                return line, which, 0, column

            return pl.BlockSpec((lines, 1, self.rows, columns), index_map, **more)

        return [make(0), make(1)]


def rows_of(ref):
    lines, _, rows, columns = ref.shape
    return ref[...].reshape(lines * rows, columns)


def as_columns(place, vectors, rows):
    parts = jnp.concatenate([vector.reshape(-1, rows) for vector in vectors])
    return jnp.pad(parts, ((0, LANES - parts.shape[0]), (0, 0))).T


def as_table(place, sums, rows):
    owners = place.lines * 2 * place.planes
    parts = [
        vector.reshape(owners, -1, rows).transpose(1, 0, 2).reshape(-1, owners * rows)
        for vector in sums
    ]
    table = jnp.concatenate(parts)
    return jnp.pad(table, ((0, LANES - table.shape[0]), (0, 0))).astype(BF16)


def from_table(place, table, sizes, rows):
    owners = place.lines * 2 * place.planes
    vectors, at = [], 0
    for size in sizes:
        each = size // rows
        part = table[at : at + each]
        if each > 1:
            part = part.reshape(each, owners, rows).transpose(1, 0, 2)
        vectors.append(part.reshape(1, -1))
        at += each
    return vectors


class Scatter:
    def __init__(self, place, kept, sent):
        self.place = place
        self.kept = kept
        self.stages = [
            functools.partial(place.swap_plane, stage=stage)
            for stage in reversed(range(len(place.bits)))
        ] + [functools.partial(place.swap_line, bit=bit) for bit in place.line_bits]
        self.arrived = self.stages.pop(0)(place.wait(sent))

    def next(self):
        self.kept, sent = combine(self.place, self.kept, self.place.wait(self.arrived))
        self.arrived = self.stages.pop(0)(sent)

    def spread(self):
        place = self.place
        while len(self.stages) > len(place.line_bits):
            self.next()
        self.kept, *pieces = combine(place, self.kept, place.wait(self.arrived), apart=True)
        self.arrived = [
            place.swap_line(piece, mask) for piece, mask in zip(pieces, place.reversed_lines()[1:])
        ]
        self.stages = []

    def result(self):
        while self.stages:
            self.next()
        total = self.kept[0].astype(F32)
        for arrival in jax.tree.leaves(self.place.wait(self.arrived)):
            total = total + arrival[0].astype(F32)
        return total


def combine(place, kept, arrived, apart=False):
    count, rows, width = kept.shape
    each = 1 if apart else count // 2
    outs = count // each
    steps = 2 if kept.size > 2**18 and width % 256 == 0 else 1
    tile = width // steps

    def body(_, kept_ref, arrived_ref, *refs):
        total = (kept_ref[...].astype(F32) + arrived_ref[...].astype(F32)).astype(BF16)
        for k in range(outs):
            refs[k][...] = total[k * each : (k + 1) * each]

    def block(size):
        return pl.BlockSpec((size, rows, tile), lambda n, s: (0, 0, n))

    out = jax.ShapeDtypeStruct((each, rows, width), BF16)
    return call(
        place, body, (steps,), [block(count), block(count)], [block(each)] * outs, [out] * outs,
        (kept, arrived), name="combine",
    )


def relative_block(index, flip, blocks):
    return (index % 2 ^ flip) * (blocks // 2) + index // 2


def natural_block(index, flip, blocks):
    half = blocks // 2
    return index % half * 2 + (index // half ^ flip)


def block_slice(index, size):
    return pl.ds(pl.multiple_of(index * size, size), size)


def store_relative(ref, values, flip, blocks):
    size = values.shape[1] // blocks
    for k in range(blocks):
        at = relative_block(k, flip, blocks) if blocks > 2 else k
        ref[:, block_slice(at, size)] = values[:, k * size : (k + 1) * size].astype(ref.dtype)


def normalized(values):
    center = values - jnp.mean(values, axis=1, keepdims=True)
    inverse = lax.rsqrt(jnp.mean(center * center, axis=1, keepdims=True) + EPSILON)
    return center * inverse, inverse


def norm(place, values, weight, start):
    count, width = values.shape
    block = 256
    blocks = place.blocks

    def body(flip_ref, values_ref, columns_ref, out_ref, table_ref):
        @pl.when(pl.program_id(0) == 0)
        def _():
            table_ref[...] = columns_ref[...].reshape(width, LANES).astype(F32).T

        hat, _ = normalized(values_ref[...].astype(F32))
        store_relative(out_ref, hat * table_ref[0:1] + table_ref[1:2], flip_ref[0], blocks)

    row = pl.BlockSpec((block, width), lambda m, s: (m, 0))
    lines, _, rows, _ = weight.arrays[0].shape
    return call(
        place, body, (count // block,),
        [row, pl.BlockSpec((lines, 2, rows, LANES), lambda m, s: (0, 0, 0, start // LANES))],
        [row, pl.BlockSpec((LANES, width), lambda m, s: (0, 0))],
        [jax.ShapeDtypeStruct((count, width), BF16), jax.ShapeDtypeStruct((LANES, width), F32)],
        (values, weight.arrays[0]), name="norm",
    )


def relabel(place, values):
    count, width = values.shape
    blocks = place.blocks
    if blocks == 2:
        return values
    size = width // blocks

    def body(_, values_ref, out_ref):
        out_ref[...] = values_ref[...]

    return call(
        place, body, (blocks,),
        [pl.BlockSpec((count, size), lambda k, s: (0, k))],
        pl.BlockSpec((count, size), lambda k, s: (0, relative_block(k, s[0], blocks))),
        jax.ShapeDtypeStruct((count, width), values.dtype), (values,),
        name="relabel",
    )


def project(place, inputs, weight, start, width, tile=1024, name="project"):
    count, depth = inputs.shape
    half = depth // 2

    def body(_, inputs_ref, own_ref, other_ref, out_ref):
        total = nn(inputs_ref[:, :half], rows_of(own_ref)) + nn(inputs_ref[:, half:], rows_of(other_ref))
        out_ref[...] = total.astype(BF16)

    return call(
        place, body, (width // tile,),
        [pl.BlockSpec((count, depth), lambda n, s: (0, 0))]
        + weight.specs(weight.lines, tile, lambda n: (0, start // tile + n)),
        pl.BlockSpec((count, tile), lambda n, s: (0, n)),
        jax.ShapeDtypeStruct((count, width), BF16), (inputs, *weight.arrays),
        name=name,
    )


def project_norm(place, inputs, weight, start, base, gain, bias, name):
    count, depth = inputs.shape
    half = depth // 2
    width = base.shape[1]
    block = 256
    blocks = place.blocks

    def body(flip_ref, inputs_ref, own_ref, other_ref, base_ref, gain_ref, bias_ref, after_ref, out_ref):
        total = nn(inputs_ref[:, :half], rows_of(own_ref)) + nn(inputs_ref[:, half:], rows_of(other_ref))
        total = total + base_ref[...].astype(F32)
        after_ref[...] = total
        hat, _ = normalized(total)
        store_relative(out_ref, hat * gain_ref[...] + bias_ref[...], flip_ref[0], blocks)

    row = pl.BlockSpec((block, width), lambda m, s: (m, 0))
    vector = pl.BlockSpec((1, width), lambda m, s: (0, 0))
    return call(
        place, body, (count // block,),
        [pl.BlockSpec((block, depth), lambda m, s: (m, 0))]
        + weight.specs(weight.lines, width, lambda m: (0, start // width))
        + [row, vector, vector],
        [row, row],
        [pltpu.HBM((count, width), F32), jax.ShapeDtypeStruct((count, width), BF16)],
        (inputs, *weight.arrays, pinned(base), gain, bias),
        name=name,
    )


def hidden_layer(place, inputs, weight, bias):
    count, depth = inputs.shape
    half = depth // 2
    width = weight.width
    size = width // place.blocks

    def body(flip_ref, inputs_ref, own_ref, other_ref, bias_ref, middle_own, middle_other, slope_ref):
        scale = 0.7978845608028654
        for k, middle_ref in enumerate((middle_own, middle_other)):
            at = block_slice(k ^ flip_ref[0], size)
            upper = own_ref[:, 0, :, at].reshape(half, size)
            lower = other_ref[:, 0, :, at].reshape(half, size)
            before = nn(inputs_ref[:, :half], upper) + nn(inputs_ref[:, half:], lower)
            before = before + bias_ref[:, at]
            square = before * before
            half_sum = 0.5 + 0.5 * jnp.tanh(before * (scale + scale * 0.044715 * square))
            middle = before * half_sum
            middle_ref[...] = middle.astype(BF16)
            slope = half_sum + middle * (1.0 - half_sum) * (2.0 * scale + 6.0 * scale * 0.044715 * square)
            slope_ref[:, at] = slope.astype(BF16)

    column = pl.BlockSpec((count, size), lambda n, s: (0, n))
    return call(
        place, body, (place.blocks // 2,),
        [pl.BlockSpec((count, depth), lambda n, s: (0, 0))]
        + weight.specs(weight.lines, 2 * size, lambda n: (0, n))
        + [pl.BlockSpec((1, 2 * size), lambda n, s: (0, n))],
        [column, column, pl.BlockSpec((count, 2 * size), lambda n, s: (0, n))],
        [jax.ShapeDtypeStruct((count, width // 2), BF16)] * 2 + [pltpu.HBM((count, width), BF16)],
        (inputs, *weight.arrays, bias),
        name="hidden_layer",
    )


def last_layer(place, inputs, weight, bias, base):
    count, half = inputs[0].shape
    width = base.shape[1]
    steps = 4 if place.relative else 1
    size = half // steps

    def body(_, inputs_own, inputs_other, own_ref, other_ref, bias_ref, base_ref, out_ref, total_ref):
        step = pl.program_id(0)
        part = nn(inputs_own[...], rows_of(own_ref)) + nn(inputs_other[...], rows_of(other_ref))

        @pl.when(step == 0)
        def _():
            total_ref[...] = part

        @pl.when((step > 0) & (step < steps - 1))
        def _():
            total_ref[...] += part

        @pl.when(step == steps - 1)
        def _():
            total = total_ref[...] + part if steps > 1 else part
            out_ref[...] = (base_ref[...] + (total + bias_ref[...])).astype(BF16)

    column = pl.BlockSpec((count, size), lambda n, s: (0, n))
    rest = pl.BlockSpec((count, width), lambda n, s: (0, 0))
    return call(
        place, body, (steps,),
        [column, column]
        + weight.specs(weight.lines // steps, width, lambda n: (n, 0))
        + [pl.BlockSpec((1, width), lambda n, s: (0, 0)), rest],
        rest, jax.ShapeDtypeStruct((count, width), BF16), (*inputs, *weight.arrays, bias, base),
        scratch=[pltpu.VMEM((count, width), F32)],
        name="last_layer",
    )


def hidden_grad(place, grads, weight, slope):
    count, width = grads.shape
    hidden = slope.shape[1]
    pairs = place.blocks // 2
    size = hidden // place.blocks

    def body(flip_ref, grads_ref, own_ref, other_ref, slope_ref, out_ref, sum_ref):
        for k, weight_ref in enumerate((own_ref, other_ref)):
            at = block_slice(k ^ flip_ref[0], size)
            value = (nt(grads_ref[...], rows_of(weight_ref)) * slope_ref[:, at].astype(F32)).astype(BF16)
            out_ref[:, at] = value
            sum_ref[:, at] = jnp.sum(value.astype(F32), axis=0, keepdims=True)

    column = pl.BlockSpec((count, 2 * size), lambda n, s: (0, n))
    return call(
        place, body, (pairs,),
        [pl.BlockSpec((count, width), lambda n, s: (0, 0))]
        + weight.specs(1, width, lambda n: (n, 0))
        + [column],
        [column, pl.BlockSpec((1, 2 * size), lambda n, s: (0, n))],
        [jax.ShapeDtypeStruct((count, hidden), BF16), jax.ShapeDtypeStruct((1, hidden), F32)],
        (grads, *weight.arrays, pinned(slope)),
        name="hidden_grad",
    )


def back_project(place, grads, weight, start, name):
    count, width = grads.shape
    half = weight.half
    block = 256

    def body(_, grads_ref, own_ref, other_ref, out_ref):
        out_ref[:, :half] = nt(grads_ref[...], rows_of(own_ref)).astype(BF16)
        out_ref[:, half:] = nt(grads_ref[...], rows_of(other_ref)).astype(BF16)

    return call(
        place, body, (count // block,),
        [pl.BlockSpec((block, width), lambda m, s: (m, 0))]
        + weight.specs(weight.lines, width, lambda m: (0, start // width)),
        pl.BlockSpec((block, 2 * half), lambda m, s: (m, 0)),
        jax.ShapeDtypeStruct((count, 2 * half), BF16), (grads, *weight.arrays),
        name=name,
    )


def back_project_natural(place, grads, weight, start, name):
    count, width = grads.shape
    half = weight.half
    block = 256
    blocks = place.blocks
    size = 2 * half // blocks

    def body(flip_ref, grads_ref, own_ref, other_ref, out_ref):
        for k, weight_ref in enumerate((own_ref, other_ref)):
            total = nt(grads_ref[...], rows_of(weight_ref)).astype(BF16)
            for b in range(blocks // 2):
                at = natural_block(k * (blocks // 2) + b, flip_ref[0], blocks) if blocks > 2 else k
                out_ref[:, block_slice(at, size)] = total[:, b * size : (b + 1) * size]

    return call(
        place, body, (count // block,),
        [pl.BlockSpec((block, width), lambda m, s: (m, 0))]
        + weight.specs(weight.lines, width, lambda m: (0, start // width)),
        pl.BlockSpec((block, 2 * half), lambda m, s: (m, 0)),
        jax.ShapeDtypeStruct((count, 2 * half), BF16), (grads, *weight.arrays),
        name=name,
    )


def back_project_norm(place, grads, weight, start, values, gain, base, kinds, name):
    count, width = grads.shape
    half = weight.half
    features = 2 * half
    block = 256
    blocks = place.blocks
    size = features // blocks

    def body(flip_ref, grads_ref, own_ref, other_ref, values_ref, gain_ref, base_ref, *refs):
        outs, sums_ref, upstream_ref = refs[: len(kinds)], refs[len(kinds)], refs[len(kinds) + 1]
        for k, weight_ref in enumerate((own_ref, other_ref)):
            total = nt(grads_ref[...], rows_of(weight_ref))
            for b in range(blocks // 2):
                at = natural_block(k * (blocks // 2) + b, flip_ref[0], blocks) if blocks > 2 else k
                upstream_ref[:, block_slice(at, size)] = total[:, b * size : (b + 1) * size]
        upstream = upstream_ref[...]
        hat, inverse = normalized(values_ref[...].astype(F32))
        weighted = upstream * gain_ref[...]
        base_values = base_ref[...].astype(F32)
        grad = base_values + inverse * (
            weighted
            - jnp.mean(weighted, axis=1, keepdims=True)
            - hat * jnp.mean(weighted * hat, axis=1, keepdims=True)
        )
        for out in outs:
            out[...] = grad.astype(out.dtype)

        @pl.when(pl.program_id(0) == 0)
        def _():
            sums_ref[...] = jnp.zeros_like(sums_ref)

        sums_ref[0:1] += jnp.sum(upstream * hat, axis=0, keepdims=True)
        sums_ref[1:2] += jnp.sum(upstream, axis=0, keepdims=True)
        sums_ref[2:3] += jnp.sum(base_values, axis=0, keepdims=True)

    row = pl.BlockSpec((block, features), lambda m, s: (m, 0))
    sums = pl.BlockSpec((8, features), lambda m, s: (0, 0))
    return call(
        place, body, (count // block,),
        [pl.BlockSpec((block, width), lambda m, s: (m, 0))]
        + weight.specs(
            weight.lines, width, lambda m: (0, start // width), pipeline_mode=pl.Buffered(1)
        )
        + [row, pl.BlockSpec((1, features), lambda m, s: (0, 0)), row],
        [row] * len(kinds) + [sums],
        [(pltpu.HBM if kind == F32 else jax.ShapeDtypeStruct)((count, features), kind) for kind in kinds]
        + [jax.ShapeDtypeStruct((8, features), F32)],
        (pinned(grads) if width > 2 * features else grads, *weight.arrays, pinned(values), gain, pinned(base)),
        scratch=[pltpu.VMEM((block, features), F32)],
        name=name,
    )


def part_of(inputs, part):
    if isinstance(inputs, tuple):
        return inputs[part], 0, inputs[part].shape[1]
    return inputs, part, inputs.shape[1] // 2


def weight_part(place, inputs, grads, part, name, total=None, start=0, into=None):
    inputs, part, depth = part_of(inputs, part)
    count, width = grads.shape
    rows = min(1024, depth)
    tile = width if width <= 1024 else width // 2
    steps = depth // rows

    def body(_, inputs_ref, grads_ref, *refs):
        refs[-1][...] = tn(inputs_ref[...], grads_ref[...]).astype(BF16)

    return call(
        place, body, (steps, width // tile),
        [
            pl.BlockSpec((count, rows), lambda k, n, s: (0, part * steps + k)),
            pl.BlockSpec((count, tile), lambda k, n, s: (0, n)),
        ]
        + [pl.BlockSpec(memory_space=pl.ANY)] * (into is not None),
        pl.BlockSpec((rows, tile), lambda k, n, s: (k, start // tile + n)),
        jax.ShapeDtypeStruct((depth, total or width), BF16),
        (inputs, grads) + ((into,) if into is not None else ()),
        name=name, aliases={3: 0} if into is not None else {},
    )


def weight_sums(place, inputs, grads, arrived, name, total=None, start=0, into=None):
    inputs, _, depth = part_of(inputs, 0)
    count, width = grads.shape
    planes, lines = place.planes, place.lines
    each = depth // (lines * planes)
    tile = width if width * depth <= 2**19 else width // 2
    first, arrived = arrived
    pieces = planes // 2 * lines

    def body(slots_ref, inputs_ref, grads_ref, arrived_ref, *refs):
        kept_ref, sent_ref, total_ref = refs[-3:]
        total_ref[...] = tn(inputs_ref[...], grads_ref[...]) + arrived_ref[...].astype(F32)
        for k in range(planes):
            out_ref = kept_ref if k < planes // 2 else sent_ref
            for n in range(lines):
                line = slots_ref[place.at_lines + n]
                here = pl.multiple_of((line * planes + slots_ref[place.at_plane + k]) * each, each)
                out_ref[k % (planes // 2) * lines + n] = total_ref[pl.ds(here, each)].astype(BF16)

    block = pl.BlockSpec((pieces, each, tile), lambda n, s: (0, 0, start // tile + n))
    out = jax.ShapeDtypeStruct((pieces, each, total or width), BF16)
    return call(
        place, body, (width // tile,),
        [
            pl.BlockSpec((count, depth), lambda n, s: (0, 0)),
            pl.BlockSpec((count, tile), lambda n, s: (0, n)),
            pl.BlockSpec((depth, tile), lambda n, s: (0, first // tile + n)),
        ]
        + [pl.BlockSpec(memory_space=pl.ANY)] * (2 if into is not None else 0),
        [block, block], [out, out], (inputs, grads, arrived) + (tuple(into) if into is not None else ()),
        scratch=[pltpu.VMEM((depth, tile), F32)],
        name=name, aliases={4: 0, 5: 1} if into is not None else {},
    )


class WeightGrad:
    def __init__(self, place, inputs, grads, names):
        if not isinstance(inputs, list):
            inputs, grads, names = [inputs], [grads], [names]
        self.place = place
        self.inputs, self.grads, self.names = inputs, grads, names
        self.starts = [sum(grad.shape[1] for grad in grads[:k]) for k in range(len(grads))]
        total = sum(grad.shape[1] for grad in grads)
        sides = []
        for part in (1,) if place.relative else (1, 0):
            into = None
            for k, name in enumerate(names):
                into = weight_part(
                    place, inputs[k], grads[k], part, name + ("_own", "_other")[part], total,
                    self.starts[k], into,
                )
            sides.append(into)
        first = sides[0]
        if not place.relative:
            each = first.shape[0] // place.lines
            both = jnp.concatenate(sides[::-1]).reshape(place.lines, 2, each, -1)
            self.own = lax.dynamic_index_in_dim(both, place.core, 1, keepdims=False)
            first = lax.dynamic_index_in_dim(both, 1 - place.core, 1, keepdims=False)
            first = first.reshape(-1, total)
        self.arrived = place.swap_core(first)

    def sums(self, more=None):
        place = self.place
        parts = [self] if more is None else [self, more]
        arrived = [place.wait(part.arrived) for part in parts]
        total = sum(value.shape[1] for value in arrived)
        if place.relative:
            into, before = None, 0
            for part, value in zip(parts, arrived):
                for k, name in enumerate(part.names):
                    into = weight_sums(
                        place, part.inputs[k], part.grads[k], (part.starts[k], value), name + "_own",
                        total, before + part.starts[k], into,
                    )
                before += value.shape[1]
            return into
        own = jnp.concatenate([part.own for part in parts], axis=2)
        sums = own.astype(F32) + jnp.concatenate(arrived, axis=1).astype(F32).reshape(own.shape)
        sums = sums.astype(BF16).reshape(place.lines, place.planes, -1, total)
        sums = sums.transpose(1, 0, 2, 3)[place.plane_slots]
        sums = sums[:, place.line ^ jnp.array(place.reversed_lines())]
        return jnp.split(sums.reshape(place.planes * place.lines, -1, total), 2)


def own_lanes(head, values, scaling=None):
    lane = lax.broadcasted_iota(jnp.int32, values.shape, 1)
    size = values.shape[1] // 2
    scaled = values if scaling is None else values * scaling
    return jnp.where((lane >= head * size) & (lane < (head + 1) * size), scaled, 0).astype(BF16)


def softmax(scores):
    weights = jnp.exp(scores - jnp.max(scores, axis=1, keepdims=True))
    return weights * (1.0 / jnp.sum(weights, axis=1, keepdims=True))


def relative_lanes(place, width):
    per = width // place.blocks // LANES

    def column(p, flip):
        return relative_block(p // per, flip, place.blocks) * per + p % per

    return column


def lane_block(k):
    return slice(k * LANES, (k + 1) * LANES)


def attention(place, query, key_value, starts, items, per, masked, name):
    count = query.shape[0]
    rows, keys = count // items, key_value.shape[0] // items
    pairs = HEADS // 2
    width = pairs * LANES
    scaling = (width // HEADS) ** (-0.5)
    column = relative_lanes(place, width)

    def body(scalars_ref, query_ref, key_ref, value_ref, out_ref, prob_ref):
        for k in range(per):
            total = 0.0
            for head in range(2):
                scores = nt(own_lanes(head, query_ref[:, lane_block(k)], scaling), key_ref[:, lane_block(k)])
                weights = softmax(masked(scores, scalars_ref, pl.program_id(0))).astype(BF16)
                prob_ref[0, 2 * k + head] = weights
                total = total + nn(weights, own_lanes(head, value_ref[:, lane_block(k)]))
            at = column(pl.program_id(1) * per + k, scalars_ref[0])
            out_ref[:, block_slice(at, LANES)] = total.astype(BF16)

    spec = lambda size, start: pl.BlockSpec((size, per * LANES), lambda b, p, s: (b, start // per + p))
    return call(
        place, body, (items, pairs // per),
        [spec(rows, 0), spec(keys, starts[0]), spec(keys, starts[1])],
        [
            pl.BlockSpec((rows, width), lambda b, p, s: (b, 0)),
            pl.BlockSpec((1, 2 * per, rows, keys), lambda b, p, s: (b, p, 0, 0)),
        ],
        [
            jax.ShapeDtypeStruct((count, width), BF16),
            pltpu.HBM((items, HEADS, rows, keys), BF16),
        ],
        (query, key_value, key_value),
        name=name,
    )


def attention_grads(place, query, key_value, starts, probability, grad, out_widths, items, per, name):
    count = query.shape[0]
    rows, keys = count // items, key_value.shape[0] // items
    pairs = HEADS // 2
    width = pairs * LANES
    scaling = (width // HEADS) ** (-0.5)
    column = relative_lanes(place, width)
    alone = len(out_widths) == 1

    def body(scalars_ref, query_ref, key_ref, value_ref, prob_ref, grad_ref, *outs):
        for k in range(per):
            pair = pl.program_id(1) * per + k
            at = block_slice(column(pair, scalars_ref[0]), LANES)
            query_total = key_total = value_total = 0.0
            for head in range(2):
                weights = prob_ref[0, 2 * k + head]
                own_grad = own_lanes(head, grad_ref[:, at])
                prob_grad = nt(own_grad, value_ref[:, lane_block(k)])
                wide = weights.astype(F32)
                weighted = wide * prob_grad
                centre = jnp.sum(weighted, axis=1, keepdims=True)
                score_grad = (weighted - wide * centre).astype(BF16)
                query_total = query_total + nn(
                    score_grad, own_lanes(head, key_ref[:, lane_block(k)], scaling)
                )
                key_total = key_total + tn(
                    score_grad, own_lanes(head, query_ref[:, lane_block(k)], scaling)
                )
                value_total = value_total + tn(weights, own_grad)
            first = pairs if alone else 0
            outs[0][:, block_slice(pair, LANES)] = query_total.astype(BF16)
            outs[-1][:, block_slice(first + pair, LANES)] = key_total.astype(BF16)
            outs[-1][:, block_slice(first + pairs + pair, LANES)] = value_total.astype(BF16)

    spec = lambda size, start: pl.BlockSpec((size, per * LANES), lambda b, p, s: (b, start // per + p))
    heights = [rows] if alone else [rows, keys]
    return call(
        place, body, (items, pairs // per),
        [
            spec(rows, 0), spec(keys, starts[0]), spec(keys, starts[1]),
            pl.BlockSpec((1, 2 * per, rows, keys), lambda b, p, s: (b, p, 0, 0)),
            pl.BlockSpec((rows, width), lambda b, p, s: (b, 0)),
        ],
        [
            pl.BlockSpec((height, wide), lambda b, p, s: (b, 0))
            for height, wide in zip(heights, out_widths)
        ],
        [
            jax.ShapeDtypeStruct((items * height, wide), BF16)
            for height, wide in zip(heights, out_widths)
        ],
        (query, key_value, key_value, pinned(probability), grad),
        name=name,
    )


def causal(scores, scalars_ref, item):
    row = lax.broadcasted_iota(jnp.int32, scores.shape, 0)
    column = lax.broadcasted_iota(jnp.int32, scores.shape, 1)
    return jnp.where(column <= row, scores, NEGATIVE)


def visible(first_length):
    def masked(scores, scalars_ref, item):
        column = lax.broadcasted_iota(jnp.int32, scores.shape, 1)
        return jnp.where(column < scalars_ref[first_length + item], scores, NEGATIVE)

    return masked


def per_device(
    tokens,
    text_states,
    caption_len,
    out_grad,
    norm1_gain,
    norm1_bias,
    qkv_weight,
    self_out,
    norm2_gain,
    norm2_bias,
    cross_query,
    cross_kv,
    cross_out,
    norm3_gain,
    norm3_bias,
    ff_in,
    ff_in_bias,
    ff_out,
    ff_out_bias,
):
    place = Place(lax.axis_size("dp") // 2, lax.axis_size("fsdp"), qkv_weight.shape[0], caption_len)
    items, rows, width = tokens.shape
    text = text_states.shape[1]
    count = items * rows
    values0 = tokens.reshape(count, width)
    text_rows = text_states.reshape(items * text, width)
    cot = out_grad.reshape(count, width)

    small = (
        norm1_gain, norm1_bias, norm2_gain, norm2_bias, norm3_gain, norm3_bias, ff_in_bias, ff_out_bias
    )
    sizes = [vector.shape[0] for vector in small]
    middle_group = jnp.concatenate([cross_kv, cross_query, cross_out, self_out], axis=1)
    at_kv, at_query, at_cross, at_self = 0, 2 * width, 3 * width, 4 * width

    shard_rows = qkv_weight.shape[0]
    mid_group = Gather(place, middle_group)
    full_qkv = lax.all_gather(
        jnp.concatenate([qkv_weight, as_columns(place, small, shard_rows)], axis=1),
        AXES, axis=0, tiled=True,
    )
    mid_group.join_line()
    full_out = lax.all_gather(place.wait(ff_out), AXES, axis=0, tiled=True)
    in_group = Gather(place, ff_in)
    text_relative = relabel(place, text_rows)
    mid_group.swap()
    in_group.join_line()
    mid_group.join_plane()
    w_qkv = Weight(place, place.wait(full_qkv))
    normed1, table = norm(place, values0, w_qkv, 3 * width)
    (gain1, bias1, gain2, bias2, gain3, bias3, in_bias, out_bias) = from_table(
        place, table, sizes, shard_rows
    )
    projected = project(place, normed1, w_qkv, 0, 3 * width, name="project_qkv")
    w_mid = mid_group.weight()
    text_kv = project(place, text_relative, w_mid, at_kv, 2 * width, name="project_text")
    in_group.swap()
    pairs = HEADS // 2
    attended1, probs1 = attention(
        place, projected, projected, (pairs, 2 * pairs), items, 4, causal, "self_attention"
    )
    values1, normed2 = project_norm(
        place, attended1, w_mid, at_self, values0, gain2, bias2, "self_out_norm"
    )
    query2 = project(place, normed2, w_mid, at_query, width, name="project_query")
    attended2, probs2 = attention(
        place, query2, text_kv, (0, pairs), items, 4, visible(place.at_length), "cross_attention"
    )
    in_group.join_plane()
    values2, normed3 = project_norm(
        place, attended2, w_mid, at_cross, values1, gain3, bias3, "cross_out_norm"
    )
    w_in = in_group.weight()
    *middle, slope = hidden_layer(place, normed3, w_in, in_bias)
    ff_out_terms = WeightGrad(place, tuple(middle), cot, "ff_out_grad")
    w_out = Weight(place, place.wait(full_out))

    before_grad, in_bias_sum = hidden_grad(place, cot, w_out, slope)
    ff_out_own = ff_out_terms.sums()
    ff_in_terms = WeightGrad(place, normed3, before_grad, "ff_in_grad")

    ff_out_sums = Scatter(place, *ff_out_own)
    cross_grad, cross_round, sums3 = back_project_norm(
        place, before_grad, w_in, 0, values2, gain3, cot, (F32, BF16), "norm3_grad"
    )
    ff_in_own = ff_in_terms.sums()
    attended2_grad = back_project(place, cross_round, w_mid, at_cross, "attended2_grad")
    query2_grad, text_kv_grad = attention_grads(
        place, query2, text_kv, (0, pairs), probs2, attended2_grad, (width, 2 * width), items, 4,
        "cross_attention_grads",
    )
    ff_out_sums.next()
    middle_terms = WeightGrad(
        place,
        [text_relative, normed2, attended2],
        [text_kv_grad, query2_grad, cross_round],
        ["cross_kv_grad", "cross_query_grad", "cross_out_grad"],
    )

    ff_in_sums = Scatter(place, *ff_in_own)
    self_grad, self_round, sums2 = back_project_norm(
        place, query2_grad, w_mid, at_query, values1, gain2, cross_grad, (F32, BF16), "norm2_grad"
    )
    middle_own = middle_terms.sums()
    attended1_grad = back_project(place, self_round, w_mid, at_self, "attended1_grad")
    (projected_grad,) = attention_grads(
        place, projected, projected, (pairs, 2 * pairs), probs1, attended1_grad, (3 * width,), items, 4,
        "self_attention_grads",
    )
    ff_out_sums.next()
    ff_in_sums.next()
    last_terms = WeightGrad(
        place, [normed1, attended1], [projected_grad, self_round], ["qkv_grad", "self_out_grad"]
    )

    middle_sums = Scatter(place, *middle_own)
    tokens_grad, sums1 = back_project_norm(
        place, projected_grad, w_qkv, 0, values0, gain1, self_grad, (BF16,), "norm1_grad"
    )
    table = relabel(place, as_table(place, (
        sums1[0], sums1[1], sums2[0], sums2[1], sums3[0], sums3[1], in_bias_sum[0], sums3[2]
    ), shard_rows))
    small_terms = WeightGrad(place, table, jnp.eye(LANES, dtype=BF16), "small_grad")
    ff_out_sums.next()
    last_own = last_terms.sums(small_terms)
    ff_in_sums.next()
    middle_sums.next()

    last_sums = Scatter(place, *last_own)
    text_grad = back_project_natural(place, text_kv_grad, w_mid, at_kv, "text_grad")
    result = last_layer(place, middle, w_out, out_bias, values2)
    ff_in_sums.next()
    ff_out_grad = ff_out_sums.result()
    middle_sums.next()
    last_sums.next()
    last_sums.next()
    middle_sums.next()
    ff_in_grad = ff_in_sums.result()
    last_sums.next()
    middle_grads = middle_sums.result()
    last_grads = last_sums.result()
    small_grads = last_grads[:, 4 * width :].T
    own, at = [], 0
    for size in sizes:
        own.append(small_grads[at : at + size // shard_rows].reshape(-1))
        at += size // shard_rows
    return (
        result.reshape(items, rows, width),
        tokens_grad.reshape(items, rows, width),
        text_grad.reshape(items, text, width),
        own[0],
        own[1],
        last_grads[:, : 3 * width],
        last_grads[:, 3 * width : 4 * width],
        own[2],
        own[3],
        middle_grads[:, at_query : at_query + width],
        middle_grads[:, at_kv : at_kv + 2 * width],
        middle_grads[:, at_cross : at_cross + width],
        own[4],
        own[5],
        ff_in_grad,
        own[6],
        ff_out_grad,
        own[7],
    )


def solution(mesh):
    whole = P(AXES, None, None)
    matrix = P(AXES, None)
    vector = P(AXES)
    weights = (
        vector, vector, matrix, matrix, vector, vector, matrix, matrix, matrix, vector, vector, matrix,
        vector, matrix, vector,
    )
    return jax.shard_map(
        per_device,
        mesh=mesh,
        in_specs=(whole, whole, vector, whole) + weights,
        out_specs=(whole, whole, whole) + weights,
        check_vma=False,
    )
```

profile of v0, /device:TPU:0, one launch (start us, length us, event | category | flops | bytes accessed | tf_op | source)
XLA Modules:
  0.0 475.0 jit_solution(13697720683661840229)
XLA Ops:
  13.9 3.1 collective-permute-start
  16.9 2.6 collective-permute-start.1
  20.9 6.8 %collective-permute-done = bf16[32,5120]{1,0:T(8,128)(2,1)S(1)} collective-permute-done((bf16[32,5120]{1,0:T(8,128)(2,1)S(1)}, bf16[32,5120]{1,0:T(8,128)(2,1)S(1)}, u32[]{:S(2)}, u32[]{:S(2)}) %collective-permute-start) | collective-permute-done | bytes 327712 | tf_op jit(solution)/shard_map/ppermute | solution.py:144
  27.6 17.4 %collective-permute-done.1 = bf16[32,5120]{1,0:T(8,128)(2,1)S(1)} collective-permute-done((bf16[32,5120]{1,0:T(8,128)(2,1)S(1)}, bf16[32,5120]{1,0:T(8,128)(2,1)S(1)}, u32[]{:S(2)}, u32[]{:S(2)}) %collective-permute-start.1) | collective-permute-done | bytes 327712 | tf_op jit(solution)/shard_map/ppermute | solution.py:144
  49.4 21.7 %collective-permute-done.6.refs_1_ = bf16[4,32,5120]{2,1,0:T(8,128)(2,1)} collective-permute-done((bf16[4,32,5120]{2,1,0:T(8,128)(2,1)}, bf16[4,32,5120]{2,1,0:T(8,128)(2,1)}, u32[]{:S(2)}, u32[]{:S(2)}) %collective-permute-start.6) | collective-permute-done | bytes 1310752 | tf_op jit(solution)/shard_map/ppermute | solution.py:144
  73.2 5.3 %collective-permute-start.3 = (bf16[32,4096]{1,0:T(8,128)(2,1)S(1)}, bf16[32,4096]{1,0:T(8,128)(2,1)S(1)}, u32[]{:S(2)}, u32[]{:S(2)}) collective-permute-start(bf16[32,4096]{1,0:T(8,128)(2,1)S(1)} %copy-done.36), channel_id=1, source_target_pairs={{0,8},{1,9},{2,10},{3,11},{4,12},{5,13},{6,14},{7,15},{8,16},{9,17... | collective-permute-start | bytes 786440 | tf_op jit(solution)/shard_map/ppermute | solution.py:144
  78.5 3.0 collective-permute-start.4
  82.7 10.9 %collective-permute-done.3 = bf16[32,4096]{1,0:T(8,128)(2,1)S(1)} collective-permute-done((bf16[32,4096]{1,0:T(8,128)(2,1)S(1)}, bf16[32,4096]{1,0:T(8,128)(2,1)S(1)}, u32[]{:S(2)}, u32[]{:S(2)}) %collective-permute-start.3) | collective-permute-done | bytes 262176 | tf_op jit(solution)/shard_map/ppermute | solution.py:144
  93.7 15.9 %collective-permute-done.4 = bf16[32,4096]{1,0:T(8,128)(2,1)S(1)} collective-permute-done((bf16[32,4096]{1,0:T(8,128)(2,1)S(1)}, bf16[32,4096]{1,0:T(8,128)(2,1)S(1)}, u32[]{:S(2)}, u32[]{:S(2)}) %collective-permute-start.4) | collective-permute-done | bytes 262176 | tf_op jit(solution)/shard_map/ppermute | solution.py:144
  111.1 3.5 collective-permute-done.9.refs_3_
  114.6 5.1 %interleave.6 = bf16[4,4,32,5120]{3,2,1,0:T(8,128)(2,1)} custom-call(s32[17]{0:T(128)S(1)} %concatenate.18.slots_ref._.flip_ref.scalars_ref, bf16[4,32,5120]{2,1,0:T(8,128)(2,1)} %bitcast.5.refs_0_, bf16[4,32,5120]{2,1,0:T(8,128)(2,1)} %collective-permute-done.6.refs_1_, bf16[4,32,5120]{2,1,0:T(8,128)(2,1)S(1)} %collective-permute-done.8.refs_2_, ...), custom_call_target="tpu_custom_call" | custom-call | flops 1 | bytes 1 | tf_op jit(solution)/shard_map/interleave/pallas_call | solution.py:65
  121.3 3.1 norm.1
  124.5 8.0 %project_qkv.1.query_ref.key_ref.value_ref = bf16[768,3072]{1,0:T(8,128)(2,1)S(1)} custom-call(s32[17]{0:T(128)S(1)} %concatenate.18.slots_ref._.flip_ref.scalars_ref, bf16[768,1024]{1,0:T(8,128)(2,1)S(1)} %get-tuple-element.343.inputs_ref, bf16[4,2,128,3200]{3,2,1,0:T(8,128)(2,1)} %bitcast.69, bf16[4,2,128,3200]{3,2,1,0:T(8,128)(2,1)} %bitcast.70), custom_call_target="tpu_custom_call" | custom-call | flops 1 | bytes 1 | tf_op jit(solution)/shard_map/project_qkv/pallas_call | solution.py:65
  132.5 4.7 project_text.1.key_ref.value_ref
  139.3 13.8 %self_attention.1 = (bf16[768,1024]{1,0:T(8,128)(2,1)S(1)}, bf16[2,16,384,384]{3,2,1,0:T(8,128)(2,1)}) custom-call(s32[17]{0:T(128)S(1)} %concatenate.18.slots_ref._.flip_ref.scalars_ref, bf16[768,3072]{1,0:T(8,128)(2,1)S(1)} %project_qkv.1.query_ref.key_ref.value_ref, bf16[768,3072]{1,0:T(8,128)(2,1)S(1)} %project_qkv.1.query_ref.key_ref.value_ref, ...), custom_call_target="tpu_custom_call" | custom-call | flops 1 | bytes 1 | tf_op jit(solution)/shard_map/self_attention/pallas_call | solution.py:65
  153.1 6.5 %self_out_norm.1 = (f32[768,1024]{1,0:T(8,128)}, bf16[768,1024]{1,0:T(8,128)(2,1)S(1)}) custom-call(s32[17]{0:T(128)S(1)} %concatenate.18.slots_ref._.flip_ref.scalars_ref, bf16[768,1024]{1,0:T(8,128)(2,1)S(1)} %get-tuple-element.356.inputs_ref, bf16[4,1,128,5120]{3,2,1,0:T(8,128)(2,1)} %bitcast.23.own_ref, bf16[4,1,128,5120]{3,2,1,0:T(8,128)(2,1)} %bitcast.24.other_ref, ...), custom_call_target="tpu_custom_call" | custom-call | flops 1 | bytes 1 | tf_op jit(solution)/shard_map/self_out_norm/pallas_call | solution.py:65
  159.6 3.9 project_query.1.query_ref
  163.5 6.6 %cross_attention.1 = (bf16[768,1024]{1,0:T(8,128)(2,1)S(1)}, bf16[2,16,384,128]{3,2,1,0:T(8,128)(2,1)}) custom-call(s32[17]{0:T(128)S(1)} %concatenate.18.slots_ref._.flip_ref.scalars_ref, bf16[768,1024]{1,0:T(8,128)(2,1)S(1)} %project_query.1.query_ref, bf16[256,2048]{1,0:T(8,128)(2,1)S(1)} %project_text.1.key_ref.value_ref, ...), custom_call_target="tpu_custom_call" | custom-call | flops 1 | bytes 1 | tf_op jit(solution)/shard_map/cross_attention/pallas_call | solution.py:65
  170.1 5.1 %interleave.7 = bf16[4,4,32,4096]{3,2,1,0:T(8,128)(2,1)} custom-call(s32[17]{0:T(128)S(1)} %concatenate.18.slots_ref._.flip_ref.scalars_ref, bf16[4,32,4096]{2,1,0:T(8,128)(2,1)} %bitcast.11.refs_0_, bf16[4,32,4096]{2,1,0:T(8,128)(2,1)} %collective-permute-done.7.refs_1_, bf16[4,32,4096]{2,1,0:T(8,128)(2,1)S(1)} %collective-permute-done.11.refs_2_, ...), custom_call_target="tpu_custom_call" | custom-call | flops 1 | bytes 1 | tf_op jit(solution)/shard_map/interleave/pallas_call | solution.py:65
  175.5 6.7 %cross_out_norm.1 = (f32[768,1024]{1,0:T(8,128)}, bf16[768,1024]{1,0:T(8,128)(2,1)S(1)}) custom-call(s32[17]{0:T(128)S(1)} %concatenate.18.slots_ref._.flip_ref.scalars_ref, bf16[768,1024]{1,0:T(8,128)(2,1)S(1)} %get-tuple-element.375.inputs_ref, bf16[4,1,128,5120]{3,2,1,0:T(8,128)(2,1)} %bitcast.23.own_ref, bf16[4,1,128,5120]{3,2,1,0:T(8,128)(2,1)} %bitcast.24.other_ref, ...), custom_call_target="tpu_custom_call" | custom-call | flops 1 | bytes 1 | tf_op jit(solution)/shard_map/cross_out_norm/pallas_call | solution.py:65
  182.7 16.7 %hidden_layer.1 = (bf16[768,2048]{1,0:T(8,128)(2,1)S(1)}, bf16[768,2048]{1,0:T(8,128)(2,1)S(1)}, bf16[768,4096]{1,0:T(8,128)(2,1)}) custom-call(s32[17]{0:T(128)S(1)} %concatenate.18.slots_ref._.flip_ref.scalars_ref, bf16[768,1024]{1,0:T(8,128)(2,1)S(1)} %get-tuple-element.381.inputs_ref, bf16[4,1,128,4096]{3,2,1,0:T(8,128)(2,1)} %bitcast.26.own_ref, ...), custom_call_target="tpu_custom_call" | custom-call | flops 1 | bytes 1 | tf_op jit(solution)/shard_map/hidden_layer/pallas_call | solution.py:65
  199.4 5.8 %ff_out_grad_other.1 = bf16[2048,1024]{1,0:T(8,128)(2,1)} custom-call(s32[17]{0:T(128)S(1)} %concatenate.18.slots_ref._.flip_ref.scalars_ref, bf16[768,2048]{1,0:T(8,128)(2,1)S(1)} %get-tuple-element.387.inputs_ref.inputs_other, bf16[768,1024]{1,0:T(8,128)(2,1)S(1)} %bitcast.53), custom_call_target="tpu_custom_call" | custom-call | flops 1 | bytes 1 | tf_op jit(solution)/shard_map/ff_out_grad_other/pallas_call | solution.py:65
  205.3 11.3 %hidden_grad.1 = (bf16[768,4096]{1,0:T(8,128)(2,1)S(1)}, f32[1,4096]{1,0:T(1,128)S(1)}) custom-call(s32[17]{0:T(128)S(1)} %concatenate.18.slots_ref._.flip_ref.scalars_ref, bf16[768,1024]{1,0:T(8,128)(2,1)S(1)} %bitcast.54, bf16[4,2,512,1024]{3,2,1,0:T(8,128)(2,1)} %bitcast.73, bf16[4,2,512,1024]{3,2,1,0:T(8,128)(2,1)} %bitcast.74, ...), custom_call_target="tpu_custom_call" | custom-call | flops 1 | bytes 1 | tf_op jit(solution)/shard_map/hidden_grad/pallas_call | solution.py:65
  216.7 8.8 %ff_out_grad_own.1 = (bf16[8,128,1024]{2,1,0:T(8,128)(2,1)S(1)}, bf16[8,128,1024]{2,1,0:T(8,128)(2,1)S(1)}) custom-call(s32[17]{0:T(128)S(1)} %concatenate.18.slots_ref._.flip_ref.scalars_ref, bf16[768,2048]{1,0:T(8,128)(2,1)S(1)} %copy-done.25, bf16[768,1024]{1,0:T(8,128)(2,1)S(1)} %bitcast.55, bf16[2048,1024]{1,0:T(8,128)(2,1)} %collective-permute-done.14.arrived_ref), custom_call_target="tpu_custom_call" | custom-call | flops 1 | bytes 1 | tf_op jit(solution)/shard_map/ff_out_grad_own/pallas_call | solution.py:65
  225.6 5.0 %ff_in_grad_other.1 = bf16[512,4096]{1,0:T(8,128)(2,1)S(1)} custom-call(s32[17]{0:T(128)S(1)} %concatenate.18.slots_ref._.flip_ref.scalars_ref, bf16[768,1024]{1,0:T(8,128)(2,1)S(1)} %copy-done.7, bf16[768,4096]{1,0:T(8,128)(2,1)S(1)} %get-tuple-element.404.grads_ref), custom_call_target="tpu_custom_call" | custom-call | flops 1 | bytes 1 | tf_op jit(solution)/shard_map/ff_in_grad_other/pallas_call | solution.py:65
  232.4 17.2 %norm3_grad.1 = (f32[768,1024]{1,0:T(8,128)}, bf16[768,1024]{1,0:T(8,128)(2,1)S(1)}, f32[8,1024]{1,0:T(8,128)S(1)}) custom-call(s32[17]{0:T(128)S(1)} %concatenate.18.slots_ref._.flip_ref.scalars_ref, bf16[768,4096]{1,0:T(8,128)(2,1)} %copy-done.3, bf16[4,1,128,4096]{3,2,1,0:T(8,128)(2,1)} %bitcast.26.own_ref, bf16[4,1,128,4096]{3,2,1,0:T(8,128)(2,1)} %bitcast.27.other_ref, ...), custom_call_target="tpu_custom_call" | custom-call | flops 1 | bytes 1 | tf_op jit(solution)/shard_map/norm3_grad/pallas_call | solution.py:65
  249.6 5.7 %ff_in_grad_own.1 = (bf16[8,32,4096]{2,1,0:T(8,128)(2,1)S(1)}, bf16[8,32,4096]{2,1,0:T(8,128)(2,1)S(1)}) custom-call(s32[17]{0:T(128)S(1)} %concatenate.18.slots_ref._.flip_ref.scalars_ref, bf16[768,1024]{1,0:T(8,128)(2,1)S(1)} %copy-done.7, bf16[768,4096]{1,0:T(8,128)(2,1)S(1)} %copy-done.4, bf16[512,4096]{1,0:T(8,128)(2,1)S(1)} %collective-permute-done.16.arrived_ref), custom_call_target="tpu_custom_call" | custom-call | flops 1 | bytes 1 | tf_op jit(solution)/shard_map/ff_in_grad_own/pallas_call | solution.py:65
  255.3 4.4 attended2_grad.1.grad_ref
  259.7 10.0 %cross_attention_grads.1 = (bf16[768,1024]{1,0:T(8,128)(2,1)S(1)}, bf16[256,2048]{1,0:T(8,128)(2,1)S(1)}) custom-call(s32[17]{0:T(128)S(1)} %concatenate.18.slots_ref._.flip_ref.scalars_ref, bf16[768,1024]{1,0:T(8,128)(2,1)S(1)} %copy-done.9, bf16[256,2048]{1,0:T(8,128)(2,1)S(1)} %project_text.1.key_ref.value_ref, ...), custom_call_target="tpu_custom_call" | custom-call | flops 1 | bytes 1 | tf_op jit(solution)/shard_map/cross_attention_grads/pallas_call | solution.py:65
  278.1 8.7 %norm2_grad.1 = (f32[768,1024]{1,0:T(8,128)}, bf16[768,1024]{1,0:T(8,128)(2,1)S(1)}, f32[8,1024]{1,0:T(8,128)S(1)}) custom-call(s32[17]{0:T(128)S(1)} %concatenate.18.slots_ref._.flip_ref.scalars_ref, bf16[768,1024]{1,0:T(8,128)(2,1)S(1)} %get-tuple-element.434.grads_ref, bf16[4,1,128,5120]{3,2,1,0:T(8,128)(2,1)} %bitcast.23.own_ref, ...), custom_call_target="tpu_custom_call" | custom-call | flops 1 | bytes 1 | tf_op jit(solution)/shard_map/norm2_grad/pallas_call | solution.py:65
  286.8 3.0 cross_kv_grad_own.1
  294.9 4.4 attended1_grad.1.grad_ref
  299.3 17.1 %self_attention_grads.1.grads_ref = bf16[768,3072]{1,0:T(8,128)(2,1)S(1)} custom-call(s32[17]{0:T(128)S(1)} %concatenate.18.slots_ref._.flip_ref.scalars_ref, bf16[768,3072]{1,0:T(8,128)(2,1)S(1)} %bitcast.51, bf16[768,3072]{1,0:T(8,128)(2,1)S(1)} %bitcast.51, bf16[768,3072]{1,0:T(8,128)(2,1)S(1)} %bitcast.51, ...), custom_call_target="tpu_custom_call" | custom-call | flops 1 | bytes 1 | tf_op jit(solution)/shard_map/self_attention_grads/pallas_call | solution.py:65
  321.8 5.1 %qkv_grad_other.1.refs_0_ = bf16[512,4096]{1,0:T(8,128)(2,1)} custom-call(s32[17]{0:T(128)S(1)} %concatenate.18.slots_ref._.flip_ref.scalars_ref, bf16[768,1024]{1,0:T(8,128)(2,1)S(1)} %copy-done.21, bf16[768,3072]{1,0:T(8,128)(2,1)S(1)} %self_attention_grads.1.grads_ref), custom_call_target="tpu_custom_call" | custom-call | flops 1 | bytes 1 | tf_op jit(solution)/shard_map/qkv_grad_other/pallas_call | solution.py:65
  327.0 2.6 self_out_grad_other.1
  331.8 7.7 %collective-permute-start.22 = (bf16[2,128,1024]{2,1,0:T(8,128)(2,1)}, bf16[2,128,1024]{2,1,0:T(8,128)(2,1)}, u32[]{:S(2)}, u32[]{:S(2)}) collective-permute-start(bf16[2,128,1024]{2,1,0:T(8,128)(2,1)} %get-tuple-element.499), channel_id=1, source_target_pairs={{0,8},{1,9},{2,10},{3,11},{4,12},{5,13},{6,14},{7,15},{8,0},{9,1},... | collective-permute-start | bytes 1572872 | tf_op jit(solution)/shard_map/ppermute | solution.py:144
  339.8 13.5 %norm1_grad.1 = (bf16[768,1024]{1,0:T(8,128)(2,1)}, f32[8,1024]{1,0:T(8,128)S(1)}) custom-call(s32[17]{0:T(128)S(1)} %concatenate.18.slots_ref._.flip_ref.scalars_ref, bf16[768,3072]{1,0:T(8,128)(2,1)} %copy-done.1, bf16[4,2,128,3200]{3,2,1,0:T(8,128)(2,1)} %bitcast.71, bf16[4,2,128,3200]{3,2,1,0:T(8,128)(2,1)} %bitcast.72, bf16[768,1024]{1,0:T(8,128)(2,1)} %bitcast.57, ...), custom_call_target="tpu_custom_call" | custom-call | flops 1 | bytes 1 | tf_op jit(solution)/shard_map/norm1_grad/pallas_call | solution.py:65
  360.5 5.9 %qkv_grad_own.1 = (bf16[8,32,4224]{2,1,0:T(8,128)(2,1)S(1)}, bf16[8,32,4224]{2,1,0:T(8,128)(2,1)S(1)}) custom-call(s32[17]{0:T(128)S(1)} %concatenate.18.slots_ref._.flip_ref.scalars_ref, bf16[768,1024]{1,0:T(8,128)(2,1)S(1)} %copy-done.22, bf16[768,3072]{1,0:T(8,128)(2,1)S(1)} %copy-done.2, bf16[512,4096]{1,0:T(8,128)(2,1)} %collective-permute-done.21.arrived_ref), custom_call_target="tpu_custom_call" | custom-call | flops 1 | bytes 1 | tf_op jit(solution)/shard_map/qkv_grad_own/pallas_call | solution.py:65
  366.4 3.0 self_out_grad_own.1
  379.6 5.2 %text_grad.1 = bf16[256,1024]{1,0:T(8,128)(2,1)} custom-call(s32[17]{0:T(128)S(1)} %concatenate.18.slots_ref._.flip_ref.scalars_ref, bf16[256,2048]{1,0:T(8,128)(2,1)S(1)} %get-tuple-element.432.grads_ref, bf16[4,1,128,5120]{3,2,1,0:T(8,128)(2,1)} %bitcast.23.own_ref, bf16[4,1,128,5120]{3,2,1,0:T(8,128)(2,1)} %bitcast.24.other_ref), custom_call_target="tpu_custom_call" | custom-call | flops 1 | bytes 1 | tf_op jit(solution)/shard_map/text_grad/pallas_call | solution.py:65
  384.8 12.4 %last_layer.1 = bf16[768,1024]{1,0:T(8,128)(2,1)} custom-call(s32[17]{0:T(128)S(1)} %concatenate.18.slots_ref._.flip_ref.scalars_ref, bf16[768,2048]{1,0:T(8,128)(2,1)S(1)} %copy-done.26, bf16[768,2048]{1,0:T(8,128)(2,1)S(1)} %copy-done.28, bf16[4,2,512,1024]{3,2,1,0:T(8,128)(2,1)} %bitcast.75, bf16[4,2,512,1024]{3,2,1,0:T(8,128)(2,1)} %bitcast.76, ...), custom_call_target="tpu_custom_call" | custom-call | flops 1 | bytes 1 | tf_op jit(solution)/shard_map/last_layer/pallas_call | solution.py:65
  397.9 3.5 collective-permute-done.26.arrived_ref
  402.4 10.4 %collective-permute-done.25.arrived_ref = bf16[8,32,4224]{2,1,0:T(8,128)(2,1)S(1)} collective-permute-done((bf16[8,32,4224]{2,1,0:T(8,128)(2,1)S(1)}, bf16[8,32,4224]{2,1,0:T(8,128)(2,1)S(1)}, u32[]{:S(2)}, u32[]{:S(2)}) %collective-permute-start.25) | collective-permute-done | bytes 2162720 | tf_op jit(solution)/shard_map/ppermute | solution.py:144
  418.1 10.9 %collective-permute-done.29.arrived_ref = bf16[4,32,4224]{2,1,0:T(8,128)(2,1)S(1)} collective-permute-done((bf16[4,32,4224]{2,1,0:T(8,128)(2,1)S(1)}, bf16[4,32,4224]{2,1,0:T(8,128)(2,1)S(1)}, u32[]{:S(2)}, u32[]{:S(2)}) %collective-permute-start.29) | collective-permute-done | bytes 1081376 | tf_op jit(solution)/shard_map/ppermute | solution.py:144
  431.5 3.7 collective-permute-done.32.arrived_ref
  438.5 11.3 %collective-permute-done.34 = bf16[1,32,4096]{2,1,0:T(8,128)(2,1)S(1)} collective-permute-done((bf16[1,32,4096]{2,1,0:T(8,128)(2,1)S(1)}, bf16[1,32,4096]{2,1,0:T(8,128)(2,1)S(1)}, u32[]{:S(2)}, u32[]{:S(2)}) %collective-permute-start.34) | collective-permute-done | bytes 262176 | tf_op jit(solution)/shard_map/ppermute | solution.py:144
  451.3 2.6 collective-permute-start.33
  455.4 9.3 %collective-permute-done.33 = bf16[1,32,4224]{2,1,0:T(8,128)(2,1)S(1)} collective-permute-done((bf16[1,32,4224]{2,1,0:T(8,128)(2,1)S(1)}, bf16[1,32,4224]{2,1,0:T(8,128)(2,1)S(1)}, u32[]{:S(2)}, u32[]{:S(2)}) %collective-permute-start.33) | collective-permute-done | bytes 270368 | tf_op jit(solution)/shard_map/ppermute | solution.py:144
  (199 shorter events, 81.3 us)
Async XLA Ops:
  7.2 114.1 %all-gather.3.cloned.1.call-start = ((), (), s32[]{:S(2)}) async-start(), calls=%async_computation | async-start | bytes 6758400 | tf_op jit(solution)/shard_map/all_gather | solution.py:925
  8.0 40.3 %copy-start.33 = (bf16[2,128,1024]{2,1,0:T(8,128)(2,1)S(1)}, bf16[2,128,1024]{2,1,0:T(8,128)(2,1)}, u32[]{:S(2)}) copy-start(bf16[2,128,1024]{2,1,0:T(8,128)(2,1)} %param.23) | copy-start | bytes 1572868
  11.3 194.0 %all-gather.5.cloned.1.call-start = ((), (), s32[]{:S(2)}) async-start(), calls=%async_computation.1 | async-start | bytes 8650752 | tf_op jit(solution)/shard_map/all_gather | solution.py:930
  12.8 60.4 %copy-start.36 = (bf16[32,4096]{1,0:T(8,128)(2,1)S(1)}, bf16[32,4096]{1,0:T(8,128)(2,1)}, u32[]{:S(2)}) copy-start(bf16[32,4096]{1,0:T(8,128)(2,1)} %param.37) | copy-start | bytes 786436
  13.9 13.8 %collective-permute-start = (bf16[32,5120]{1,0:T(8,128)(2,1)S(1)}, bf16[32,5120]{1,0:T(8,128)(2,1)S(1)}, u32[]{:S(2)}, u32[]{:S(2)}) collective-permute-start(bf16[32,5120]{1,0:T(8,128)(2,1)S(1)} %pad_maximum_fusion), channel_id=1, source_target_pairs={{0,8},{1,9},{2,10},{3,11},{4,12},{5,13},{6,14},{7,15},{8,16},{9,17... | collective-permute-start | bytes 983048 | tf_op jit(solution)/shard_map/ppermute | solution.py:144
  16.9 28.1 %collective-permute-start.1 = (bf16[32,5120]{1,0:T(8,128)(2,1)S(1)}, bf16[32,5120]{1,0:T(8,128)(2,1)S(1)}, u32[]{:S(2)}, u32[]{:S(2)}) collective-permute-start(bf16[32,5120]{1,0:T(8,128)(2,1)S(1)} %pad_maximum_fusion), channel_id=1, source_target_pairs={{0,16},{1,17},{2,18},{3,19},{4,20},{5,21},{6,22},{7,23},{8,24},{9,... | collective-permute-start | bytes 983048 | tf_op jit(solution)/shard_map/ppermute | solution.py:144
  19.5 25.5 %collective-permute-start.2 = (bf16[32,5120]{1,0:T(8,128)(2,1)S(1)}, bf16[32,5120]{1,0:T(8,128)(2,1)S(1)}, u32[]{:S(2)}, u32[]{:S(2)}) collective-permute-start(bf16[32,5120]{1,0:T(8,128)(2,1)S(1)} %pad_maximum_fusion), channel_id=1, source_target_pairs={{0,24},{1,25},{2,26},{3,27},{4,28},{5,29},{6,30},{7,31},{8,0},{9,1... | collective-permute-start | bytes 983048 | tf_op jit(solution)/shard_map/ppermute | solution.py:144
  46.7 24.4 %collective-permute-start.6 = (bf16[4,32,5120]{2,1,0:T(8,128)(2,1)}, bf16[4,32,5120]{2,1,0:T(8,128)(2,1)}, u32[]{:S(2)}, u32[]{:S(2)}) collective-permute-start(bf16[4,32,5120]{2,1,0:T(8,128)(2,1)} %bitcast.5.refs_0_), channel_id=1, source_target_pairs={{0,1},{1,0},{2,3},{3,2},{4,6},{5,7},{6,4},{7,5},{8,9},{9,8},{10,11... | collective-permute-start | bytes 3932168 | tf_op jit(solution)/shard_map/ppermute | solution.py:144
  49.4 83.1 %copy-start.29 = (bf16[256,1024]{1,0:T(8,128)(2,1)}, bf16[256,1024]{1,0:T(8,128)(2,1)S(1)}, u32[]{:S(2)}) copy-start(bf16[256,1024]{1,0:T(8,128)(2,1)S(1)} %relabel.2.inputs_ref) | copy-start | bytes 1572868
  71.1 40.0 %collective-permute-start.8 = (bf16[4,32,5120]{2,1,0:T(8,128)(2,1)}, bf16[4,32,5120]{2,1,0:T(8,128)(2,1)S(1)}, u32[]{:S(2)}, u32[]{:S(2)}) collective-permute-start(bf16[4,32,5120]{2,1,0:T(8,128)(2,1)} %bitcast.5.refs_0_), channel_id=1, source_target_pairs={{0,2},{1,3},{2,0},{3,1},{4,5},{5,4},{6,7},{7,6},{8,10},{9,11},{10,... | collective-permute-start | bytes 3932168 | tf_op jit(solution)/shard_map/ppermute | solution.py:144
  72.8 41.8 %collective-permute-start.9 = (bf16[4,32,5120]{2,1,0:T(8,128)(2,1)}, bf16[4,32,5120]{2,1,0:T(8,128)(2,1)S(1)}, u32[]{:S(2)}, u32[]{:S(2)}) collective-permute-start(bf16[4,32,5120]{2,1,0:T(8,128)(2,1)} %collective-permute-done.6.refs_1_), channel_id=1, source_target_pairs={{0,2},{1,3},{2,0},{3,1},{4,5},{5,4},{6,7},{7,6},{8,10},{9,11},{10,... | collective-permute-start | bytes 3932168 | tf_op jit(solution)/shard_map/ppermute | solution.py:144
  73.2 20.5 %collective-permute-start.3 = (bf16[32,4096]{1,0:T(8,128)(2,1)S(1)}, bf16[32,4096]{1,0:T(8,128)(2,1)S(1)}, u32[]{:S(2)}, u32[]{:S(2)}) collective-permute-start(bf16[32,4096]{1,0:T(8,128)(2,1)S(1)} %copy-done.36), channel_id=1, source_target_pairs={{0,8},{1,9},{2,10},{3,11},{4,12},{5,13},{6,14},{7,15},{8,16},{9,17... | collective-permute-start | bytes 786440 | tf_op jit(solution)/shard_map/ppermute | solution.py:144
  78.5 31.0 %collective-permute-start.4 = (bf16[32,4096]{1,0:T(8,128)(2,1)S(1)}, bf16[32,4096]{1,0:T(8,128)(2,1)S(1)}, u32[]{:S(2)}, u32[]{:S(2)}) collective-permute-start(bf16[32,4096]{1,0:T(8,128)(2,1)S(1)} %copy-done.36), channel_id=1, source_target_pairs={{0,16},{1,17},{2,18},{3,19},{4,20},{5,21},{6,22},{7,23},{8,24},{9,... | collective-permute-start | bytes 786440 | tf_op jit(solution)/shard_map/ppermute | solution.py:144
  81.5 28.1 %collective-permute-start.5 = (bf16[32,4096]{1,0:T(8,128)(2,1)S(1)}, bf16[32,4096]{1,0:T(8,128)(2,1)S(1)}, u32[]{:S(2)}, u32[]{:S(2)}) collective-permute-start(bf16[32,4096]{1,0:T(8,128)(2,1)S(1)} %copy-done.36), channel_id=1, source_target_pairs={{0,24},{1,25},{2,26},{3,27},{4,28},{5,29},{6,30},{7,31},{8,0},{9,1... | collective-permute-start | bytes 786440 | tf_op jit(solution)/shard_map/ppermute | solution.py:144
  111.1 10.2 %copy-start.10 = (bf16[2,384,1024]{2,1,0:T(8,128)(2,1)S(1)}, bf16[2,384,1024]{2,1,0:T(8,128)(2,1)}, u32[]{:S(2)}) copy-start(bf16[2,384,1024]{2,1,0:T(8,128)(2,1)} %param.22) | copy-start | bytes 4718596
  119.7 12.8 %collective-permute-start.10 = (bf16[4,128,5120]{2,1,0:T(8,128)(2,1)}, bf16[4,128,5120]{2,1,0:T(8,128)(2,1)}, u32[]{:S(2)}, u32[]{:S(2)}) collective-permute-start(bf16[4,128,5120]{2,1,0:T(8,128)(2,1)} %bitcast.12), channel_id=1, source_target_pairs={{0,4},{1,5},{2,6},{3,7},{4,0},{5,1},{6,2},{7,3},{8,12},{9,13},{10,... | collective-permute-start | bytes 15728648 | tf_op jit(solution)/shard_map/ppermute | solution.py:144
  119.7 17.5 %collective-permute-start.7 = (bf16[4,32,4096]{2,1,0:T(8,128)(2,1)}, bf16[4,32,4096]{2,1,0:T(8,128)(2,1)}, u32[]{:S(2)}, u32[]{:S(2)}) collective-permute-start(bf16[4,32,4096]{2,1,0:T(8,128)(2,1)} %bitcast.11.refs_0_), channel_id=1, source_target_pairs={{0,1},{1,0},{2,3},{3,2},{4,6},{5,7},{6,4},{7,5},{8,9},{9,8},{10,11... | collective-permute-start | bytes 3145736 | tf_op jit(solution)/shard_map/ppermute | solution.py:144
  137.2 32.9 %collective-permute-start.11 = (bf16[4,32,4096]{2,1,0:T(8,128)(2,1)}, bf16[4,32,4096]{2,1,0:T(8,128)(2,1)S(1)}, u32[]{:S(2)}, u32[]{:S(2)}) collective-permute-start(bf16[4,32,4096]{2,1,0:T(8,128)(2,1)} %bitcast.11.refs_0_), channel_id=1, source_target_pairs={{0,2},{1,3},{2,0},{3,1},{4,5},{5,4},{6,7},{7,6},{8,10},{9,11},{10,... | collective-permute-start | bytes 3145736 | tf_op jit(solution)/shard_map/ppermute | solution.py:144
  138.7 31.4 %collective-permute-start.12 = (bf16[4,32,4096]{2,1,0:T(8,128)(2,1)}, bf16[4,32,4096]{2,1,0:T(8,128)(2,1)S(1)}, u32[]{:S(2)}, u32[]{:S(2)}) collective-permute-start(bf16[4,32,4096]{2,1,0:T(8,128)(2,1)} %collective-permute-done.7.refs_1_), channel_id=1, source_target_pairs={{0,2},{1,3},{2,0},{3,1},{4,5},{5,4},{6,7},{7,6},{8,10},{9,11},{10,... | collective-permute-start | bytes 3145736 | tf_op jit(solution)/shard_map/ppermute | solution.py:144
  163.5 11.7 %copy-start.8 = (bf16[768,1024]{1,0:T(8,128)(2,1)}, bf16[768,1024]{1,0:T(8,128)(2,1)S(1)}, u32[]{:S(2)}) copy-start(bf16[768,1024]{1,0:T(8,128)(2,1)S(1)} %project_query.1.query_ref) | copy-start | bytes 4718596
  175.2 7.5 %collective-permute-start.13 = (bf16[4,128,4096]{2,1,0:T(8,128)(2,1)}, bf16[4,128,4096]{2,1,0:T(8,128)(2,1)}, u32[]{:S(2)}, u32[]{:S(2)}) collective-permute-start(bf16[4,128,4096]{2,1,0:T(8,128)(2,1)} %bitcast.25), channel_id=1, source_target_pairs={{0,4},{1,5},{2,6},{3,7},{4,0},{5,1},{6,2},{7,3},{8,12},{9,13},{10,... | collective-permute-start | bytes 12582920 | tf_op jit(solution)/shard_map/ppermute | solution.py:144
  182.2 17.2 %copy-start.6 = (bf16[768,1024]{1,0:T(8,128)(2,1)}, bf16[768,1024]{1,0:T(8,128)(2,1)S(1)}, u32[]{:S(2)}) copy-start(bf16[768,1024]{1,0:T(8,128)(2,1)S(1)} %get-tuple-element.381.inputs_ref) | copy-start | bytes 4718596
  182.7 16.7 %copy-start.5 = (bf16[2,384,1024]{2,1,0:T(8,128)(2,1)S(1)}, bf16[2,384,1024]{2,1,0:T(8,128)(2,1)}, u32[]{:S(2)}) copy-start(bf16[2,384,1024]{2,1,0:T(8,128)(2,1)} %param.25) | copy-start | bytes 4718596
  205.2 11.5 %collective-permute-start.14 = (bf16[2048,1024]{1,0:T(8,128)(2,1)}, bf16[2048,1024]{1,0:T(8,128)(2,1)}, u32[]{:S(2)}, u32[]{:S(2)}) collective-permute-start(bf16[2048,1024]{1,0:T(8,128)(2,1)} %ff_out_grad_other.1), channel_id=1, source_target_pairs={{0,4},{1,5},{2,6},{3,7},{4,0},{5,1},{6,2},{7,3},{8,12},{9,13},{10,... | collective-permute-start | bytes 12582920 | tf_op jit(solution)/shard_map/ppermute | solution.py:144
  205.3 11.4 %copy-start.25 = (bf16[768,2048]{1,0:T(8,128)(2,1)S(1)}, bf16[768,2048]{1,0:T(8,128)(2,1)}, u32[]{:S(2)}) copy-start(bf16[768,2048]{1,0:T(8,128)(2,1)} %copy-done.24) | copy-start | bytes 9437188
  216.7 8.9 %copy-start.3 = (bf16[768,4096]{1,0:T(8,128)(2,1)}, bf16[768,4096]{1,0:T(8,128)(2,1)S(1)}, u32[]{:S(2)}) copy-start(bf16[768,4096]{1,0:T(8,128)(2,1)S(1)} %get-tuple-element.404.grads_ref) | copy-start | bytes 18874372
  230.5 19.1 %collective-permute-start.16 = (bf16[512,4096]{1,0:T(8,128)(2,1)S(1)}, bf16[512,4096]{1,0:T(8,128)(2,1)S(1)}, u32[]{:S(2)}, u32[]{:S(2)}) collective-permute-start(bf16[512,4096]{1,0:T(8,128)(2,1)S(1)} %ff_in_grad_other.1), channel_id=1, source_target_pairs={{0,4},{1,5},{2,6},{3,7},{4,0},{5,1},{6,2},{7,3},{8,12},{9,13},{10,... | collective-permute-start | bytes 12582920 | tf_op jit(solution)/shard_map/ppermute | solution.py:144
  231.0 38.8 %collective-permute-start.15 = (bf16[8,128,1024]{2,1,0:T(8,128)(2,1)S(1)}, bf16[8,128,1024]{2,1,0:T(8,128)(2,1)S(1)}, u32[]{:S(2)}, u32[]{:S(2)}) collective-permute-start(bf16[8,128,1024]{2,1,0:T(8,128)(2,1)S(1)} %get-tuple-element.406), channel_id=1, source_target_pairs={{0,2},{1,3},{2,0},{3,1},{4,5},{5,4},{6,7},{7,6},{8,10},{9,11},{10,... | collective-permute-start | bytes 6291464 | tf_op jit(solution)/shard_map/ppermute | solution.py:144
  232.4 17.2 %copy-start.4 = (bf16[768,4096]{1,0:T(8,128)(2,1)S(1)}, bf16[768,4096]{1,0:T(8,128)(2,1)}, u32[]{:S(2)}) copy-start(bf16[768,4096]{1,0:T(8,128)(2,1)} %copy-done.3) | copy-start | bytes 18874372
  276.1 10.7 %collective-permute-start.17 = (bf16[512,4096]{1,0:T(8,128)(2,1)S(1)}, bf16[512,4096]{1,0:T(8,128)(2,1)S(1)}, u32[]{:S(2)}, u32[]{:S(2)}) collective-permute-start(bf16[512,4096]{1,0:T(8,128)(2,1)S(1)} %cross_out_grad_other.1), channel_id=1, source_target_pairs={{0,4},{1,5},{2,6},{3,7},{4,0},{5,1},{6,2},{7,3},{8,12},{9,13},{10,... | collective-permute-start | bytes 12582920 | tf_op jit(solution)/shard_map/ppermute | solution.py:144
  276.2 42.4 %collective-permute-start.18 = (bf16[8,32,4096]{2,1,0:T(8,128)(2,1)S(1)}, bf16[8,32,4096]{2,1,0:T(8,128)(2,1)S(1)}, u32[]{:S(2)}, u32[]{:S(2)}) collective-permute-start(bf16[8,32,4096]{2,1,0:T(8,128)(2,1)S(1)} %get-tuple-element.462), channel_id=1, source_target_pairs={{0,2},{1,3},{2,0},{3,1},{4,5},{5,4},{6,7},{7,6},{8,10},{9,11},{10,... | collective-permute-start | bytes 6291464 | tf_op jit(solution)/shard_map/ppermute | solution.py:144
  277.2 39.2 %collective-permute-start.19 = (bf16[4,128,1024]{2,1,0:T(8,128)(2,1)S(1)}, bf16[4,128,1024]{2,1,0:T(8,128)(2,1)S(1)}, u32[]{:S(2)}, u32[]{:S(2)}) collective-permute-start(bf16[4,128,1024]{2,1,0:T(8,128)(2,1)S(1)} %get-tuple-element.463), channel_id=1, source_target_pairs={{0,1},{1,0},{2,3},{3,2},{4,6},{5,7},{6,4},{7,5},{8,9},{9,8},{10,11... | collective-permute-start | bytes 3145736 | tf_op jit(solution)/shard_map/ppermute | solution.py:144
  286.8 40.2 %copy-start.18 = (bf16[768,1024]{1,0:T(8,128)(2,1)}, bf16[768,1024]{1,0:T(8,128)(2,1)S(1)}, u32[]{:S(2)}) copy-start(bf16[768,1024]{1,0:T(8,128)(2,1)S(1)} %get-tuple-element.465.grads_ref) | copy-start | bytes 4718596
  329.6 28.6 %collective-permute-start.21 = (bf16[512,4096]{1,0:T(8,128)(2,1)}, bf16[512,4096]{1,0:T(8,128)(2,1)}, u32[]{:S(2)}, u32[]{:S(2)}) collective-permute-start(bf16[512,4096]{1,0:T(8,128)(2,1)} %self_out_grad_other.1), channel_id=1, source_target_pairs={{0,4},{1,5},{2,6},{3,7},{4,0},{5,1},{6,2},{7,3},{8,12},{9,13},{10,... | collective-permute-start | bytes 12582920 | tf_op jit(solution)/shard_map/ppermute | solution.py:144
  329.6 43.0 %collective-permute-start.23 = (bf16[8,32,4096]{2,1,0:T(8,128)(2,1)}, bf16[8,32,4096]{2,1,0:T(8,128)(2,1)}, u32[]{:S(2)}, u32[]{:S(2)}) collective-permute-start(bf16[8,32,4096]{2,1,0:T(8,128)(2,1)} %get-tuple-element.524), channel_id=1, source_target_pairs={{0,2},{1,3},{2,0},{3,1},{4,5},{5,4},{6,7},{7,6},{8,10},{9,11},{10,... | collective-permute-start | bytes 6291464 | tf_op jit(solution)/shard_map/ppermute | solution.py:144
  331.0 39.3 %collective-permute-start.24 = (bf16[4,32,4096]{2,1,0:T(8,128)(2,1)}, bf16[4,32,4096]{2,1,0:T(8,128)(2,1)}, u32[]{:S(2)}, u32[]{:S(2)}) collective-permute-start(bf16[4,32,4096]{2,1,0:T(8,128)(2,1)} %get-tuple-element.525), channel_id=1, source_target_pairs={{0,1},{1,0},{2,3},{3,2},{4,6},{5,7},{6,4},{7,5},{8,9},{9,8},{10,11... | collective-permute-start | bytes 3145736 | tf_op jit(solution)/shard_map/ppermute | solution.py:144
  331.8 23.6 %collective-permute-start.22 = (bf16[2,128,1024]{2,1,0:T(8,128)(2,1)}, bf16[2,128,1024]{2,1,0:T(8,128)(2,1)}, u32[]{:S(2)}, u32[]{:S(2)}) collective-permute-start(bf16[2,128,1024]{2,1,0:T(8,128)(2,1)} %get-tuple-element.499), channel_id=1, source_target_pairs={{0,8},{1,9},{2,10},{3,11},{4,12},{5,13},{6,14},{7,15},{8,0},{9,1},... | collective-permute-start | bytes 1572872 | tf_op jit(solution)/shard_map/ppermute | solution.py:144
  355.3 2.9 collective-permute-start.20
  375.1 37.6 %collective-permute-start.25 = (bf16[8,32,4224]{2,1,0:T(8,128)(2,1)S(1)}, bf16[8,32,4224]{2,1,0:T(8,128)(2,1)S(1)}, u32[]{:S(2)}, u32[]{:S(2)}) collective-permute-start(bf16[8,32,4224]{2,1,0:T(8,128)(2,1)S(1)} %get-tuple-element.544), channel_id=1, source_target_pairs={{0,2},{1,3},{2,0},{3,1},{4,5},{5,4},{6,7},{7,6},{8,10},{9,11},{10,... | collective-permute-start | bytes 6488072 | tf_op jit(solution)/shard_map/ppermute | solution.py:144
  375.4 26.0 %collective-permute-start.26 = (bf16[4,32,4096]{2,1,0:T(8,128)(2,1)S(1)}, bf16[4,32,4096]{2,1,0:T(8,128)(2,1)S(1)}, u32[]{:S(2)}, u32[]{:S(2)}) collective-permute-start(bf16[4,32,4096]{2,1,0:T(8,128)(2,1)S(1)} %get-tuple-element.545), channel_id=1, source_target_pairs={{0,1},{1,0},{2,3},{3,2},{4,6},{5,7},{6,4},{7,5},{8,9},{9,8},{10,11... | collective-permute-start | bytes 3145736 | tf_op jit(solution)/shard_map/ppermute | solution.py:144
  377.2 20.0 %collective-permute-start.28 = (bf16[2,32,4096]{2,1,0:T(8,128)(2,1)S(1)}, bf16[2,32,4096]{2,1,0:T(8,128)(2,1)S(1)}, u32[]{:S(2)}, u32[]{:S(2)}) collective-permute-start(bf16[2,32,4096]{2,1,0:T(8,128)(2,1)S(1)} %get-tuple-element.547), channel_id=1, source_target_pairs={{0,8},{1,9},{2,10},{3,11},{4,12},{5,13},{6,14},{7,15},{8,0},{9,1},... | collective-permute-start | bytes 1572872 | tf_op jit(solution)/shard_map/ppermute | solution.py:144
  379.2 18.7 %collective-permute-start.27 = (bf16[1,128,1024]{2,1,0:T(8,128)(2,1)S(1)}, bf16[1,128,1024]{2,1,0:T(8,128)(2,1)S(1)}, u32[]{:S(2)}, u32[]{:S(2)}) collective-permute-start(bf16[1,128,1024]{2,1,0:T(8,128)(2,1)S(1)} %get-tuple-element.546), channel_id=1, source_target_pairs={{0,16},{1,17},{2,18},{3,19},{4,20},{5,21},{6,22},{7,23},{8,24},{9,... | collective-permute-start | bytes 786440 | tf_op jit(solution)/shard_map/ppermute | solution.py:144
  413.8 15.2 %collective-permute-start.29 = (bf16[4,32,4224]{2,1,0:T(8,128)(2,1)S(1)}, bf16[4,32,4224]{2,1,0:T(8,128)(2,1)S(1)}, u32[]{:S(2)}, u32[]{:S(2)}) collective-permute-start(bf16[4,32,4224]{2,1,0:T(8,128)(2,1)S(1)} %get-tuple-element.567), channel_id=1, source_target_pairs={{0,1},{1,0},{2,3},{3,2},{4,6},{5,7},{6,4},{7,5},{8,9},{9,8},{10,11... | collective-permute-start | bytes 3244040 | tf_op jit(solution)/shard_map/ppermute | solution.py:144
  414.5 20.6 %collective-permute-start.32 = (bf16[2,32,4096]{2,1,0:T(8,128)(2,1)S(1)}, bf16[2,32,4096]{2,1,0:T(8,128)(2,1)S(1)}, u32[]{:S(2)}, u32[]{:S(2)}) collective-permute-start(bf16[2,32,4096]{2,1,0:T(8,128)(2,1)S(1)} %get-tuple-element.576), channel_id=1, source_target_pairs={{0,8},{1,9},{2,10},{3,11},{4,12},{5,13},{6,14},{7,15},{8,0},{9,1},... | collective-permute-start | bytes 1572872 | tf_op jit(solution)/shard_map/ppermute | solution.py:144
  416.9 18.9 %collective-permute-start.31 = (bf16[1,32,4096]{2,1,0:T(8,128)(2,1)S(1)}, bf16[1,32,4096]{2,1,0:T(8,128)(2,1)S(1)}, u32[]{:S(2)}, u32[]{:S(2)}) collective-permute-start(bf16[1,32,4096]{2,1,0:T(8,128)(2,1)S(1)} %get-tuple-element.575), channel_id=1, source_target_pairs={{0,16},{1,17},{2,18},{3,19},{4,20},{5,21},{6,22},{7,23},{8,24},{9,... | collective-permute-start | bytes 786440 | tf_op jit(solution)/shard_map/ppermute | solution.py:144
  429.8 20.8 %collective-permute-start.30 = (bf16[2,32,4224]{2,1,0:T(8,128)(2,1)S(1)}, bf16[2,32,4224]{2,1,0:T(8,128)(2,1)S(1)}, u32[]{:S(2)}, u32[]{:S(2)}) collective-permute-start(bf16[2,32,4224]{2,1,0:T(8,128)(2,1)S(1)} %get-tuple-element.574), channel_id=1, source_target_pairs={{0,8},{1,9},{2,10},{3,11},{4,12},{5,13},{6,14},{7,15},{8,0},{9,1},... | collective-permute-start | bytes 1622024 | tf_op jit(solution)/shard_map/ppermute | solution.py:144
  435.8 13.9 %collective-permute-start.34 = (bf16[1,32,4096]{2,1,0:T(8,128)(2,1)S(1)}, bf16[1,32,4096]{2,1,0:T(8,128)(2,1)S(1)}, u32[]{:S(2)}, u32[]{:S(2)}) collective-permute-start(bf16[1,32,4096]{2,1,0:T(8,128)(2,1)S(1)} %get-tuple-element.593), channel_id=1, source_target_pairs={{0,16},{1,17},{2,18},{3,19},{4,20},{5,21},{6,22},{7,23},{8,24},{9,... | collective-permute-start | bytes 786440 | tf_op jit(solution)/shard_map/ppermute | solution.py:144
  451.3 13.4 %collective-permute-start.33 = (bf16[1,32,4224]{2,1,0:T(8,128)(2,1)S(1)}, bf16[1,32,4224]{2,1,0:T(8,128)(2,1)S(1)}, u32[]{:S(2)}, u32[]{:S(2)}) collective-permute-start(bf16[1,32,4224]{2,1,0:T(8,128)(2,1)S(1)} %get-tuple-element.591), channel_id=1, source_target_pairs={{0,16},{1,17},{2,18},{3,19},{4,20},{5,21},{6,22},{7,23},{8,24},{9,... | collective-permute-start | bytes 811016 | tf_op jit(solution)/shard_map/ppermute | solution.py:144
  (28 other events, 131.4 us)
Sparse Core Ops, SparseCore 0:
  11.5 104.4 all-gather.2
  118.8 81.4 all-gather.4
where the time goes:
time: 484 us; the launch traced here: 475 us
  Pallas kernels  263 us (54%)
  waiting for transfers between devices  127 us (26%)
  starting transfers between devices  51.8 us (11%)
  between operations  15.3 us (3%)
  local copies, waits for them, and re-layouts  13.1 us (3%)
  other arithmetic  5.27 us (1%)
    pallas_call x53, Pallas kernels, call(): pl.pallas_call(body, grid_spec=spec, out_shape=out_shape, name=name, inpu...  263 us
    ppermute x35, waiting for transfers between devices, _permute(): return lax.ppermute(value, AXES, pairs)  127 us
    ppermute x35, starting transfers between devices, _permute(): return lax.ppermute(value, AXES, pairs)  51.7 us
  transfers between devices with their start and end apart: 37, of which 14 were waited for; matrix products, arithmetic and copies ran while one was open for 1% of the time, Pallas kernels for 48%

commit v1 on v0

--- a/solution.py
+++ b/solution.py
@@ -25,9 +25,9 @@
     "last_layer": 20,
     "hidden_grad": 14,
     "norm3_grad": 25,
-    "cross_attention_grads": 10,
+    "cross_attention_grads": 13,
     "norm2_grad": 17,
-    "self_attention_grads": 22,
+    "self_attention_grads": 25,
     "norm1_grad": 20,
     "qkv_grad_other": 11,
     "qkv_grad_own": 17,
@@ -291,28 +291,21 @@
         self.kept, sent = combine(self.place, self.kept, self.place.wait(self.arrived))
         self.arrived = self.stages.pop(0)(sent)
 
-    def spread(self):
-        place = self.place
-        while len(self.stages) > len(place.line_bits):
-            self.next()
-        self.kept, *pieces = combine(place, self.kept, place.wait(self.arrived), apart=True)
-        self.arrived = [
-            place.swap_line(piece, mask) for piece, mask in zip(pieces, place.reversed_lines()[1:])
-        ]
-        self.stages = []
-
-    def result(self):
+    def result(self, *widths):
         while self.stages:
             self.next()
-        total = self.kept[0].astype(F32)
-        for arrival in jax.tree.leaves(self.place.wait(self.arrived)):
-            total = total + arrival[0].astype(F32)
-        return total
-
-
-def combine(place, kept, arrived, apart=False):
+        arrived = self.place.wait(self.arrived)
+        parts, at = [], 0
+        for width in widths:
+            here = slice(at, at + width)
+            parts.append(self.kept[0][:, here].astype(F32) + arrived[0][:, here].astype(F32))
+            at += width
+        return parts
+
+
+def combine(place, kept, arrived):
     count, rows, width = kept.shape
-    each = 1 if apart else count // 2
+    each = count // 2
     outs = count // each
     steps = 2 if kept.size > 2**18 and width % 256 == 0 else 1
     tile = width // steps
@@ -814,7 +807,9 @@
     )
 
 
-def attention_grads(place, query, key_value, starts, probability, grad, out_widths, items, per, name):
+def attention_grads(
+    place, query, key_value, starts, probability, attended, grad, out_widths, items, per, name
+):
     count = query.shape[0]
     rows, keys = count // items, key_value.shape[0] // items
     pairs = HEADS // 2
@@ -823,7 +818,7 @@
     column = relative_lanes(place, width)
     alone = len(out_widths) == 1
 
-    def body(scalars_ref, query_ref, key_ref, value_ref, prob_ref, grad_ref, *outs):
+    def body(scalars_ref, query_ref, key_ref, value_ref, prob_ref, attended_ref, grad_ref, *outs):
         for k in range(per):
             pair = pl.program_id(1) * per + k
             at = block_slice(column(pair, scalars_ref[0]), LANES)
@@ -832,10 +827,10 @@
                 weights = prob_ref[0, 2 * k + head]
                 own_grad = own_lanes(head, grad_ref[:, at])
                 prob_grad = nt(own_grad, value_ref[:, lane_block(k)])
-                wide = weights.astype(F32)
-                weighted = wide * prob_grad
-                centre = jnp.sum(weighted, axis=1, keepdims=True)
-                score_grad = (weighted - wide * centre).astype(BF16)
+                centre = jnp.sum(
+                    own_grad.astype(F32) * attended_ref[:, at].astype(F32), axis=1, keepdims=True
+                )
+                score_grad = (weights.astype(F32) * (prob_grad - centre)).astype(BF16)
                 query_total = query_total + nn(
                     score_grad, own_lanes(head, key_ref[:, lane_block(k)], scaling)
                 )
@@ -856,6 +851,7 @@
             spec(rows, 0), spec(keys, starts[0]), spec(keys, starts[1]),
             pl.BlockSpec((1, 2 * per, rows, keys), lambda b, p, s: (b, p, 0, 0)),
             pl.BlockSpec((rows, width), lambda b, p, s: (b, 0)),
+            pl.BlockSpec((rows, width), lambda b, p, s: (b, 0)),
         ],
         [
             pl.BlockSpec((height, wide), lambda b, p, s: (b, 0))
@@ -865,7 +861,7 @@
             jax.ShapeDtypeStruct((items * height, wide), BF16)
             for height, wide in zip(heights, out_widths)
         ],
-        (query, key_value, key_value, pinned(probability), grad),
+        (query, key_value, key_value, pinned(probability), attended, grad),
         name=name,
     )
 
@@ -973,7 +969,7 @@
     ff_in_own = ff_in_terms.sums()
     attended2_grad = back_project(place, cross_round, w_mid, at_cross, "attended2_grad")
     query2_grad, text_kv_grad = attention_grads(
-        place, query2, text_kv, (0, pairs), probs2, attended2_grad, (width, 2 * width), items, 4,
+        place, query2, text_kv, (0, pairs), probs2, attended2, attended2_grad, (width, 2 * width), items, 4,
         "cross_attention_grads",
     )
     ff_out_sums.next()
@@ -991,7 +987,7 @@
     middle_own = middle_terms.sums()
     attended1_grad = back_project(place, self_round, w_mid, at_self, "attended1_grad")
     (projected_grad,) = attention_grads(
-        place, projected, projected, (pairs, 2 * pairs), probs1, attended1_grad, (3 * width,), items, 4,
+        place, projected, projected, (pairs, 2 * pairs), probs1, attended1, attended1_grad, (3 * width,), items, 4,
         "self_attention_grads",
     )
     ff_out_sums.next()
@@ -1001,6 +997,14 @@
     )
 
     middle_sums = Scatter(place, *middle_own)
+    text_grad = back_project_natural(place, text_kv_grad, w_mid, at_kv, "text_grad")
+    last_own = last_terms.sums()
+    result = last_layer(place, middle, w_out, out_bias, values2)
+    ff_out_sums.next()
+    ff_in_sums.next()
+    middle_sums.next()
+
+    last_sums = Scatter(place, *last_own)
     tokens_grad, sums1 = back_project_norm(
         place, projected_grad, w_qkv, 0, values0, gain1, self_grad, (BF16,), "norm1_grad"
     )
@@ -1008,25 +1012,21 @@
         sums1[0], sums1[1], sums2[0], sums2[1], sums3[0], sums3[1], in_bias_sum[0], sums3[2]
     ), shard_rows))
     small_terms = WeightGrad(place, table, jnp.eye(LANES, dtype=BF16), "small_grad")
-    ff_out_sums.next()
-    last_own = last_terms.sums(small_terms)
     ff_in_sums.next()
-    middle_sums.next()
-
-    last_sums = Scatter(place, *last_own)
-    text_grad = back_project_natural(place, text_kv_grad, w_mid, at_kv, "text_grad")
-    result = last_layer(place, middle, w_out, out_bias, values2)
-    ff_in_sums.next()
-    ff_out_grad = ff_out_sums.result()
+    (ff_out_grad,) = ff_out_sums.result(width)
+    small_sums = Scatter(place, *small_terms.sums())
     middle_sums.next()
     last_sums.next()
     last_sums.next()
+    small_sums.next()
     middle_sums.next()
-    ff_in_grad = ff_in_sums.result()
+    (ff_in_grad,) = ff_in_sums.result(ff_in.shape[1])
+    small_sums.next()
     last_sums.next()
-    middle_grads = middle_sums.result()
-    last_grads = last_sums.result()
-    small_grads = last_grads[:, 4 * width :].T
+    small_sums.next()
+    cross_kv_grad, cross_query_grad, cross_out_grad = middle_sums.result(2 * width, width, width)
+    small_grads = small_sums.result(LANES)[0].T
+    qkv_grad, self_out_grad = last_sums.result(3 * width, width)
     own, at = [], 0
     for size in sizes:
         own.append(small_grads[at : at + size // shard_rows].reshape(-1))
@@ -1037,13 +1037,13 @@
         text_grad.reshape(items, text, width),
         own[0],
         own[1],
-        last_grads[:, : 3 * width],
-        last_grads[:, 3 * width : 4 * width],
+        qkv_grad,
+        self_out_grad,
         own[2],
         own[3],
-        middle_grads[:, at_query : at_query + width],
-        middle_grads[:, at_kv : at_kv + 2 * width],
-        middle_grads[:, at_cross : at_cross + width],
+        cross_query_grad,
+        cross_kv_grad,
+        cross_out_grad,
         own[4],
         own[5],
         ff_in_grad,

time: 484 us -> 480 us (level)
  waiting for transfers between devices: 127 us -> 115 us
  starting transfers between devices: 51.8 us -> 60.6 us
  Pallas kernels: 263 us -> 257 us
    ppermute x35 -> x39, waiting for transfers between devices: 127 us -> 115 us  [_permute(): return lax.ppermute(value, AXES, pairs)]
    ppermute x35 -> x39, starting transfers between devices: 51.7 us -> 60.5 us  [_permute(): return lax.ppermute(value, AXES, pairs)]
    pallas_call x53 -> x56, Pallas kernels: 263 us -> 257 us  [call(): pl.pallas_call(body, grid_spec=spec, out_shape=out_shape, name=name, inpu...]
  transfers between devices with their start and end apart: 37 -> 41, of which waited for: 14 -> 14; matrix products, arithmetic and copies ran while one was open for 1% -> 2% of each run, Pallas kernels for 48% -> 48%
where the time goes in v1:
time: 480 us; the launch traced here: 470 us
  Pallas kernels  257 us (54%)
  waiting for transfers between devices  115 us (24%)
  starting transfers between devices  60.6 us (13%)
  between operations  15.3 us (3%)
  local copies, waits for them, and re-layouts  13.1 us (3%)
  other arithmetic  9.05 us (2%)
    pallas_call x56, Pallas kernels, call(): pl.pallas_call(body, grid_spec=spec, out_shape=out_shape, name=name, inpu...  257 us
    ppermute x39, waiting for transfers between devices, _permute(): return lax.ppermute(value, AXES, pairs)  115 us
    ppermute x39, starting transfers between devices, _permute(): return lax.ppermute(value, AXES, pairs)  60.5 us
  transfers between devices with their start and end apart: 41, of which 14 were waited for; matrix products, arithmetic and copies ran while one was open for 2% of the time, Pallas kernels for 48%

profile of v1, /device:TPU:0, one launch (start us, length us, event | category | flops | bytes accessed | tf_op | source)
XLA Modules:
  0.0 470.1 jit_solution(7086065469071620569)
XLA Ops:
  13.8 3.1 collective-permute-start
  16.9 2.6 collective-permute-start.1
  20.9 6.8 %collective-permute-done = bf16[32,5120]{1,0:T(8,128)(2,1)S(1)} collective-permute-done((bf16[32,5120]{1,0:T(8,128)(2,1)S(1)}, bf16[32,5120]{1,0:T(8,128)(2,1)S(1)}, u32[]{:S(2)}, u32[]{:S(2)}) %collective-permute-start) | collective-permute-done | bytes 327712 | tf_op jit(solution)/shard_map/ppermute | solution.py:144
  27.6 17.4 %collective-permute-done.1 = bf16[32,5120]{1,0:T(8,128)(2,1)S(1)} collective-permute-done((bf16[32,5120]{1,0:T(8,128)(2,1)S(1)}, bf16[32,5120]{1,0:T(8,128)(2,1)S(1)}, u32[]{:S(2)}, u32[]{:S(2)}) %collective-permute-start.1) | collective-permute-done | bytes 327712 | tf_op jit(solution)/shard_map/ppermute | solution.py:144
  49.4 21.7 %collective-permute-done.6.refs_1_ = bf16[4,32,5120]{2,1,0:T(8,128)(2,1)} collective-permute-done((bf16[4,32,5120]{2,1,0:T(8,128)(2,1)}, bf16[4,32,5120]{2,1,0:T(8,128)(2,1)}, u32[]{:S(2)}, u32[]{:S(2)}) %collective-permute-start.6) | collective-permute-done | bytes 1310752 | tf_op jit(solution)/shard_map/ppermute | solution.py:144
  73.1 5.4 %collective-permute-start.3 = (bf16[32,4096]{1,0:T(8,128)(2,1)S(1)}, bf16[32,4096]{1,0:T(8,128)(2,1)S(1)}, u32[]{:S(2)}, u32[]{:S(2)}) collective-permute-start(bf16[32,4096]{1,0:T(8,128)(2,1)S(1)} %copy-done.29), channel_id=1, source_target_pairs={{0,8},{1,9},{2,10},{3,11},{4,12},{5,13},{6,14},{7,15},{8,16},{9,17... | collective-permute-start | bytes 786440 | tf_op jit(solution)/shard_map/ppermute | solution.py:144
  78.5 3.0 collective-permute-start.4
  82.7 10.9 %collective-permute-done.3 = bf16[32,4096]{1,0:T(8,128)(2,1)S(1)} collective-permute-done((bf16[32,4096]{1,0:T(8,128)(2,1)S(1)}, bf16[32,4096]{1,0:T(8,128)(2,1)S(1)}, u32[]{:S(2)}, u32[]{:S(2)}) %collective-permute-start.3) | collective-permute-done | bytes 262176 | tf_op jit(solution)/shard_map/ppermute | solution.py:144
  93.7 15.8 %collective-permute-done.4 = bf16[32,4096]{1,0:T(8,128)(2,1)S(1)} collective-permute-done((bf16[32,4096]{1,0:T(8,128)(2,1)S(1)}, bf16[32,4096]{1,0:T(8,128)(2,1)S(1)}, u32[]{:S(2)}, u32[]{:S(2)}) %collective-permute-start.4) | collective-permute-done | bytes 262176 | tf_op jit(solution)/shard_map/ppermute | solution.py:144
  111.1 3.4 collective-permute-done.9.refs_3_
  114.5 5.1 %interleave.6 = bf16[4,4,32,5120]{3,2,1,0:T(8,128)(2,1)} custom-call(s32[17]{0:T(128)S(1)} %concatenate.18.slots_ref._.flip_ref.scalars_ref, bf16[4,32,5120]{2,1,0:T(8,128)(2,1)} %bitcast.5.refs_0_, bf16[4,32,5120]{2,1,0:T(8,128)(2,1)} %collective-permute-done.6.refs_1_, bf16[4,32,5120]{2,1,0:T(8,128)(2,1)S(1)} %collective-permute-done.8.refs_2_, ...), custom_call_target="tpu_custom_call" | custom-call | flops 1 | bytes 1 | tf_op jit(solution)/shard_map/interleave/pallas_call | solution.py:65
  121.3 3.1 norm.1
  124.4 8.0 %project_qkv.1.query_ref.key_ref.value_ref = bf16[768,3072]{1,0:T(8,128)(2,1)S(1)} custom-call(s32[17]{0:T(128)S(1)} %concatenate.18.slots_ref._.flip_ref.scalars_ref, bf16[768,1024]{1,0:T(8,128)(2,1)S(1)} %get-tuple-element.366.inputs_ref, bf16[4,2,128,3200]{3,2,1,0:T(8,128)(2,1)} %bitcast.75, bf16[4,2,128,3200]{3,2,1,0:T(8,128)(2,1)} %bitcast.76), custom_call_target="tpu_custom_call" | custom-call | flops 1 | bytes 1 | tf_op jit(solution)/shard_map/project_qkv/pallas_call | solution.py:65
  132.4 4.7 project_text.1.key_ref.value_ref
  139.2 13.8 %self_attention.1 = (bf16[768,1024]{1,0:T(8,128)(2,1)S(1)}, bf16[2,16,384,384]{3,2,1,0:T(8,128)(2,1)}) custom-call(s32[17]{0:T(128)S(1)} %concatenate.18.slots_ref._.flip_ref.scalars_ref, bf16[768,3072]{1,0:T(8,128)(2,1)S(1)} %project_qkv.1.query_ref.key_ref.value_ref, bf16[768,3072]{1,0:T(8,128)(2,1)S(1)} %project_qkv.1.query_ref.key_ref.value_ref, ...), custom_call_target="tpu_custom_call" | custom-call | flops 1 | bytes 1 | tf_op jit(solution)/shard_map/self_attention/pallas_call | solution.py:65
  153.0 6.4 %self_out_norm.1 = (f32[768,1024]{1,0:T(8,128)}, bf16[768,1024]{1,0:T(8,128)(2,1)S(1)}) custom-call(s32[17]{0:T(128)S(1)} %concatenate.18.slots_ref._.flip_ref.scalars_ref, bf16[768,1024]{1,0:T(8,128)(2,1)S(1)} %get-tuple-element.379.inputs_ref.attended_ref, bf16[4,1,128,5120]{3,2,1,0:T(8,128)(2,1)} %bitcast.23.own_ref, ...), custom_call_target="tpu_custom_call" | custom-call | flops 1 | bytes 1 | tf_op jit(solution)/shard_map/self_out_norm/pallas_call | solution.py:65
  159.4 3.9 project_query.1.query_ref
  163.4 6.6 %cross_attention.1 = (bf16[768,1024]{1,0:T(8,128)(2,1)S(1)}, bf16[2,16,384,128]{3,2,1,0:T(8,128)(2,1)}) custom-call(s32[17]{0:T(128)S(1)} %concatenate.18.slots_ref._.flip_ref.scalars_ref, bf16[768,1024]{1,0:T(8,128)(2,1)S(1)} %project_query.1.query_ref, bf16[256,2048]{1,0:T(8,128)(2,1)S(1)} %project_text.1.key_ref.value_ref, ...), custom_call_target="tpu_custom_call" | custom-call | flops 1 | bytes 1 | tf_op jit(solution)/shard_map/cross_attention/pallas_call | solution.py:65
  171.1 4.8 %interleave.7 = bf16[4,4,32,4096]{3,2,1,0:T(8,128)(2,1)} custom-call(s32[17]{0:T(128)S(1)} %concatenate.18.slots_ref._.flip_ref.scalars_ref, bf16[4,32,4096]{2,1,0:T(8,128)(2,1)} %bitcast.11.refs_0_, bf16[4,32,4096]{2,1,0:T(8,128)(2,1)} %collective-permute-done.7.refs_1_, bf16[4,32,4096]{2,1,0:T(8,128)(2,1)S(1)} %collective-permute-done.11.refs_2_, ...), custom_call_target="tpu_custom_call" | custom-call | flops 1 | bytes 1 | tf_op jit(solution)/shard_map/interleave/pallas_call | solution.py:65
  177.6 6.7 %cross_out_norm.1 = (f32[768,1024]{1,0:T(8,128)}, bf16[768,1024]{1,0:T(8,128)(2,1)S(1)}) custom-call(s32[17]{0:T(128)S(1)} %concatenate.18.slots_ref._.flip_ref.scalars_ref, bf16[768,1024]{1,0:T(8,128)(2,1)S(1)} %copy-done.8, bf16[4,1,128,5120]{3,2,1,0:T(8,128)(2,1)} %bitcast.23.own_ref, bf16[4,1,128,5120]{3,2,1,0:T(8,128)(2,1)} %bitcast.24.other_ref, ...), custom_call_target="tpu_custom_call" | custom-call | flops 1 | bytes 1 | tf_op jit(solution)/shard_map/cross_out_norm/pallas_call | solution.py:65
  184.3 16.7 %hidden_layer.1 = (bf16[768,2048]{1,0:T(8,128)(2,1)S(1)}, bf16[768,2048]{1,0:T(8,128)(2,1)S(1)}, bf16[768,4096]{1,0:T(8,128)(2,1)}) custom-call(s32[17]{0:T(128)S(1)} %concatenate.18.slots_ref._.flip_ref.scalars_ref, bf16[768,1024]{1,0:T(8,128)(2,1)S(1)} %get-tuple-element.404.inputs_ref, bf16[4,1,128,4096]{3,2,1,0:T(8,128)(2,1)} %bitcast.26.own_ref, ...), custom_call_target="tpu_custom_call" | custom-call | flops 1 | bytes 1 | tf_op jit(solution)/shard_map/hidden_layer/pallas_call | solution.py:65
  201.0 5.9 %ff_out_grad_other.1 = bf16[2048,1024]{1,0:T(8,128)(2,1)} custom-call(s32[17]{0:T(128)S(1)} %concatenate.18.slots_ref._.flip_ref.scalars_ref, bf16[768,2048]{1,0:T(8,128)(2,1)S(1)} %get-tuple-element.410.inputs_ref.inputs_other, bf16[768,1024]{1,0:T(8,128)(2,1)S(1)} %bitcast.55), custom_call_target="tpu_custom_call" | custom-call | flops 1 | bytes 1 | tf_op jit(solution)/shard_map/ff_out_grad_other/pallas_call | solution.py:65
  208.8 11.6 %hidden_grad.1 = (bf16[768,4096]{1,0:T(8,128)(2,1)S(1)}, f32[1,4096]{1,0:T(1,128)S(1)}) custom-call(s32[17]{0:T(128)S(1)} %concatenate.18.slots_ref._.flip_ref.scalars_ref, bf16[768,1024]{1,0:T(8,128)(2,1)S(1)} %bitcast.56, bf16[4,2,512,1024]{3,2,1,0:T(8,128)(2,1)} %bitcast.79, bf16[4,2,512,1024]{3,2,1,0:T(8,128)(2,1)} %bitcast.80, ...), custom_call_target="tpu_custom_call" | custom-call | flops 1 | bytes 1 | tf_op jit(solution)/shard_map/hidden_grad/pallas_call | solution.py:65
  220.4 8.8 %ff_out_grad_own.1 = (bf16[8,128,1024]{2,1,0:T(8,128)(2,1)S(1)}, bf16[8,128,1024]{2,1,0:T(8,128)(2,1)S(1)}) custom-call(s32[17]{0:T(128)S(1)} %concatenate.18.slots_ref._.flip_ref.scalars_ref, bf16[768,2048]{1,0:T(8,128)(2,1)S(1)} %copy-done.21, bf16[768,1024]{1,0:T(8,128)(2,1)S(1)} %bitcast.57, bf16[2048,1024]{1,0:T(8,128)(2,1)} %collective-permute-done.14.arrived_ref), custom_call_target="tpu_custom_call" | custom-call | flops 1 | bytes 1 | tf_op jit(solution)/shard_map/ff_out_grad_own/pallas_call | solution.py:65
  229.2 5.0 %ff_in_grad_other.1 = bf16[512,4096]{1,0:T(8,128)(2,1)S(1)} custom-call(s32[17]{0:T(128)S(1)} %concatenate.18.slots_ref._.flip_ref.scalars_ref, bf16[768,1024]{1,0:T(8,128)(2,1)S(1)} %copy-done.11, bf16[768,4096]{1,0:T(8,128)(2,1)S(1)} %get-tuple-element.426.grads_ref), custom_call_target="tpu_custom_call" | custom-call | flops 1 | bytes 1 | tf_op jit(solution)/shard_map/ff_in_grad_other/pallas_call | solution.py:65
  235.8 17.2 %norm3_grad.1 = (f32[768,1024]{1,0:T(8,128)}, bf16[768,1024]{1,0:T(8,128)(2,1)S(1)}, f32[8,1024]{1,0:T(8,128)S(1)}) custom-call(s32[17]{0:T(128)S(1)} %concatenate.18.slots_ref._.flip_ref.scalars_ref, bf16[768,4096]{1,0:T(8,128)(2,1)} %copy-done.2, bf16[4,1,128,4096]{3,2,1,0:T(8,128)(2,1)} %bitcast.26.own_ref, bf16[4,1,128,4096]{3,2,1,0:T(8,128)(2,1)} %bitcast.27.other_ref, ...), custom_call_target="tpu_custom_call" | custom-call | flops 1 | bytes 1 | tf_op jit(solution)/shard_map/norm3_grad/pallas_call | solution.py:65
  253.0 6.5 %ff_in_grad_own.1 = (bf16[8,32,4096]{2,1,0:T(8,128)(2,1)S(1)}, bf16[8,32,4096]{2,1,0:T(8,128)(2,1)}) custom-call(s32[17]{0:T(128)S(1)} %concatenate.18.slots_ref._.flip_ref.scalars_ref, bf16[768,1024]{1,0:T(8,128)(2,1)S(1)} %copy-done.11, bf16[768,4096]{1,0:T(8,128)(2,1)S(1)} %copy-done.3, bf16[512,4096]{1,0:T(8,128)(2,1)S(1)} %collective-permute-done.15.arrived_ref), custom_call_target="tpu_custom_call" | custom-call | flops 1 | bytes 1 | tf_op jit(solution)/shard_map/ff_in_grad_own/pallas_call | solution.py:65
  259.5 4.6 attended2_grad.1.grad_ref
  264.1 8.6 %cross_attention_grads.1 = (bf16[768,1024]{1,0:T(8,128)(2,1)S(1)}, bf16[256,2048]{1,0:T(8,128)(2,1)S(1)}) custom-call(s32[17]{0:T(128)S(1)} %concatenate.18.slots_ref._.flip_ref.scalars_ref, bf16[768,1024]{1,0:T(8,128)(2,1)S(1)} %copy-done.13, bf16[256,2048]{1,0:T(8,128)(2,1)S(1)} %project_text.1.key_ref.value_ref, ...), custom_call_target="tpu_custom_call" | custom-call | flops 1 | bytes 1 | tf_op jit(solution)/shard_map/cross_attention_grads/pallas_call | solution.py:65
  272.8 2.5 combine.15
  282.5 8.7 %norm2_grad.1 = (f32[768,1024]{1,0:T(8,128)}, bf16[768,1024]{1,0:T(8,128)(2,1)S(1)}, f32[8,1024]{1,0:T(8,128)S(1)}) custom-call(s32[17]{0:T(128)S(1)} %concatenate.18.slots_ref._.flip_ref.scalars_ref, bf16[768,1024]{1,0:T(8,128)(2,1)S(1)} %get-tuple-element.458.grads_ref, bf16[4,1,128,5120]{3,2,1,0:T(8,128)(2,1)} %bitcast.23.own_ref, ...), custom_call_target="tpu_custom_call" | custom-call | flops 1 | bytes 1 | tf_op jit(solution)/shard_map/norm2_grad/pallas_call | solution.py:65
  296.9 4.4 attended1_grad.1.grad_ref
  301.2 14.6 %self_attention_grads.1.grads_ref = bf16[768,3072]{1,0:T(8,128)(2,1)S(1)} custom-call(s32[17]{0:T(128)S(1)} %concatenate.18.slots_ref._.flip_ref.scalars_ref, bf16[768,3072]{1,0:T(8,128)(2,1)S(1)} %bitcast.53, bf16[768,3072]{1,0:T(8,128)(2,1)S(1)} %bitcast.53, bf16[768,3072]{1,0:T(8,128)(2,1)S(1)} %bitcast.53, ...), custom_call_target="tpu_custom_call" | custom-call | flops 1 | bytes 1 | tf_op jit(solution)/shard_map/self_attention_grads/pallas_call | solution.py:65
  319.3 4.2 qkv_grad_other.1.refs_0_
  327.1 6.6 %collective-permute-start.23 = (bf16[2,128,1024]{2,1,0:T(8,128)(2,1)S(1)}, bf16[2,128,1024]{2,1,0:T(8,128)(2,1)S(1)}, u32[]{:S(2)}, u32[]{:S(2)}) collective-permute-start(bf16[2,128,1024]{2,1,0:T(8,128)(2,1)S(1)} %get-tuple-element.526), channel_id=1, source_target_pairs={{0,8},{1,9},{2,10},{3,11},{4,12},{5,13},{6,14},{7,15},{8,0},{9,1},... | collective-permute-start | bytes 1572872 | tf_op jit(solution)/shard_map/ppermute | solution.py:144
  333.7 5.0 %text_grad.1 = bf16[256,1024]{1,0:T(8,128)(2,1)} custom-call(s32[17]{0:T(128)S(1)} %concatenate.18.slots_ref._.flip_ref.scalars_ref, bf16[256,2048]{1,0:T(8,128)(2,1)S(1)} %get-tuple-element.456.grads_ref, bf16[4,1,128,5120]{3,2,1,0:T(8,128)(2,1)} %bitcast.23.own_ref, bf16[4,1,128,5120]{3,2,1,0:T(8,128)(2,1)} %bitcast.24.other_ref), custom_call_target="tpu_custom_call" | custom-call | flops 1 | bytes 1 | tf_op jit(solution)/shard_map/text_grad/pallas_call | solution.py:65
  338.7 5.7 %qkv_grad_own.1 = (bf16[8,32,4096]{2,1,0:T(8,128)(2,1)S(1)}, bf16[8,32,4096]{2,1,0:T(8,128)(2,1)}) custom-call(s32[17]{0:T(128)S(1)} %concatenate.18.slots_ref._.flip_ref.scalars_ref, bf16[768,1024]{1,0:T(8,128)(2,1)S(1)} %copy-done.18, bf16[768,3072]{1,0:T(8,128)(2,1)S(1)} %self_attention_grads.1.grads_ref, ...), custom_call_target="tpu_custom_call" | custom-call | flops 1 | bytes 1 | tf_op jit(solution)/shard_map/qkv_grad_own/pallas_call | solution.py:65
  344.4 2.5 self_out_grad_own.1
  348.2 12.6 %last_layer.1 = bf16[768,1024]{1,0:T(8,128)(2,1)} custom-call(s32[17]{0:T(128)S(1)} %concatenate.18.slots_ref._.flip_ref.scalars_ref, bf16[768,2048]{1,0:T(8,128)(2,1)S(1)} %copy-done.21, bf16[768,2048]{1,0:T(8,128)(2,1)S(1)} %copy-done.23, bf16[4,2,512,1024]{3,2,1,0:T(8,128)(2,1)} %bitcast.81, bf16[4,2,512,1024]{3,2,1,0:T(8,128)(2,1)} %bitcast.82, ...), custom_call_target="tpu_custom_call" | custom-call | flops 1 | bytes 1 | tf_op jit(solution)/shard_map/last_layer/pallas_call | solution.py:65
  368.2 4.7 collective-permute-start.26
  375.0 13.2 %norm1_grad.1 = (bf16[768,1024]{1,0:T(8,128)(2,1)}, f32[8,1024]{1,0:T(8,128)S(1)}) custom-call(s32[17]{0:T(128)S(1)} %concatenate.18.slots_ref._.flip_ref.scalars_ref, bf16[768,3072]{1,0:T(8,128)(2,1)} %copy-done.1, bf16[4,2,128,3200]{3,2,1,0:T(8,128)(2,1)} %bitcast.77, bf16[4,2,128,3200]{3,2,1,0:T(8,128)(2,1)} %bitcast.78, bf16[768,1024]{1,0:T(8,128)(2,1)} %bitcast.59, ...), custom_call_target="tpu_custom_call" | custom-call | flops 1 | bytes 1 | tf_op jit(solution)/shard_map/norm1_grad/pallas_call | solution.py:65
  395.9 6.5 %collective-permute-done.28.arrived_ref = bf16[8,32,4096]{2,1,0:T(8,128)(2,1)S(1)} collective-permute-done((bf16[8,32,4096]{2,1,0:T(8,128)(2,1)}, bf16[8,32,4096]{2,1,0:T(8,128)(2,1)S(1)}, u32[]{:S(2)}, u32[]{:S(2)}) %collective-permute-start.28) | collective-permute-done | bytes 2097184 | tf_op jit(solution)/shard_map/ppermute | solution.py:144
  405.4 5.4 %collective-permute-start.33 = (bf16[2,32,4096]{2,1,0:T(8,128)(2,1)S(1)}, bf16[2,32,4096]{2,1,0:T(8,128)(2,1)S(1)}, u32[]{:S(2)}, u32[]{:S(2)}) collective-permute-start(bf16[2,32,4096]{2,1,0:T(8,128)(2,1)S(1)} %get-tuple-element.606), channel_id=1, source_target_pairs={{0,8},{1,9},{2,10},{3,11},{4,12},{5,13},{6,14},{7,15},{8,0},{9,1},... | collective-permute-start | bytes 1572872 | tf_op jit(solution)/shard_map/ppermute | solution.py:144
  413.3 6.1 %collective-permute-done.30.arrived_ref = bf16[4,32,4096]{2,1,0:T(8,128)(2,1)S(1)} collective-permute-done((bf16[4,32,4096]{2,1,0:T(8,128)(2,1)S(1)}, bf16[4,32,4096]{2,1,0:T(8,128)(2,1)S(1)}, u32[]{:S(2)}, u32[]{:S(2)}) %collective-permute-start.30) | collective-permute-done | bytes 1048608 | tf_op jit(solution)/shard_map/ppermute | solution.py:144
  422.6 4.4 collective-permute-done.33.arrived_ref
  433.1 10.3 %collective-permute-done.38 = bf16[1,32,4096]{2,1,0:T(8,128)(2,1)S(1)} collective-permute-done((bf16[1,32,4096]{2,1,0:T(8,128)(2,1)S(1)}, bf16[1,32,4096]{2,1,0:T(8,128)(2,1)S(1)}, u32[]{:S(2)}, u32[]{:S(2)}) %collective-permute-start.38) | collective-permute-done | bytes 262176 | tf_op jit(solution)/shard_map/ppermute | solution.py:144
  446.4 2.5 collective-permute-start.36
  452.6 8.7 %collective-permute-done.37 = bf16[1,32,4096]{2,1,0:T(8,128)(2,1)S(1)} collective-permute-done((bf16[1,32,4096]{2,1,0:T(8,128)(2,1)S(1)}, bf16[1,32,4096]{2,1,0:T(8,128)(2,1)S(1)}, u32[]{:S(2)}, u32[]{:S(2)}) %collective-permute-start.37) | collective-permute-done | bytes 262176 | tf_op jit(solution)/shard_map/ppermute | solution.py:144
  (194 shorter events, 88.4 us)
Async XLA Ops:
  7.2 114.1 %all-gather.3.cloned.1.call-start = ((), (), s32[]{:S(2)}) async-start(), calls=%async_computation | async-start | bytes 6758400 | tf_op jit(solution)/shard_map/all_gather | solution.py:921
  9.6 38.7 %copy-start.26 = (bf16[2,128,1024]{2,1,0:T(8,128)(2,1)S(1)}, bf16[2,128,1024]{2,1,0:T(8,128)(2,1)}, u32[]{:S(2)}) copy-start(bf16[2,128,1024]{2,1,0:T(8,128)(2,1)} %param.23) | copy-start | bytes 1572868
  11.3 196.1 %all-gather.5.cloned.1.call-start = ((), (), s32[]{:S(2)}) async-start(), calls=%async_computation.1 | async-start | bytes 8650752 | tf_op jit(solution)/shard_map/all_gather | solution.py:926
  13.8 59.3 %copy-start.29 = (bf16[32,4096]{1,0:T(8,128)(2,1)S(1)}, bf16[32,4096]{1,0:T(8,128)(2,1)}, u32[]{:S(2)}) copy-start(bf16[32,4096]{1,0:T(8,128)(2,1)} %param.37) | copy-start | bytes 786436
  13.8 13.8 %collective-permute-start = (bf16[32,5120]{1,0:T(8,128)(2,1)S(1)}, bf16[32,5120]{1,0:T(8,128)(2,1)S(1)}, u32[]{:S(2)}, u32[]{:S(2)}) collective-permute-start(bf16[32,5120]{1,0:T(8,128)(2,1)S(1)} %pad_maximum_fusion), channel_id=1, source_target_pairs={{0,8},{1,9},{2,10},{3,11},{4,12},{5,13},{6,14},{7,15},{8,16},{9,17... | collective-permute-start | bytes 983048 | tf_op jit(solution)/shard_map/ppermute | solution.py:144
  16.9 28.1 %collective-permute-start.1 = (bf16[32,5120]{1,0:T(8,128)(2,1)S(1)}, bf16[32,5120]{1,0:T(8,128)(2,1)S(1)}, u32[]{:S(2)}, u32[]{:S(2)}) collective-permute-start(bf16[32,5120]{1,0:T(8,128)(2,1)S(1)} %pad_maximum_fusion), channel_id=1, source_target_pairs={{0,16},{1,17},{2,18},{3,19},{4,20},{5,21},{6,22},{7,23},{8,24},{9,... | collective-permute-start | bytes 983048 | tf_op jit(solution)/shard_map/ppermute | solution.py:144
  19.5 25.5 %collective-permute-start.2 = (bf16[32,5120]{1,0:T(8,128)(2,1)S(1)}, bf16[32,5120]{1,0:T(8,128)(2,1)S(1)}, u32[]{:S(2)}, u32[]{:S(2)}) collective-permute-start(bf16[32,5120]{1,0:T(8,128)(2,1)S(1)} %pad_maximum_fusion), channel_id=1, source_target_pairs={{0,24},{1,25},{2,26},{3,27},{4,28},{5,29},{6,30},{7,31},{8,0},{9,1... | collective-permute-start | bytes 983048 | tf_op jit(solution)/shard_map/ppermute | solution.py:144
  46.7 24.3 %collective-permute-start.6 = (bf16[4,32,5120]{2,1,0:T(8,128)(2,1)}, bf16[4,32,5120]{2,1,0:T(8,128)(2,1)}, u32[]{:S(2)}, u32[]{:S(2)}) collective-permute-start(bf16[4,32,5120]{2,1,0:T(8,128)(2,1)} %bitcast.5.refs_0_), channel_id=1, source_target_pairs={{0,1},{1,0},{2,3},{3,2},{4,6},{5,7},{6,4},{7,5},{8,9},{9,8},{10,11... | collective-permute-start | bytes 3932168 | tf_op jit(solution)/shard_map/ppermute | solution.py:144
  71.1 40.0 %collective-permute-start.8 = (bf16[4,32,5120]{2,1,0:T(8,128)(2,1)}, bf16[4,32,5120]{2,1,0:T(8,128)(2,1)S(1)}, u32[]{:S(2)}, u32[]{:S(2)}) collective-permute-start(bf16[4,32,5120]{2,1,0:T(8,128)(2,1)} %bitcast.5.refs_0_), channel_id=1, source_target_pairs={{0,2},{1,3},{2,0},{3,1},{4,5},{5,4},{6,7},{7,6},{8,10},{9,11},{10,... | collective-permute-start | bytes 3932168 | tf_op jit(solution)/shard_map/ppermute | solution.py:144
  72.7 41.8 %collective-permute-start.9 = (bf16[4,32,5120]{2,1,0:T(8,128)(2,1)}, bf16[4,32,5120]{2,1,0:T(8,128)(2,1)S(1)}, u32[]{:S(2)}, u32[]{:S(2)}) collective-permute-start(bf16[4,32,5120]{2,1,0:T(8,128)(2,1)} %collective-permute-done.6.refs_1_), channel_id=1, source_target_pairs={{0,2},{1,3},{2,0},{3,1},{4,5},{5,4},{6,7},{7,6},{8,10},{9,11},{10,... | collective-permute-start | bytes 3932168 | tf_op jit(solution)/shard_map/ppermute | solution.py:144
  73.1 20.6 %collective-permute-start.3 = (bf16[32,4096]{1,0:T(8,128)(2,1)S(1)}, bf16[32,4096]{1,0:T(8,128)(2,1)S(1)}, u32[]{:S(2)}, u32[]{:S(2)}) collective-permute-start(bf16[32,4096]{1,0:T(8,128)(2,1)S(1)} %copy-done.29), channel_id=1, source_target_pairs={{0,8},{1,9},{2,10},{3,11},{4,12},{5,13},{6,14},{7,15},{8,16},{9,17... | collective-permute-start | bytes 786440 | tf_op jit(solution)/shard_map/ppermute | solution.py:144
  78.5 31.0 %collective-permute-start.4 = (bf16[32,4096]{1,0:T(8,128)(2,1)S(1)}, bf16[32,4096]{1,0:T(8,128)(2,1)S(1)}, u32[]{:S(2)}, u32[]{:S(2)}) collective-permute-start(bf16[32,4096]{1,0:T(8,128)(2,1)S(1)} %copy-done.29), channel_id=1, source_target_pairs={{0,16},{1,17},{2,18},{3,19},{4,20},{5,21},{6,22},{7,23},{8,24},{9,... | collective-permute-start | bytes 786440 | tf_op jit(solution)/shard_map/ppermute | solution.py:144
  81.5 28.0 %collective-permute-start.5 = (bf16[32,4096]{1,0:T(8,128)(2,1)S(1)}, bf16[32,4096]{1,0:T(8,128)(2,1)S(1)}, u32[]{:S(2)}, u32[]{:S(2)}) collective-permute-start(bf16[32,4096]{1,0:T(8,128)(2,1)S(1)} %copy-done.29), channel_id=1, source_target_pairs={{0,24},{1,25},{2,26},{3,27},{4,28},{5,29},{6,30},{7,31},{8,0},{9,1... | collective-permute-start | bytes 786440 | tf_op jit(solution)/shard_map/ppermute | solution.py:144
  119.6 12.8 %collective-permute-start.10 = (bf16[4,128,5120]{2,1,0:T(8,128)(2,1)}, bf16[4,128,5120]{2,1,0:T(8,128)(2,1)}, u32[]{:S(2)}, u32[]{:S(2)}) collective-permute-start(bf16[4,128,5120]{2,1,0:T(8,128)(2,1)} %bitcast.12), channel_id=1, source_target_pairs={{0,4},{1,5},{2,6},{3,7},{4,0},{5,1},{6,2},{7,3},{8,12},{9,13},{10,... | collective-permute-start | bytes 15728648 | tf_op jit(solution)/shard_map/ppermute | solution.py:144
  119.6 17.5 %collective-permute-start.7 = (bf16[4,32,4096]{2,1,0:T(8,128)(2,1)}, bf16[4,32,4096]{2,1,0:T(8,128)(2,1)}, u32[]{:S(2)}, u32[]{:S(2)}) collective-permute-start(bf16[4,32,4096]{2,1,0:T(8,128)(2,1)} %bitcast.11.refs_0_), channel_id=1, source_target_pairs={{0,1},{1,0},{2,3},{3,2},{4,6},{5,7},{6,4},{7,5},{8,9},{9,8},{10,11... | collective-permute-start | bytes 3145736 | tf_op jit(solution)/shard_map/ppermute | solution.py:144
  137.1 34.0 %collective-permute-start.11 = (bf16[4,32,4096]{2,1,0:T(8,128)(2,1)}, bf16[4,32,4096]{2,1,0:T(8,128)(2,1)S(1)}, u32[]{:S(2)}, u32[]{:S(2)}) collective-permute-start(bf16[4,32,4096]{2,1,0:T(8,128)(2,1)} %bitcast.11.refs_0_), channel_id=1, source_target_pairs={{0,2},{1,3},{2,0},{3,1},{4,5},{5,4},{6,7},{7,6},{8,10},{9,11},{10,... | collective-permute-start | bytes 3145736 | tf_op jit(solution)/shard_map/ppermute | solution.py:144
  138.7 32.4 %collective-permute-start.12 = (bf16[4,32,4096]{2,1,0:T(8,128)(2,1)}, bf16[4,32,4096]{2,1,0:T(8,128)(2,1)S(1)}, u32[]{:S(2)}, u32[]{:S(2)}) collective-permute-start(bf16[4,32,4096]{2,1,0:T(8,128)(2,1)} %collective-permute-done.7.refs_1_), channel_id=1, source_target_pairs={{0,2},{1,3},{2,0},{3,1},{4,5},{5,4},{6,7},{7,6},{8,10},{9,11},{10,... | collective-permute-start | bytes 3145736 | tf_op jit(solution)/shard_map/ppermute | solution.py:144
  175.9 8.4 %collective-permute-start.13 = (bf16[4,128,4096]{2,1,0:T(8,128)(2,1)}, bf16[4,128,4096]{2,1,0:T(8,128)(2,1)}, u32[]{:S(2)}, u32[]{:S(2)}) collective-permute-start(bf16[4,128,4096]{2,1,0:T(8,128)(2,1)} %bitcast.25), channel_id=1, source_target_pairs={{0,4},{1,5},{2,6},{3,7},{4,0},{5,1},{6,2},{7,3},{8,12},{9,13},{10,... | collective-permute-start | bytes 12582920 | tf_op jit(solution)/shard_map/ppermute | solution.py:144
  184.3 16.7 %copy-start.10 = (bf16[768,1024]{1,0:T(8,128)(2,1)}, bf16[768,1024]{1,0:T(8,128)(2,1)S(1)}, u32[]{:S(2)}) copy-start(bf16[768,1024]{1,0:T(8,128)(2,1)S(1)} %get-tuple-element.404.inputs_ref) | copy-start | bytes 4718596
  184.3 16.7 %copy-start.4 = (bf16[2,384,1024]{2,1,0:T(8,128)(2,1)S(1)}, bf16[2,384,1024]{2,1,0:T(8,128)(2,1)}, u32[]{:S(2)}) copy-start(bf16[2,384,1024]{2,1,0:T(8,128)(2,1)} %param.25) | copy-start | bytes 4718596
  206.9 13.5 %collective-permute-start.14 = (bf16[2048,1024]{1,0:T(8,128)(2,1)}, bf16[2048,1024]{1,0:T(8,128)(2,1)}, u32[]{:S(2)}, u32[]{:S(2)}) collective-permute-start(bf16[2048,1024]{1,0:T(8,128)(2,1)} %ff_out_grad_other.1), channel_id=1, source_target_pairs={{0,4},{1,5},{2,6},{3,7},{4,0},{5,1},{6,2},{7,3},{8,12},{9,13},{10,... | collective-permute-start | bytes 12582920 | tf_op jit(solution)/shard_map/ppermute | solution.py:144
  234.2 18.8 %collective-permute-start.15 = (bf16[512,4096]{1,0:T(8,128)(2,1)S(1)}, bf16[512,4096]{1,0:T(8,128)(2,1)S(1)}, u32[]{:S(2)}, u32[]{:S(2)}) collective-permute-start(bf16[512,4096]{1,0:T(8,128)(2,1)S(1)} %ff_in_grad_other.1), channel_id=1, source_target_pairs={{0,4},{1,5},{2,6},{3,7},{4,0},{5,1},{6,2},{7,3},{8,12},{9,13},{10,... | collective-permute-start | bytes 12582920 | tf_op jit(solution)/shard_map/ppermute | solution.py:144
  234.3 38.5 %collective-permute-start.16 = (bf16[8,128,1024]{2,1,0:T(8,128)(2,1)S(1)}, bf16[8,128,1024]{2,1,0:T(8,128)(2,1)}, u32[]{:S(2)}, u32[]{:S(2)}) collective-permute-start(bf16[8,128,1024]{2,1,0:T(8,128)(2,1)S(1)} %get-tuple-element.441), channel_id=1, source_target_pairs={{0,2},{1,3},{2,0},{3,1},{4,5},{5,4},{6,7},{7,6},{8,10},{9,11},{10,... | collective-permute-start | bytes 6291464 | tf_op jit(solution)/shard_map/ppermute | solution.py:144
  235.8 17.2 %copy-start.3 = (bf16[768,4096]{1,0:T(8,128)(2,1)S(1)}, bf16[768,4096]{1,0:T(8,128)(2,1)}, u32[]{:S(2)}) copy-start(bf16[768,4096]{1,0:T(8,128)(2,1)} %copy-done.2) | copy-start | bytes 18874372
  280.2 11.0 %collective-permute-start.19 = (bf16[512,4096]{1,0:T(8,128)(2,1)S(1)}, bf16[512,4096]{1,0:T(8,128)(2,1)S(1)}, u32[]{:S(2)}, u32[]{:S(2)}) collective-permute-start(bf16[512,4096]{1,0:T(8,128)(2,1)S(1)} %cross_out_grad_other.1), channel_id=1, source_target_pairs={{0,4},{1,5},{2,6},{3,7},{4,0},{5,1},{6,2},{7,3},{8,12},{9,13},{10,... | collective-permute-start | bytes 12582920 | tf_op jit(solution)/shard_map/ppermute | solution.py:144
  280.3 37.5 %collective-permute-start.17 = (bf16[8,32,4096]{2,1,0:T(8,128)(2,1)}, bf16[8,32,4096]{2,1,0:T(8,128)(2,1)S(1)}, u32[]{:S(2)}, u32[]{:S(2)}) collective-permute-start(bf16[8,32,4096]{2,1,0:T(8,128)(2,1)} %get-tuple-element.463), channel_id=1, source_target_pairs={{0,2},{1,3},{2,0},{3,1},{4,5},{5,4},{6,7},{7,6},{8,10},{9,11},{10,... | collective-permute-start | bytes 6291464 | tf_op jit(solution)/shard_map/ppermute | solution.py:144
  281.5 34.4 %collective-permute-start.18 = (bf16[4,128,1024]{2,1,0:T(8,128)(2,1)S(1)}, bf16[4,128,1024]{2,1,0:T(8,128)(2,1)S(1)}, u32[]{:S(2)}, u32[]{:S(2)}) collective-permute-start(bf16[4,128,1024]{2,1,0:T(8,128)(2,1)S(1)} %get-tuple-element.464), channel_id=1, source_target_pairs={{0,1},{1,0},{2,3},{3,2},{4,6},{5,7},{6,4},{7,5},{8,9},{9,8},{10,11... | collective-permute-start | bytes 3145736 | tf_op jit(solution)/shard_map/ppermute | solution.py:144
  315.9 22.8 %copy-start.1 = (bf16[768,3072]{1,0:T(8,128)(2,1)}, bf16[768,3072]{1,0:T(8,128)(2,1)S(1)}, u32[]{:S(2)}) copy-start(bf16[768,3072]{1,0:T(8,128)(2,1)S(1)} %self_attention_grads.1.grads_ref) | copy-start | bytes 14155780
  325.1 13.5 %collective-permute-start.20 = (bf16[512,4096]{1,0:T(8,128)(2,1)S(1)}, bf16[512,4096]{1,0:T(8,128)(2,1)S(1)}, u32[]{:S(2)}, u32[]{:S(2)}) collective-permute-start(bf16[512,4096]{1,0:T(8,128)(2,1)S(1)} %self_out_grad_other.1), channel_id=1, source_target_pairs={{0,4},{1,5},{2,6},{3,7},{4,0},{5,1},{6,2},{7,3},{8,12},{9,13},{10,... | collective-permute-start | bytes 12582920 | tf_op jit(solution)/shard_map/ppermute | solution.py:144
  325.2 38.6 %collective-permute-start.21 = (bf16[8,32,4096]{2,1,0:T(8,128)(2,1)S(1)}, bf16[8,32,4096]{2,1,0:T(8,128)(2,1)S(1)}, u32[]{:S(2)}, u32[]{:S(2)}) collective-permute-start(bf16[8,32,4096]{2,1,0:T(8,128)(2,1)S(1)} %get-tuple-element.524), channel_id=1, source_target_pairs={{0,2},{1,3},{2,0},{3,1},{4,5},{5,4},{6,7},{7,6},{8,10},{9,11},{10,... | collective-permute-start | bytes 6291464 | tf_op jit(solution)/shard_map/ppermute | solution.py:144
  326.0 36.0 %collective-permute-start.22 = (bf16[4,32,4096]{2,1,0:T(8,128)(2,1)S(1)}, bf16[4,32,4096]{2,1,0:T(8,128)(2,1)S(1)}, u32[]{:S(2)}, u32[]{:S(2)}) collective-permute-start(bf16[4,32,4096]{2,1,0:T(8,128)(2,1)S(1)} %get-tuple-element.525), channel_id=1, source_target_pairs={{0,1},{1,0},{2,3},{3,2},{4,6},{5,7},{6,4},{7,5},{8,9},{9,8},{10,11... | collective-permute-start | bytes 3145736 | tf_op jit(solution)/shard_map/ppermute | solution.py:144
  327.1 33.6 %collective-permute-start.23 = (bf16[2,128,1024]{2,1,0:T(8,128)(2,1)S(1)}, bf16[2,128,1024]{2,1,0:T(8,128)(2,1)S(1)}, u32[]{:S(2)}, u32[]{:S(2)}) collective-permute-start(bf16[2,128,1024]{2,1,0:T(8,128)(2,1)S(1)} %get-tuple-element.526), channel_id=1, source_target_pairs={{0,8},{1,9},{2,10},{3,11},{4,12},{5,13},{6,14},{7,15},{8,0},{9,1},... | collective-permute-start | bytes 1572872 | tf_op jit(solution)/shard_map/ppermute | solution.py:144
  366.0 36.3 %collective-permute-start.28 = (bf16[8,32,4096]{2,1,0:T(8,128)(2,1)}, bf16[8,32,4096]{2,1,0:T(8,128)(2,1)S(1)}, u32[]{:S(2)}, u32[]{:S(2)}) collective-permute-start(bf16[8,32,4096]{2,1,0:T(8,128)(2,1)} %get-tuple-element.577), channel_id=1, source_target_pairs={{0,2},{1,3},{2,0},{3,1},{4,5},{5,4},{6,7},{7,6},{8,10},{9,11},{10,... | collective-permute-start | bytes 6291464 | tf_op jit(solution)/shard_map/ppermute | solution.py:144
  366.8 27.1 %collective-permute-start.29 = (bf16[4,32,4096]{2,1,0:T(8,128)(2,1)}, bf16[4,32,4096]{2,1,0:T(8,128)(2,1)}, u32[]{:S(2)}, u32[]{:S(2)}) collective-permute-start(bf16[4,32,4096]{2,1,0:T(8,128)(2,1)} %get-tuple-element.578), channel_id=1, source_target_pairs={{0,1},{1,0},{2,3},{3,2},{4,6},{5,7},{6,4},{7,5},{8,9},{9,8},{10,11... | collective-permute-start | bytes 3145736 | tf_op jit(solution)/shard_map/ppermute | solution.py:144
  368.2 22.1 %collective-permute-start.26 = (bf16[2,32,4096]{2,1,0:T(8,128)(2,1)}, bf16[2,32,4096]{2,1,0:T(8,128)(2,1)}, u32[]{:S(2)}, u32[]{:S(2)}) collective-permute-start(bf16[2,32,4096]{2,1,0:T(8,128)(2,1)} %get-tuple-element.561), channel_id=1, source_target_pairs={{0,8},{1,9},{2,10},{3,11},{4,12},{5,13},{6,14},{7,15},{8,0},{9,1},... | collective-permute-start | bytes 1572872 | tf_op jit(solution)/shard_map/ppermute | solution.py:144
  372.9 20.2 %collective-permute-start.25 = (bf16[1,128,1024]{2,1,0:T(8,128)(2,1)}, bf16[1,128,1024]{2,1,0:T(8,128)(2,1)}, u32[]{:S(2)}, u32[]{:S(2)}) collective-permute-start(bf16[1,128,1024]{2,1,0:T(8,128)(2,1)} %get-tuple-element.560), channel_id=1, source_target_pairs={{0,16},{1,17},{2,18},{3,19},{4,20},{5,21},{6,22},{7,23},{8,24},{9,... | collective-permute-start | bytes 786440 | tf_op jit(solution)/shard_map/ppermute | solution.py:144
  389.5 12.8 %copy-start.25 = (bf16[8,32,4096]{2,1,0:T(8,128)(2,1)S(1)}, bf16[8,32,4096]{2,1,0:T(8,128)(2,1)}, u32[]{:S(2)}) copy-start(bf16[8,32,4096]{2,1,0:T(8,128)(2,1)} %copy-done.24) | copy-start | bytes 6291460
  390.2 2.9 collective-permute-start.24
  403.8 15.6 %collective-permute-start.30 = (bf16[4,32,4096]{2,1,0:T(8,128)(2,1)S(1)}, bf16[4,32,4096]{2,1,0:T(8,128)(2,1)S(1)}, u32[]{:S(2)}, u32[]{:S(2)}) collective-permute-start(bf16[4,32,4096]{2,1,0:T(8,128)(2,1)S(1)} %get-tuple-element.591), channel_id=1, source_target_pairs={{0,1},{1,0},{2,3},{3,2},{4,6},{5,7},{6,4},{7,5},{8,9},{9,8},{10,11... | collective-permute-start | bytes 3145736 | tf_op jit(solution)/shard_map/ppermute | solution.py:144
  405.4 21.6 %collective-permute-start.33 = (bf16[2,32,4096]{2,1,0:T(8,128)(2,1)S(1)}, bf16[2,32,4096]{2,1,0:T(8,128)(2,1)S(1)}, u32[]{:S(2)}, u32[]{:S(2)}) collective-permute-start(bf16[2,32,4096]{2,1,0:T(8,128)(2,1)S(1)} %get-tuple-element.606), channel_id=1, source_target_pairs={{0,8},{1,9},{2,10},{3,11},{4,12},{5,13},{6,14},{7,15},{8,0},{9,1},... | collective-permute-start | bytes 1572872 | tf_op jit(solution)/shard_map/ppermute | solution.py:144
  410.8 16.8 %collective-permute-start.32 = (bf16[1,32,4096]{2,1,0:T(8,128)(2,1)S(1)}, bf16[1,32,4096]{2,1,0:T(8,128)(2,1)S(1)}, u32[]{:S(2)}, u32[]{:S(2)}) collective-permute-start(bf16[1,32,4096]{2,1,0:T(8,128)(2,1)S(1)} %get-tuple-element.605), channel_id=1, source_target_pairs={{0,16},{1,17},{2,18},{3,19},{4,20},{5,21},{6,22},{7,23},{8,24},{9,... | collective-permute-start | bytes 786440 | tf_op jit(solution)/shard_map/ppermute | solution.py:144
  411.0 9.4 %collective-permute-start.27 = (bf16[8,32,128]{2,1,0:T(8,128)(2,1)S(1)}, bf16[8,32,128]{2,1,0:T(8,128)(2,1)S(1)}, u32[]{:S(2)}, u32[]{:S(2)}) collective-permute-start(bf16[8,32,128]{2,1,0:T(8,128)(2,1)S(1)} %get-tuple-element.576), channel_id=1, source_target_pairs={{0,2},{1,3},{2,0},{3,1},{4,5},{5,4},{6,7},{7,6},{8,10},{9,11},{10,... | collective-permute-start | bytes 196616 | tf_op jit(solution)/shard_map/ppermute | solution.py:144
  421.0 9.6 %collective-permute-start.31 = (bf16[4,32,128]{2,1,0:T(8,128)(2,1)S(1)}, bf16[4,32,128]{2,1,0:T(8,128)(2,1)S(1)}, u32[]{:S(2)}, u32[]{:S(2)}) collective-permute-start(bf16[4,32,128]{2,1,0:T(8,128)(2,1)S(1)} %get-tuple-element.604), channel_id=1, source_target_pairs={{0,1},{1,0},{2,3},{3,2},{4,6},{5,7},{6,4},{7,5},{8,9},{9,8},{10,11... | collective-permute-start | bytes 98312 | tf_op jit(solution)/shard_map/ppermute | solution.py:144
  427.6 17.5 %collective-permute-start.35 = (bf16[2,32,4096]{2,1,0:T(8,128)(2,1)S(1)}, bf16[2,32,4096]{2,1,0:T(8,128)(2,1)S(1)}, u32[]{:S(2)}, u32[]{:S(2)}) collective-permute-start(bf16[2,32,4096]{2,1,0:T(8,128)(2,1)S(1)} %get-tuple-element.621), channel_id=1, source_target_pairs={{0,8},{1,9},{2,10},{3,11},{4,12},{5,13},{6,14},{7,15},{8,0},{9,1},... | collective-permute-start | bytes 1572872 | tf_op jit(solution)/shard_map/ppermute | solution.py:144
  428.0 15.4 %collective-permute-start.38 = (bf16[1,32,4096]{2,1,0:T(8,128)(2,1)S(1)}, bf16[1,32,4096]{2,1,0:T(8,128)(2,1)S(1)}, u32[]{:S(2)}, u32[]{:S(2)}) collective-permute-start(bf16[1,32,4096]{2,1,0:T(8,128)(2,1)S(1)} %get-tuple-element.639), channel_id=1, source_target_pairs={{0,16},{1,17},{2,18},{3,19},{4,20},{5,21},{6,22},{7,23},{8,24},{9,... | collective-permute-start | bytes 786440 | tf_op jit(solution)/shard_map/ppermute | solution.py:144
  431.2 14.6 %collective-permute-start.34 = (bf16[2,32,128]{2,1,0:T(8,128)(2,1)S(1)}, bf16[2,32,128]{2,1,0:T(8,128)(2,1)S(1)}, u32[]{:S(2)}, u32[]{:S(2)}) collective-permute-start(bf16[2,32,128]{2,1,0:T(8,128)(2,1)S(1)} %get-tuple-element.620), channel_id=1, source_target_pairs={{0,8},{1,9},{2,10},{3,11},{4,12},{5,13},{6,14},{7,15},{8,0},{9,1},... | collective-permute-start | bytes 49160 | tf_op jit(solution)/shard_map/ppermute | solution.py:144
  446.4 4.7 collective-permute-start.36
  449.6 11.8 %collective-permute-start.37 = (bf16[1,32,4096]{2,1,0:T(8,128)(2,1)S(1)}, bf16[1,32,4096]{2,1,0:T(8,128)(2,1)S(1)}, u32[]{:S(2)}, u32[]{:S(2)}) collective-permute-start(bf16[1,32,4096]{2,1,0:T(8,128)(2,1)S(1)} %get-tuple-element.637), channel_id=1, source_target_pairs={{0,16},{1,17},{2,18},{3,19},{4,20},{5,21},{6,22},{7,23},{8,24},{9,... | collective-permute-start | bytes 786440 | tf_op jit(solution)/shard_map/ppermute | solution.py:144
  (25 other events, 134.1 us)
Sparse Core Ops, SparseCore 0:
  11.5 104.3 all-gather.2
  118.8 81.5 all-gather.4

commit v2 on v1

--- a/solution.py
+++ b/solution.py
@@ -531,7 +531,7 @@
         + [column],
         [column, pl.BlockSpec((1, 2 * size), lambda n, s: (0, n))],
         [jax.ShapeDtypeStruct((count, hidden), BF16), jax.ShapeDtypeStruct((1, hidden), F32)],
-        (grads, *weight.arrays, pinned(slope)),
+        (pinned(grads), *weight.arrays, pinned(slope)),
         name="hidden_grad",
     )
 

time: 480 us -> 479 us (level)
  the two profiles are of different devices: /device:TPU:0 before, /device:TPU:5 now
where the time goes in v2:
time: 479 us; the launch traced here: 470 us
  Pallas kernels  258 us (54%)
  waiting for transfers between devices  120 us (25%)
  starting transfers between devices  56.1 us (12%)
  between operations  15.3 us (3%)
  local copies, waits for them, and re-layouts  11.8 us (2%)
  other arithmetic  9.05 us (2%)
    pallas_call x56, Pallas kernels, call(): pl.pallas_call(body, grid_spec=spec, out_shape=out_shape, name=name, inpu...  258 us
    ppermute x39, waiting for transfers between devices, _permute(): return lax.ppermute(value, AXES, pairs)  120 us
    ppermute x39, starting transfers between devices, _permute(): return lax.ppermute(value, AXES, pairs)  56 us
  transfers between devices with their start and end apart: 41, of which 16 were waited for; matrix products, arithmetic and copies ran while one was open for 2% of the time, Pallas kernels for 48%

profile of v2, /device:TPU:5, one launch (start us, length us, event | category | flops | bytes accessed | tf_op | source)
XLA Modules:
  0.0 470.1 jit_solution(1217907858822769103)
XLA Ops:
  15.2 2.3 collective-permute-start.1
  18.6 5.9 %collective-permute-done = bf16[32,5120]{1,0:T(8,128)(2,1)S(1)} collective-permute-done((bf16[32,5120]{1,0:T(8,128)(2,1)S(1)}, bf16[32,5120]{1,0:T(8,128)(2,1)S(1)}, u32[]{:S(2)}, u32[]{:S(2)}) %collective-permute-start) | collective-permute-done | bytes 327712 | tf_op jit(solution)/shard_map/ppermute | solution.py:144
  24.5 19.2 %collective-permute-done.1 = bf16[32,5120]{1,0:T(8,128)(2,1)S(1)} collective-permute-done((bf16[32,5120]{1,0:T(8,128)(2,1)S(1)}, bf16[32,5120]{1,0:T(8,128)(2,1)S(1)}, u32[]{:S(2)}, u32[]{:S(2)}) %collective-permute-start.1) | collective-permute-done | bytes 327712 | tf_op jit(solution)/shard_map/ppermute | solution.py:144
  47.0 18.4 %collective-permute-done.6.refs_1_ = bf16[4,32,5120]{2,1,0:T(8,128)(2,1)} collective-permute-done((bf16[4,32,5120]{2,1,0:T(8,128)(2,1)}, bf16[4,32,5120]{2,1,0:T(8,128)(2,1)}, u32[]{:S(2)}, u32[]{:S(2)}) %collective-permute-start.6) | collective-permute-done | bytes 1310752 | tf_op jit(solution)/shard_map/ppermute | solution.py:144
  66.9 5.6 %collective-permute-start.3 = (bf16[32,4096]{1,0:T(8,128)(2,1)S(1)}, bf16[32,4096]{1,0:T(8,128)(2,1)S(1)}, u32[]{:S(2)}, u32[]{:S(2)}) collective-permute-start(bf16[32,4096]{1,0:T(8,128)(2,1)S(1)} %copy-done.28), channel_id=1, source_target_pairs={{0,8},{1,9},{2,10},{3,11},{4,12},{5,13},{6,14},{7,15},{8,16},{9,17... | collective-permute-start | bytes 786440 | tf_op jit(solution)/shard_map/ppermute | solution.py:144
  75.6 5.8 %collective-permute-done.3 = bf16[32,4096]{1,0:T(8,128)(2,1)S(1)} collective-permute-done((bf16[32,4096]{1,0:T(8,128)(2,1)S(1)}, bf16[32,4096]{1,0:T(8,128)(2,1)S(1)}, u32[]{:S(2)}, u32[]{:S(2)}) %collective-permute-start.3) | collective-permute-done | bytes 262176 | tf_op jit(solution)/shard_map/ppermute | solution.py:144
  81.4 23.5 %collective-permute-done.4 = bf16[32,4096]{1,0:T(8,128)(2,1)S(1)} collective-permute-done((bf16[32,4096]{1,0:T(8,128)(2,1)S(1)}, bf16[32,4096]{1,0:T(8,128)(2,1)S(1)}, u32[]{:S(2)}, u32[]{:S(2)}) %collective-permute-start.4) | collective-permute-done | bytes 262176 | tf_op jit(solution)/shard_map/ppermute | solution.py:144
  106.6 2.6 collective-permute-done.9.refs_3_
  109.1 5.2 %interleave.6 = bf16[4,4,32,5120]{3,2,1,0:T(8,128)(2,1)} custom-call(s32[17]{0:T(128)S(1)} %concatenate.18.slots_ref._.flip_ref.scalars_ref, bf16[4,32,5120]{2,1,0:T(8,128)(2,1)} %bitcast.5.refs_0_, bf16[4,32,5120]{2,1,0:T(8,128)(2,1)} %collective-permute-done.6.refs_1_, bf16[4,32,5120]{2,1,0:T(8,128)(2,1)S(1)} %collective-permute-done.8.refs_2_, ...), custom_call_target="tpu_custom_call" | custom-call | flops 1 | bytes 1 | tf_op jit(solution)/shard_map/interleave/pallas_call | solution.py:65
  114.3 4.7 collective-permute-start.10
  119.1 3.1 norm.1
  122.3 7.9 %project_qkv.1.query_ref.key_ref.value_ref = bf16[768,3072]{1,0:T(8,128)(2,1)S(1)} custom-call(s32[17]{0:T(128)S(1)} %concatenate.18.slots_ref._.flip_ref.scalars_ref, bf16[768,1024]{1,0:T(8,128)(2,1)S(1)} %get-tuple-element.366.inputs_ref, bf16[4,2,128,3200]{3,2,1,0:T(8,128)(2,1)} %bitcast.75, bf16[4,2,128,3200]{3,2,1,0:T(8,128)(2,1)} %bitcast.76), custom_call_target="tpu_custom_call" | custom-call | flops 1 | bytes 1 | tf_op jit(solution)/shard_map/project_qkv/pallas_call | solution.py:65
  130.2 4.7 project_text.1.key_ref.value_ref
  136.6 13.8 %self_attention.1 = (bf16[768,1024]{1,0:T(8,128)(2,1)S(1)}, bf16[2,16,384,384]{3,2,1,0:T(8,128)(2,1)}) custom-call(s32[17]{0:T(128)S(1)} %concatenate.18.slots_ref._.flip_ref.scalars_ref, bf16[768,3072]{1,0:T(8,128)(2,1)S(1)} %project_qkv.1.query_ref.key_ref.value_ref, bf16[768,3072]{1,0:T(8,128)(2,1)S(1)} %project_qkv.1.query_ref.key_ref.value_ref, ...), custom_call_target="tpu_custom_call" | custom-call | flops 1 | bytes 1 | tf_op jit(solution)/shard_map/self_attention/pallas_call | solution.py:65
  150.4 6.4 %self_out_norm.1 = (f32[768,1024]{1,0:T(8,128)}, bf16[768,1024]{1,0:T(8,128)(2,1)S(1)}) custom-call(s32[17]{0:T(128)S(1)} %concatenate.18.slots_ref._.flip_ref.scalars_ref, bf16[768,1024]{1,0:T(8,128)(2,1)S(1)} %get-tuple-element.379.inputs_ref.attended_ref, bf16[4,1,128,5120]{3,2,1,0:T(8,128)(2,1)} %bitcast.23.own_ref, ...), custom_call_target="tpu_custom_call" | custom-call | flops 1 | bytes 1 | tf_op jit(solution)/shard_map/self_out_norm/pallas_call | solution.py:65
  156.8 3.9 project_query.1.query_ref
  160.8 6.6 %cross_attention.1 = (bf16[768,1024]{1,0:T(8,128)(2,1)S(1)}, bf16[2,16,384,128]{3,2,1,0:T(8,128)(2,1)}) custom-call(s32[17]{0:T(128)S(1)} %concatenate.18.slots_ref._.flip_ref.scalars_ref, bf16[768,1024]{1,0:T(8,128)(2,1)S(1)} %project_query.1.query_ref, bf16[256,2048]{1,0:T(8,128)(2,1)S(1)} %project_text.1.key_ref.value_ref, ...), custom_call_target="tpu_custom_call" | custom-call | flops 1 | bytes 1 | tf_op jit(solution)/shard_map/cross_attention/pallas_call | solution.py:65
  168.5 4.9 %interleave.7 = bf16[4,4,32,4096]{3,2,1,0:T(8,128)(2,1)} custom-call(s32[17]{0:T(128)S(1)} %concatenate.18.slots_ref._.flip_ref.scalars_ref, bf16[4,32,4096]{2,1,0:T(8,128)(2,1)} %bitcast.11.refs_0_, bf16[4,32,4096]{2,1,0:T(8,128)(2,1)} %collective-permute-done.7.refs_1_, bf16[4,32,4096]{2,1,0:T(8,128)(2,1)S(1)} %collective-permute-done.11.refs_2_, ...), custom_call_target="tpu_custom_call" | custom-call | flops 1 | bytes 1 | tf_op jit(solution)/shard_map/interleave/pallas_call | solution.py:65
  176.8 6.7 %cross_out_norm.1 = (f32[768,1024]{1,0:T(8,128)}, bf16[768,1024]{1,0:T(8,128)(2,1)S(1)}) custom-call(s32[17]{0:T(128)S(1)} %concatenate.18.slots_ref._.flip_ref.scalars_ref, bf16[768,1024]{1,0:T(8,128)(2,1)S(1)} %copy-done.7, bf16[4,1,128,5120]{3,2,1,0:T(8,128)(2,1)} %bitcast.23.own_ref, bf16[4,1,128,5120]{3,2,1,0:T(8,128)(2,1)} %bitcast.24.other_ref, ...), custom_call_target="tpu_custom_call" | custom-call | flops 1 | bytes 1 | tf_op jit(solution)/shard_map/cross_out_norm/pallas_call | solution.py:65
  183.5 16.7 %hidden_layer.1 = (bf16[768,2048]{1,0:T(8,128)(2,1)S(1)}, bf16[768,2048]{1,0:T(8,128)(2,1)S(1)}, bf16[768,4096]{1,0:T(8,128)(2,1)}) custom-call(s32[17]{0:T(128)S(1)} %concatenate.18.slots_ref._.flip_ref.scalars_ref, bf16[768,1024]{1,0:T(8,128)(2,1)S(1)} %get-tuple-element.404.inputs_ref, bf16[4,1,128,4096]{3,2,1,0:T(8,128)(2,1)} %bitcast.26.own_ref, ...), custom_call_target="tpu_custom_call" | custom-call | flops 1 | bytes 1 | tf_op jit(solution)/shard_map/hidden_layer/pallas_call | solution.py:65
  200.2 5.9 %ff_out_grad_other.1 = bf16[2048,1024]{1,0:T(8,128)(2,1)} custom-call(s32[17]{0:T(128)S(1)} %concatenate.18.slots_ref._.flip_ref.scalars_ref, bf16[768,2048]{1,0:T(8,128)(2,1)S(1)} %get-tuple-element.410.inputs_ref.inputs_other, bf16[768,1024]{1,0:T(8,128)(2,1)S(1)} %bitcast.56), custom_call_target="tpu_custom_call" | custom-call | flops 1 | bytes 1 | tf_op jit(solution)/shard_map/ff_out_grad_other/pallas_call | solution.py:65
  206.1 12.4 %hidden_grad.1 = (bf16[768,4096]{1,0:T(8,128)(2,1)S(1)}, f32[1,4096]{1,0:T(1,128)S(1)}) custom-call(s32[17]{0:T(128)S(1)} %concatenate.18.slots_ref._.flip_ref.scalars_ref, bf16[768,1024]{1,0:T(8,128)(2,1)} %bitcast.54, bf16[4,2,512,1024]{3,2,1,0:T(8,128)(2,1)} %bitcast.79, bf16[4,2,512,1024]{3,2,1,0:T(8,128)(2,1)} %bitcast.80, ...), custom_call_target="tpu_custom_call" | custom-call | flops 1 | bytes 1 | tf_op jit(solution)/shard_map/hidden_grad/pallas_call | solution.py:65
  218.6 8.8 %ff_out_grad_own.1 = (bf16[8,128,1024]{2,1,0:T(8,128)(2,1)S(1)}, bf16[8,128,1024]{2,1,0:T(8,128)(2,1)S(1)}) custom-call(s32[17]{0:T(128)S(1)} %concatenate.18.slots_ref._.flip_ref.scalars_ref, bf16[768,2048]{1,0:T(8,128)(2,1)S(1)} %copy-done.20, bf16[768,1024]{1,0:T(8,128)(2,1)S(1)} %bitcast.57, bf16[2048,1024]{1,0:T(8,128)(2,1)} %collective-permute-done.14.arrived_ref), custom_call_target="tpu_custom_call" | custom-call | flops 1 | bytes 1 | tf_op jit(solution)/shard_map/ff_out_grad_own/pallas_call | solution.py:65
  227.4 5.0 %ff_in_grad_other.1 = bf16[512,4096]{1,0:T(8,128)(2,1)S(1)} custom-call(s32[17]{0:T(128)S(1)} %concatenate.18.slots_ref._.flip_ref.scalars_ref, bf16[768,1024]{1,0:T(8,128)(2,1)S(1)} %copy-done.10, bf16[768,4096]{1,0:T(8,128)(2,1)S(1)} %get-tuple-element.426.grads_ref), custom_call_target="tpu_custom_call" | custom-call | flops 1 | bytes 1 | tf_op jit(solution)/shard_map/ff_in_grad_other/pallas_call | solution.py:65
  233.7 17.2 %norm3_grad.1 = (f32[768,1024]{1,0:T(8,128)}, bf16[768,1024]{1,0:T(8,128)(2,1)S(1)}, f32[8,1024]{1,0:T(8,128)S(1)}) custom-call(s32[17]{0:T(128)S(1)} %concatenate.18.slots_ref._.flip_ref.scalars_ref, bf16[768,4096]{1,0:T(8,128)(2,1)} %copy-done.2, bf16[4,1,128,4096]{3,2,1,0:T(8,128)(2,1)} %bitcast.26.own_ref, bf16[4,1,128,4096]{3,2,1,0:T(8,128)(2,1)} %bitcast.27.other_ref, ...), custom_call_target="tpu_custom_call" | custom-call | flops 1 | bytes 1 | tf_op jit(solution)/shard_map/norm3_grad/pallas_call | solution.py:65
  250.9 6.5 %ff_in_grad_own.1 = (bf16[8,32,4096]{2,1,0:T(8,128)(2,1)S(1)}, bf16[8,32,4096]{2,1,0:T(8,128)(2,1)}) custom-call(s32[17]{0:T(128)S(1)} %concatenate.18.slots_ref._.flip_ref.scalars_ref, bf16[768,1024]{1,0:T(8,128)(2,1)S(1)} %copy-done.10, bf16[768,4096]{1,0:T(8,128)(2,1)S(1)} %copy-done.3, bf16[512,4096]{1,0:T(8,128)(2,1)S(1)} %collective-permute-done.15.arrived_ref), custom_call_target="tpu_custom_call" | custom-call | flops 1 | bytes 1 | tf_op jit(solution)/shard_map/ff_in_grad_own/pallas_call | solution.py:65
  257.4 4.6 attended2_grad.1.grad_ref
  262.1 8.7 %cross_attention_grads.1 = (bf16[768,1024]{1,0:T(8,128)(2,1)S(1)}, bf16[256,2048]{1,0:T(8,128)(2,1)S(1)}) custom-call(s32[17]{0:T(128)S(1)} %concatenate.18.slots_ref._.flip_ref.scalars_ref, bf16[768,1024]{1,0:T(8,128)(2,1)S(1)} %copy-done.12, bf16[256,2048]{1,0:T(8,128)(2,1)S(1)} %project_text.1.key_ref.value_ref, ...), custom_call_target="tpu_custom_call" | custom-call | flops 1 | bytes 1 | tf_op jit(solution)/shard_map/cross_attention_grads/pallas_call | solution.py:65
  270.7 2.5 combine.15
  280.0 8.7 %norm2_grad.1 = (f32[768,1024]{1,0:T(8,128)}, bf16[768,1024]{1,0:T(8,128)(2,1)S(1)}, f32[8,1024]{1,0:T(8,128)S(1)}) custom-call(s32[17]{0:T(128)S(1)} %concatenate.18.slots_ref._.flip_ref.scalars_ref, bf16[768,1024]{1,0:T(8,128)(2,1)S(1)} %get-tuple-element.458.grads_ref, bf16[4,1,128,5120]{3,2,1,0:T(8,128)(2,1)} %bitcast.23.own_ref, ...), custom_call_target="tpu_custom_call" | custom-call | flops 1 | bytes 1 | tf_op jit(solution)/shard_map/norm2_grad/pallas_call | solution.py:65
  288.7 2.3 cross_kv_grad_own.1
  294.4 4.4 attended1_grad.1.grad_ref
  298.8 14.6 %self_attention_grads.1.grads_ref = bf16[768,3072]{1,0:T(8,128)(2,1)S(1)} custom-call(s32[17]{0:T(128)S(1)} %concatenate.18.slots_ref._.flip_ref.scalars_ref, bf16[768,3072]{1,0:T(8,128)(2,1)S(1)} %bitcast.53, bf16[768,3072]{1,0:T(8,128)(2,1)S(1)} %bitcast.53, bf16[768,3072]{1,0:T(8,128)(2,1)S(1)} %bitcast.53, ...), custom_call_target="tpu_custom_call" | custom-call | flops 1 | bytes 1 | tf_op jit(solution)/shard_map/self_attention_grads/pallas_call | solution.py:65
  316.5 4.2 qkv_grad_other.1.refs_0_
  324.8 5.9 %collective-permute-start.23 = (bf16[2,128,1024]{2,1,0:T(8,128)(2,1)S(1)}, bf16[2,128,1024]{2,1,0:T(8,128)(2,1)S(1)}, u32[]{:S(2)}, u32[]{:S(2)}) collective-permute-start(bf16[2,128,1024]{2,1,0:T(8,128)(2,1)S(1)} %get-tuple-element.526), channel_id=1, source_target_pairs={{0,8},{1,9},{2,10},{3,11},{4,12},{5,13},{6,14},{7,15},{8,0},{9,1},... | collective-permute-start | bytes 1572872 | tf_op jit(solution)/shard_map/ppermute | solution.py:144
  330.8 5.0 %text_grad.1 = bf16[256,1024]{1,0:T(8,128)(2,1)} custom-call(s32[17]{0:T(128)S(1)} %concatenate.18.slots_ref._.flip_ref.scalars_ref, bf16[256,2048]{1,0:T(8,128)(2,1)S(1)} %get-tuple-element.456.grads_ref, bf16[4,1,128,5120]{3,2,1,0:T(8,128)(2,1)} %bitcast.23.own_ref, bf16[4,1,128,5120]{3,2,1,0:T(8,128)(2,1)} %bitcast.24.other_ref), custom_call_target="tpu_custom_call" | custom-call | flops 1 | bytes 1 | tf_op jit(solution)/shard_map/text_grad/pallas_call | solution.py:65
  335.7 5.7 %qkv_grad_own.1 = (bf16[8,32,4096]{2,1,0:T(8,128)(2,1)S(1)}, bf16[8,32,4096]{2,1,0:T(8,128)(2,1)}) custom-call(s32[17]{0:T(128)S(1)} %concatenate.18.slots_ref._.flip_ref.scalars_ref, bf16[768,1024]{1,0:T(8,128)(2,1)S(1)} %copy-done.17, bf16[768,3072]{1,0:T(8,128)(2,1)S(1)} %self_attention_grads.1.grads_ref, ...), custom_call_target="tpu_custom_call" | custom-call | flops 1 | bytes 1 | tf_op jit(solution)/shard_map/qkv_grad_own/pallas_call | solution.py:65
  341.5 2.5 self_out_grad_own.1
  345.3 12.6 %last_layer.1 = bf16[768,1024]{1,0:T(8,128)(2,1)} custom-call(s32[17]{0:T(128)S(1)} %concatenate.18.slots_ref._.flip_ref.scalars_ref, bf16[768,2048]{1,0:T(8,128)(2,1)S(1)} %copy-done.20, bf16[768,2048]{1,0:T(8,128)(2,1)S(1)} %copy-done.22, bf16[4,2,512,1024]{3,2,1,0:T(8,128)(2,1)} %bitcast.81, bf16[4,2,512,1024]{3,2,1,0:T(8,128)(2,1)} %bitcast.82, ...), custom_call_target="tpu_custom_call" | custom-call | flops 1 | bytes 1 | tf_op jit(solution)/shard_map/last_layer/pallas_call | solution.py:65
  360.8 2.2 combine.20
  364.3 5.1 %collective-permute-start.26 = (bf16[2,32,4096]{2,1,0:T(8,128)(2,1)}, bf16[2,32,4096]{2,1,0:T(8,128)(2,1)}, u32[]{:S(2)}, u32[]{:S(2)}) collective-permute-start(bf16[2,32,4096]{2,1,0:T(8,128)(2,1)} %get-tuple-element.561), channel_id=1, source_target_pairs={{0,8},{1,9},{2,10},{3,11},{4,12},{5,13},{6,14},{7,15},{8,0},{9,1},... | collective-permute-start | bytes 1572872 | tf_op jit(solution)/shard_map/ppermute | solution.py:144
  371.1 13.2 %norm1_grad.1 = (bf16[768,1024]{1,0:T(8,128)(2,1)}, f32[8,1024]{1,0:T(8,128)S(1)}) custom-call(s32[17]{0:T(128)S(1)} %concatenate.18.slots_ref._.flip_ref.scalars_ref, bf16[768,3072]{1,0:T(8,128)(2,1)} %copy-done.1, bf16[4,2,128,3200]{3,2,1,0:T(8,128)(2,1)} %bitcast.77, bf16[4,2,128,3200]{3,2,1,0:T(8,128)(2,1)} %bitcast.78, bf16[768,1024]{1,0:T(8,128)(2,1)} %bitcast.59, ...), custom_call_target="tpu_custom_call" | custom-call | flops 1 | bytes 1 | tf_op jit(solution)/shard_map/norm1_grad/pallas_call | solution.py:65
  393.9 5.7 %collective-permute-done.28.arrived_ref = bf16[8,32,4096]{2,1,0:T(8,128)(2,1)S(1)} collective-permute-done((bf16[8,32,4096]{2,1,0:T(8,128)(2,1)}, bf16[8,32,4096]{2,1,0:T(8,128)(2,1)S(1)}, u32[]{:S(2)}, u32[]{:S(2)}) %collective-permute-start.28) | collective-permute-done | bytes 2097184 | tf_op jit(solution)/shard_map/ppermute | solution.py:144
  402.2 5.1 %collective-permute-start.33 = (bf16[2,32,4096]{2,1,0:T(8,128)(2,1)S(1)}, bf16[2,32,4096]{2,1,0:T(8,128)(2,1)S(1)}, u32[]{:S(2)}, u32[]{:S(2)}) collective-permute-start(bf16[2,32,4096]{2,1,0:T(8,128)(2,1)S(1)} %get-tuple-element.606), channel_id=1, source_target_pairs={{0,8},{1,9},{2,10},{3,11},{4,12},{5,13},{6,14},{7,15},{8,0},{9,1},... | collective-permute-start | bytes 1572872 | tf_op jit(solution)/shard_map/ppermute | solution.py:144
  409.4 6.5 %collective-permute-done.30.arrived_ref = bf16[4,32,4096]{2,1,0:T(8,128)(2,1)S(1)} collective-permute-done((bf16[4,32,4096]{2,1,0:T(8,128)(2,1)S(1)}, bf16[4,32,4096]{2,1,0:T(8,128)(2,1)S(1)}, u32[]{:S(2)}, u32[]{:S(2)}) %collective-permute-start.30) | collective-permute-done | bytes 1048608 | tf_op jit(solution)/shard_map/ppermute | solution.py:144
  418.5 6.0 %collective-permute-done.33.arrived_ref = bf16[2,32,4096]{2,1,0:T(8,128)(2,1)S(1)} collective-permute-done((bf16[2,32,4096]{2,1,0:T(8,128)(2,1)S(1)}, bf16[2,32,4096]{2,1,0:T(8,128)(2,1)S(1)}, u32[]{:S(2)}, u32[]{:S(2)}) %collective-permute-start.33) | collective-permute-done | bytes 524320 | tf_op jit(solution)/shard_map/ppermute | solution.py:144
  429.5 11.6 %collective-permute-done.38 = bf16[1,32,4096]{2,1,0:T(8,128)(2,1)S(1)} collective-permute-done((bf16[1,32,4096]{2,1,0:T(8,128)(2,1)S(1)}, bf16[1,32,4096]{2,1,0:T(8,128)(2,1)S(1)}, u32[]{:S(2)}, u32[]{:S(2)}) %collective-permute-start.38) | collective-permute-done | bytes 262176 | tf_op jit(solution)/shard_map/ppermute | solution.py:144
  450.0 11.4 %collective-permute-done.37 = bf16[1,32,4096]{2,1,0:T(8,128)(2,1)S(1)} collective-permute-done((bf16[1,32,4096]{2,1,0:T(8,128)(2,1)S(1)}, bf16[1,32,4096]{2,1,0:T(8,128)(2,1)S(1)}, u32[]{:S(2)}, u32[]{:S(2)}) %collective-permute-start.37) | collective-permute-done | bytes 262176 | tf_op jit(solution)/shard_map/ppermute | solution.py:144
  (192 shorter events, 82.5 us)
Async XLA Ops:
  7.2 111.9 %all-gather.3.cloned.1.call-start = ((), (), s32[]{:S(2)}) async-start(), calls=%async_computation | async-start | bytes 6758400 | tf_op jit(solution)/shard_map/all_gather | solution.py:921
  9.6 36.2 %copy-start.25 = (bf16[2,128,1024]{2,1,0:T(8,128)(2,1)S(1)}, bf16[2,128,1024]{2,1,0:T(8,128)(2,1)}, u32[]{:S(2)}) copy-start(bf16[2,128,1024]{2,1,0:T(8,128)(2,1)} %param.23) | copy-start | bytes 1572868
  11.3 194.8 %all-gather.5.cloned.1.call-start = ((), (), s32[]{:S(2)}) async-start(), calls=%async_computation.1 | async-start | bytes 8650752 | tf_op jit(solution)/shard_map/all_gather | solution.py:926
  13.8 53.0 %copy-start.28 = (bf16[32,4096]{1,0:T(8,128)(2,1)S(1)}, bf16[32,4096]{1,0:T(8,128)(2,1)}, u32[]{:S(2)}) copy-start(bf16[32,4096]{1,0:T(8,128)(2,1)} %param.37) | copy-start | bytes 786436
  13.8 10.7 %collective-permute-start = (bf16[32,5120]{1,0:T(8,128)(2,1)S(1)}, bf16[32,5120]{1,0:T(8,128)(2,1)S(1)}, u32[]{:S(2)}, u32[]{:S(2)}) collective-permute-start(bf16[32,5120]{1,0:T(8,128)(2,1)S(1)} %pad_maximum_fusion), channel_id=1, source_target_pairs={{0,8},{1,9},{2,10},{3,11},{4,12},{5,13},{6,14},{7,15},{8,16},{9,17... | collective-permute-start | bytes 983048 | tf_op jit(solution)/shard_map/ppermute | solution.py:144
  15.2 28.5 %collective-permute-start.1 = (bf16[32,5120]{1,0:T(8,128)(2,1)S(1)}, bf16[32,5120]{1,0:T(8,128)(2,1)S(1)}, u32[]{:S(2)}, u32[]{:S(2)}) collective-permute-start(bf16[32,5120]{1,0:T(8,128)(2,1)S(1)} %pad_maximum_fusion), channel_id=1, source_target_pairs={{0,16},{1,17},{2,18},{3,19},{4,20},{5,21},{6,22},{7,23},{8,24},{9,... | collective-permute-start | bytes 983048 | tf_op jit(solution)/shard_map/ppermute | solution.py:144
  17.5 26.2 %collective-permute-start.2 = (bf16[32,5120]{1,0:T(8,128)(2,1)S(1)}, bf16[32,5120]{1,0:T(8,128)(2,1)S(1)}, u32[]{:S(2)}, u32[]{:S(2)}) collective-permute-start(bf16[32,5120]{1,0:T(8,128)(2,1)S(1)} %pad_maximum_fusion), channel_id=1, source_target_pairs={{0,24},{1,25},{2,26},{3,27},{4,28},{5,29},{6,30},{7,31},{8,0},{9,1... | collective-permute-start | bytes 983048 | tf_op jit(solution)/shard_map/ppermute | solution.py:144
  45.4 20.0 %collective-permute-start.6 = (bf16[4,32,5120]{2,1,0:T(8,128)(2,1)}, bf16[4,32,5120]{2,1,0:T(8,128)(2,1)}, u32[]{:S(2)}, u32[]{:S(2)}) collective-permute-start(bf16[4,32,5120]{2,1,0:T(8,128)(2,1)} %bitcast.5.refs_0_), channel_id=1, source_target_pairs={{0,1},{1,0},{2,3},{3,2},{4,6},{5,7},{6,4},{7,5},{8,9},{9,8},{10,11... | collective-permute-start | bytes 3932168 | tf_op jit(solution)/shard_map/ppermute | solution.py:144
  65.4 41.2 %collective-permute-start.8 = (bf16[4,32,5120]{2,1,0:T(8,128)(2,1)}, bf16[4,32,5120]{2,1,0:T(8,128)(2,1)S(1)}, u32[]{:S(2)}, u32[]{:S(2)}) collective-permute-start(bf16[4,32,5120]{2,1,0:T(8,128)(2,1)} %bitcast.5.refs_0_), channel_id=1, source_target_pairs={{0,2},{1,3},{2,0},{3,1},{4,5},{5,4},{6,7},{7,6},{8,10},{9,11},{10,... | collective-permute-start | bytes 3932168 | tf_op jit(solution)/shard_map/ppermute | solution.py:144
  66.7 42.4 %collective-permute-start.9 = (bf16[4,32,5120]{2,1,0:T(8,128)(2,1)}, bf16[4,32,5120]{2,1,0:T(8,128)(2,1)S(1)}, u32[]{:S(2)}, u32[]{:S(2)}) collective-permute-start(bf16[4,32,5120]{2,1,0:T(8,128)(2,1)} %collective-permute-done.6.refs_1_), channel_id=1, source_target_pairs={{0,2},{1,3},{2,0},{3,1},{4,5},{5,4},{6,7},{7,6},{8,10},{9,11},{10,... | collective-permute-start | bytes 3932168 | tf_op jit(solution)/shard_map/ppermute | solution.py:144
  66.9 14.6 %collective-permute-start.3 = (bf16[32,4096]{1,0:T(8,128)(2,1)S(1)}, bf16[32,4096]{1,0:T(8,128)(2,1)S(1)}, u32[]{:S(2)}, u32[]{:S(2)}) collective-permute-start(bf16[32,4096]{1,0:T(8,128)(2,1)S(1)} %copy-done.28), channel_id=1, source_target_pairs={{0,8},{1,9},{2,10},{3,11},{4,12},{5,13},{6,14},{7,15},{8,16},{9,17... | collective-permute-start | bytes 786440 | tf_op jit(solution)/shard_map/ppermute | solution.py:144
  72.4 32.5 %collective-permute-start.4 = (bf16[32,4096]{1,0:T(8,128)(2,1)S(1)}, bf16[32,4096]{1,0:T(8,128)(2,1)S(1)}, u32[]{:S(2)}, u32[]{:S(2)}) collective-permute-start(bf16[32,4096]{1,0:T(8,128)(2,1)S(1)} %copy-done.28), channel_id=1, source_target_pairs={{0,16},{1,17},{2,18},{3,19},{4,20},{5,21},{6,22},{7,23},{8,24},{9,... | collective-permute-start | bytes 786440 | tf_op jit(solution)/shard_map/ppermute | solution.py:144
  74.5 30.4 %collective-permute-start.5 = (bf16[32,4096]{1,0:T(8,128)(2,1)S(1)}, bf16[32,4096]{1,0:T(8,128)(2,1)S(1)}, u32[]{:S(2)}, u32[]{:S(2)}) collective-permute-start(bf16[32,4096]{1,0:T(8,128)(2,1)S(1)} %copy-done.28), channel_id=1, source_target_pairs={{0,24},{1,25},{2,26},{3,27},{4,28},{5,29},{6,30},{7,31},{8,0},{9,1... | collective-permute-start | bytes 786440 | tf_op jit(solution)/shard_map/ppermute | solution.py:144
  114.3 15.8 %collective-permute-start.10 = (bf16[4,128,5120]{2,1,0:T(8,128)(2,1)}, bf16[4,128,5120]{2,1,0:T(8,128)(2,1)}, u32[]{:S(2)}, u32[]{:S(2)}) collective-permute-start(bf16[4,128,5120]{2,1,0:T(8,128)(2,1)} %bitcast.12), channel_id=1, source_target_pairs={{0,4},{1,5},{2,6},{3,7},{4,0},{5,1},{6,2},{7,3},{8,12},{9,13},{10,... | collective-permute-start | bytes 15728648 | tf_op jit(solution)/shard_map/ppermute | solution.py:144
  119.0 16.1 %collective-permute-start.7 = (bf16[4,32,4096]{2,1,0:T(8,128)(2,1)}, bf16[4,32,4096]{2,1,0:T(8,128)(2,1)}, u32[]{:S(2)}, u32[]{:S(2)}) collective-permute-start(bf16[4,32,4096]{2,1,0:T(8,128)(2,1)} %bitcast.11.refs_0_), channel_id=1, source_target_pairs={{0,1},{1,0},{2,3},{3,2},{4,6},{5,7},{6,4},{7,5},{8,9},{9,8},{10,11... | collective-permute-start | bytes 3145736 | tf_op jit(solution)/shard_map/ppermute | solution.py:144
  135.1 33.4 %collective-permute-start.11 = (bf16[4,32,4096]{2,1,0:T(8,128)(2,1)}, bf16[4,32,4096]{2,1,0:T(8,128)(2,1)S(1)}, u32[]{:S(2)}, u32[]{:S(2)}) collective-permute-start(bf16[4,32,4096]{2,1,0:T(8,128)(2,1)} %bitcast.11.refs_0_), channel_id=1, source_target_pairs={{0,2},{1,3},{2,0},{3,1},{4,5},{5,4},{6,7},{7,6},{8,10},{9,11},{10,... | collective-permute-start | bytes 3145736 | tf_op jit(solution)/shard_map/ppermute | solution.py:144
  136.3 32.2 %collective-permute-start.12 = (bf16[4,32,4096]{2,1,0:T(8,128)(2,1)}, bf16[4,32,4096]{2,1,0:T(8,128)(2,1)S(1)}, u32[]{:S(2)}, u32[]{:S(2)}) collective-permute-start(bf16[4,32,4096]{2,1,0:T(8,128)(2,1)} %collective-permute-done.7.refs_1_), channel_id=1, source_target_pairs={{0,2},{1,3},{2,0},{3,1},{4,5},{5,4},{6,7},{7,6},{8,10},{9,11},{10,... | collective-permute-start | bytes 3145736 | tf_op jit(solution)/shard_map/ppermute | solution.py:144
  173.5 10.0 %collective-permute-start.13 = (bf16[4,128,4096]{2,1,0:T(8,128)(2,1)}, bf16[4,128,4096]{2,1,0:T(8,128)(2,1)}, u32[]{:S(2)}, u32[]{:S(2)}) collective-permute-start(bf16[4,128,4096]{2,1,0:T(8,128)(2,1)} %bitcast.25), channel_id=1, source_target_pairs={{0,4},{1,5},{2,6},{3,7},{4,0},{5,1},{6,2},{7,3},{8,12},{9,13},{10,... | collective-permute-start | bytes 12582920 | tf_op jit(solution)/shard_map/ppermute | solution.py:144
  183.5 16.7 %copy-start.9 = (bf16[768,1024]{1,0:T(8,128)(2,1)}, bf16[768,1024]{1,0:T(8,128)(2,1)S(1)}, u32[]{:S(2)}) copy-start(bf16[768,1024]{1,0:T(8,128)(2,1)S(1)} %get-tuple-element.404.inputs_ref) | copy-start | bytes 4718596
  183.5 16.7 %copy-start.4 = (bf16[2,384,1024]{2,1,0:T(8,128)(2,1)S(1)}, bf16[2,384,1024]{2,1,0:T(8,128)(2,1)}, u32[]{:S(2)}) copy-start(bf16[2,384,1024]{2,1,0:T(8,128)(2,1)} %param.25) | copy-start | bytes 4718596
  206.0 12.5 %collective-permute-start.14 = (bf16[2048,1024]{1,0:T(8,128)(2,1)}, bf16[2048,1024]{1,0:T(8,128)(2,1)}, u32[]{:S(2)}, u32[]{:S(2)}) collective-permute-start(bf16[2048,1024]{1,0:T(8,128)(2,1)} %ff_out_grad_other.1), channel_id=1, source_target_pairs={{0,4},{1,5},{2,6},{3,7},{4,0},{5,1},{6,2},{7,3},{8,12},{9,13},{10,... | collective-permute-start | bytes 12582920 | tf_op jit(solution)/shard_map/ppermute | solution.py:144
  232.3 18.5 %collective-permute-start.15 = (bf16[512,4096]{1,0:T(8,128)(2,1)S(1)}, bf16[512,4096]{1,0:T(8,128)(2,1)S(1)}, u32[]{:S(2)}, u32[]{:S(2)}) collective-permute-start(bf16[512,4096]{1,0:T(8,128)(2,1)S(1)} %ff_in_grad_other.1), channel_id=1, source_target_pairs={{0,4},{1,5},{2,6},{3,7},{4,0},{5,1},{6,2},{7,3},{8,12},{9,13},{10,... | collective-permute-start | bytes 12582920 | tf_op jit(solution)/shard_map/ppermute | solution.py:144
  232.9 37.9 %collective-permute-start.16 = (bf16[8,128,1024]{2,1,0:T(8,128)(2,1)S(1)}, bf16[8,128,1024]{2,1,0:T(8,128)(2,1)}, u32[]{:S(2)}, u32[]{:S(2)}) collective-permute-start(bf16[8,128,1024]{2,1,0:T(8,128)(2,1)S(1)} %get-tuple-element.441), channel_id=1, source_target_pairs={{0,2},{1,3},{2,0},{3,1},{4,5},{5,4},{6,7},{7,6},{8,10},{9,11},{10,... | collective-permute-start | bytes 6291464 | tf_op jit(solution)/shard_map/ppermute | solution.py:144
  233.7 17.2 %copy-start.3 = (bf16[768,4096]{1,0:T(8,128)(2,1)S(1)}, bf16[768,4096]{1,0:T(8,128)(2,1)}, u32[]{:S(2)}) copy-start(bf16[768,4096]{1,0:T(8,128)(2,1)} %copy-done.2) | copy-start | bytes 18874372
  278.1 10.6 %collective-permute-start.19 = (bf16[512,4096]{1,0:T(8,128)(2,1)S(1)}, bf16[512,4096]{1,0:T(8,128)(2,1)S(1)}, u32[]{:S(2)}, u32[]{:S(2)}) collective-permute-start(bf16[512,4096]{1,0:T(8,128)(2,1)S(1)} %cross_out_grad_other.1), channel_id=1, source_target_pairs={{0,4},{1,5},{2,6},{3,7},{4,0},{5,1},{6,2},{7,3},{8,12},{9,13},{10,... | collective-permute-start | bytes 12582920 | tf_op jit(solution)/shard_map/ppermute | solution.py:144
  278.2 36.7 %collective-permute-start.17 = (bf16[8,32,4096]{2,1,0:T(8,128)(2,1)}, bf16[8,32,4096]{2,1,0:T(8,128)(2,1)S(1)}, u32[]{:S(2)}, u32[]{:S(2)}) collective-permute-start(bf16[8,32,4096]{2,1,0:T(8,128)(2,1)} %get-tuple-element.463), channel_id=1, source_target_pairs={{0,2},{1,3},{2,0},{3,1},{4,5},{5,4},{6,7},{7,6},{8,10},{9,11},{10,... | collective-permute-start | bytes 6291464 | tf_op jit(solution)/shard_map/ppermute | solution.py:144
  278.9 34.5 %collective-permute-start.18 = (bf16[4,128,1024]{2,1,0:T(8,128)(2,1)S(1)}, bf16[4,128,1024]{2,1,0:T(8,128)(2,1)S(1)}, u32[]{:S(2)}, u32[]{:S(2)}) collective-permute-start(bf16[4,128,1024]{2,1,0:T(8,128)(2,1)S(1)} %get-tuple-element.464), channel_id=1, source_target_pairs={{0,1},{1,0},{2,3},{3,2},{4,6},{5,7},{6,4},{7,5},{8,9},{9,8},{10,11... | collective-permute-start | bytes 3145736 | tf_op jit(solution)/shard_map/ppermute | solution.py:144
  313.4 22.3 %copy-start.1 = (bf16[768,3072]{1,0:T(8,128)(2,1)}, bf16[768,3072]{1,0:T(8,128)(2,1)S(1)}, u32[]{:S(2)}) copy-start(bf16[768,3072]{1,0:T(8,128)(2,1)S(1)} %self_attention_grads.1.grads_ref) | copy-start | bytes 14155780
  322.3 13.4 %collective-permute-start.20 = (bf16[512,4096]{1,0:T(8,128)(2,1)S(1)}, bf16[512,4096]{1,0:T(8,128)(2,1)S(1)}, u32[]{:S(2)}, u32[]{:S(2)}) collective-permute-start(bf16[512,4096]{1,0:T(8,128)(2,1)S(1)} %self_out_grad_other.1), channel_id=1, source_target_pairs={{0,4},{1,5},{2,6},{3,7},{4,0},{5,1},{6,2},{7,3},{8,12},{9,13},{10,... | collective-permute-start | bytes 12582920 | tf_op jit(solution)/shard_map/ppermute | solution.py:144
  323.1 37.7 %collective-permute-start.21 = (bf16[8,32,4096]{2,1,0:T(8,128)(2,1)S(1)}, bf16[8,32,4096]{2,1,0:T(8,128)(2,1)S(1)}, u32[]{:S(2)}, u32[]{:S(2)}) collective-permute-start(bf16[8,32,4096]{2,1,0:T(8,128)(2,1)S(1)} %get-tuple-element.524), channel_id=1, source_target_pairs={{0,2},{1,3},{2,0},{3,1},{4,5},{5,4},{6,7},{7,6},{8,10},{9,11},{10,... | collective-permute-start | bytes 6291464 | tf_op jit(solution)/shard_map/ppermute | solution.py:144
  323.9 35.2 %collective-permute-start.22 = (bf16[4,32,4096]{2,1,0:T(8,128)(2,1)S(1)}, bf16[4,32,4096]{2,1,0:T(8,128)(2,1)S(1)}, u32[]{:S(2)}, u32[]{:S(2)}) collective-permute-start(bf16[4,32,4096]{2,1,0:T(8,128)(2,1)S(1)} %get-tuple-element.525), channel_id=1, source_target_pairs={{0,1},{1,0},{2,3},{3,2},{4,6},{5,7},{6,4},{7,5},{8,9},{9,8},{10,11... | collective-permute-start | bytes 3145736 | tf_op jit(solution)/shard_map/ppermute | solution.py:144
  324.8 33.0 %collective-permute-start.23 = (bf16[2,128,1024]{2,1,0:T(8,128)(2,1)S(1)}, bf16[2,128,1024]{2,1,0:T(8,128)(2,1)S(1)}, u32[]{:S(2)}, u32[]{:S(2)}) collective-permute-start(bf16[2,128,1024]{2,1,0:T(8,128)(2,1)S(1)} %get-tuple-element.526), channel_id=1, source_target_pairs={{0,8},{1,9},{2,10},{3,11},{4,12},{5,13},{6,14},{7,15},{8,0},{9,1},... | collective-permute-start | bytes 1572872 | tf_op jit(solution)/shard_map/ppermute | solution.py:144
  363.1 36.6 %collective-permute-start.28 = (bf16[8,32,4096]{2,1,0:T(8,128)(2,1)}, bf16[8,32,4096]{2,1,0:T(8,128)(2,1)S(1)}, u32[]{:S(2)}, u32[]{:S(2)}) collective-permute-start(bf16[8,32,4096]{2,1,0:T(8,128)(2,1)} %get-tuple-element.577), channel_id=1, source_target_pairs={{0,2},{1,3},{2,0},{3,1},{4,5},{5,4},{6,7},{7,6},{8,10},{9,11},{10,... | collective-permute-start | bytes 6291464 | tf_op jit(solution)/shard_map/ppermute | solution.py:144
  364.3 27.7 %collective-permute-start.29 = (bf16[4,32,4096]{2,1,0:T(8,128)(2,1)}, bf16[4,32,4096]{2,1,0:T(8,128)(2,1)}, u32[]{:S(2)}, u32[]{:S(2)}) collective-permute-start(bf16[4,32,4096]{2,1,0:T(8,128)(2,1)} %get-tuple-element.578), channel_id=1, source_target_pairs={{0,1},{1,0},{2,3},{3,2},{4,6},{5,7},{6,4},{7,5},{8,9},{9,8},{10,11... | collective-permute-start | bytes 3145736 | tf_op jit(solution)/shard_map/ppermute | solution.py:144
  364.3 24.2 %collective-permute-start.26 = (bf16[2,32,4096]{2,1,0:T(8,128)(2,1)}, bf16[2,32,4096]{2,1,0:T(8,128)(2,1)}, u32[]{:S(2)}, u32[]{:S(2)}) collective-permute-start(bf16[2,32,4096]{2,1,0:T(8,128)(2,1)} %get-tuple-element.561), channel_id=1, source_target_pairs={{0,8},{1,9},{2,10},{3,11},{4,12},{5,13},{6,14},{7,15},{8,0},{9,1},... | collective-permute-start | bytes 1572872 | tf_op jit(solution)/shard_map/ppermute | solution.py:144
  369.4 21.8 %collective-permute-start.25 = (bf16[1,128,1024]{2,1,0:T(8,128)(2,1)}, bf16[1,128,1024]{2,1,0:T(8,128)(2,1)}, u32[]{:S(2)}, u32[]{:S(2)}) collective-permute-start(bf16[1,128,1024]{2,1,0:T(8,128)(2,1)} %get-tuple-element.560), channel_id=1, source_target_pairs={{0,16},{1,17},{2,18},{3,19},{4,20},{5,21},{6,22},{7,23},{8,24},{9,... | collective-permute-start | bytes 786440 | tf_op jit(solution)/shard_map/ppermute | solution.py:144
  385.6 14.1 %copy-start.24 = (bf16[8,32,4096]{2,1,0:T(8,128)(2,1)S(1)}, bf16[8,32,4096]{2,1,0:T(8,128)(2,1)}, u32[]{:S(2)}) copy-start(bf16[8,32,4096]{2,1,0:T(8,128)(2,1)} %copy-done.23) | copy-start | bytes 6291460
  386.4 4.8 %collective-permute-start.24 = (bf16[512,128]{1,0:T(8,128)(2,1)S(1)}, bf16[512,128]{1,0:T(8,128)(2,1)S(1)}, u32[]{:S(2)}, u32[]{:S(2)}) collective-permute-start(bf16[512,128]{1,0:T(8,128)(2,1)S(1)} %small_grad_other.1), channel_id=1, source_target_pairs={{0,4},{1,5},{2,6},{3,7},{4,0},{5,1},{6,2},{7,3},{8,12},{9,13},{10,... | collective-permute-start | bytes 393224 | tf_op jit(solution)/shard_map/ppermute | solution.py:144
  401.2 14.7 %collective-permute-start.30 = (bf16[4,32,4096]{2,1,0:T(8,128)(2,1)S(1)}, bf16[4,32,4096]{2,1,0:T(8,128)(2,1)S(1)}, u32[]{:S(2)}, u32[]{:S(2)}) collective-permute-start(bf16[4,32,4096]{2,1,0:T(8,128)(2,1)S(1)} %get-tuple-element.591), channel_id=1, source_target_pairs={{0,1},{1,0},{2,3},{3,2},{4,6},{5,7},{6,4},{7,5},{8,9},{9,8},{10,11... | collective-permute-start | bytes 3145736 | tf_op jit(solution)/shard_map/ppermute | solution.py:144
  402.2 22.4 %collective-permute-start.33 = (bf16[2,32,4096]{2,1,0:T(8,128)(2,1)S(1)}, bf16[2,32,4096]{2,1,0:T(8,128)(2,1)S(1)}, u32[]{:S(2)}, u32[]{:S(2)}) collective-permute-start(bf16[2,32,4096]{2,1,0:T(8,128)(2,1)S(1)} %get-tuple-element.606), channel_id=1, source_target_pairs={{0,8},{1,9},{2,10},{3,11},{4,12},{5,13},{6,14},{7,15},{8,0},{9,1},... | collective-permute-start | bytes 1572872 | tf_op jit(solution)/shard_map/ppermute | solution.py:144
  407.3 17.9 %collective-permute-start.32 = (bf16[1,32,4096]{2,1,0:T(8,128)(2,1)S(1)}, bf16[1,32,4096]{2,1,0:T(8,128)(2,1)S(1)}, u32[]{:S(2)}, u32[]{:S(2)}) collective-permute-start(bf16[1,32,4096]{2,1,0:T(8,128)(2,1)S(1)} %get-tuple-element.605), channel_id=1, source_target_pairs={{0,16},{1,17},{2,18},{3,19},{4,20},{5,21},{6,22},{7,23},{8,24},{9,... | collective-permute-start | bytes 786440 | tf_op jit(solution)/shard_map/ppermute | solution.py:144
  407.3 9.6 %collective-permute-start.27 = (bf16[8,32,128]{2,1,0:T(8,128)(2,1)S(1)}, bf16[8,32,128]{2,1,0:T(8,128)(2,1)S(1)}, u32[]{:S(2)}, u32[]{:S(2)}) collective-permute-start(bf16[8,32,128]{2,1,0:T(8,128)(2,1)S(1)} %get-tuple-element.576), channel_id=1, source_target_pairs={{0,2},{1,3},{2,0},{3,1},{4,5},{5,4},{6,7},{7,6},{8,10},{9,11},{10,... | collective-permute-start | bytes 196616 | tf_op jit(solution)/shard_map/ppermute | solution.py:144
  417.5 9.9 %collective-permute-start.31 = (bf16[4,32,128]{2,1,0:T(8,128)(2,1)S(1)}, bf16[4,32,128]{2,1,0:T(8,128)(2,1)S(1)}, u32[]{:S(2)}, u32[]{:S(2)}) collective-permute-start(bf16[4,32,128]{2,1,0:T(8,128)(2,1)S(1)} %get-tuple-element.604), channel_id=1, source_target_pairs={{0,1},{1,0},{2,3},{3,2},{4,6},{5,7},{6,4},{7,5},{8,9},{9,8},{10,11... | collective-permute-start | bytes 98312 | tf_op jit(solution)/shard_map/ppermute | solution.py:144
  425.2 18.5 %collective-permute-start.35 = (bf16[2,32,4096]{2,1,0:T(8,128)(2,1)S(1)}, bf16[2,32,4096]{2,1,0:T(8,128)(2,1)S(1)}, u32[]{:S(2)}, u32[]{:S(2)}) collective-permute-start(bf16[2,32,4096]{2,1,0:T(8,128)(2,1)S(1)} %get-tuple-element.621), channel_id=1, source_target_pairs={{0,8},{1,9},{2,10},{3,11},{4,12},{5,13},{6,14},{7,15},{8,0},{9,1},... | collective-permute-start | bytes 1572872 | tf_op jit(solution)/shard_map/ppermute | solution.py:144
  425.3 15.9 %collective-permute-start.38 = (bf16[1,32,4096]{2,1,0:T(8,128)(2,1)S(1)}, bf16[1,32,4096]{2,1,0:T(8,128)(2,1)S(1)}, u32[]{:S(2)}, u32[]{:S(2)}) collective-permute-start(bf16[1,32,4096]{2,1,0:T(8,128)(2,1)S(1)} %get-tuple-element.639), channel_id=1, source_target_pairs={{0,16},{1,17},{2,18},{3,19},{4,20},{5,21},{6,22},{7,23},{8,24},{9,... | collective-permute-start | bytes 786440 | tf_op jit(solution)/shard_map/ppermute | solution.py:144
  428.0 16.4 %collective-permute-start.34 = (bf16[2,32,128]{2,1,0:T(8,128)(2,1)S(1)}, bf16[2,32,128]{2,1,0:T(8,128)(2,1)S(1)}, u32[]{:S(2)}, u32[]{:S(2)}) collective-permute-start(bf16[2,32,128]{2,1,0:T(8,128)(2,1)S(1)} %get-tuple-element.620), channel_id=1, source_target_pairs={{0,8},{1,9},{2,10},{3,11},{4,12},{5,13},{6,14},{7,15},{8,0},{9,1},... | collective-permute-start | bytes 49160 | tf_op jit(solution)/shard_map/ppermute | solution.py:144
  444.9 3.5 collective-permute-start.36
  447.0 14.4 %collective-permute-start.37 = (bf16[1,32,4096]{2,1,0:T(8,128)(2,1)S(1)}, bf16[1,32,4096]{2,1,0:T(8,128)(2,1)S(1)}, u32[]{:S(2)}, u32[]{:S(2)}) collective-permute-start(bf16[1,32,4096]{2,1,0:T(8,128)(2,1)S(1)} %get-tuple-element.637), channel_id=1, source_target_pairs={{0,16},{1,17},{2,18},{3,19},{4,20},{5,21},{6,22},{7,23},{8,24},{9,... | collective-permute-start | bytes 786440 | tf_op jit(solution)/shard_map/ppermute | solution.py:144
  (24 other events, 136.1 us)
Sparse Core Ops, SparseCore 0:
  11.5 103.3 all-gather.2
  117.7 80.9 all-gather.4
